TPU v7x, 256 devices: a whole 4x4x8 slice. The times are simulated.
256 devices in a mesh: ha: 16 (over y, x_lo, core), wa: 8 (over z), dp: 2 (over x_hi).
Axes of the slice: x: 4 (x_hi: 2, x_lo: 2; x = x_hi * 2 + x_lo), y: 4, z: 8, core: 2. Of those that a mesh axis runs over, the one named last changes fastest.
Arguments:
- tokens: bfloat16 [8, 224, 56, 384], P('dp', 'ha', 'wa'), may hold values from -6 to 6
- grad_out: bfloat16 [8, 224, 56, 384], P('dp', 'ha', 'wa'), may hold values from -6 to 6
- gain_first: float32 [384], replicated, may hold values from 0.5 to 1.5
- gain_second: float32 [384], replicated, may hold values from 0.5 to 1.5
- w_qkv: bfloat16 [1152, 384], replicated, may hold values from -0.3125 to 0.3125
- w_proj: bfloat16 [384, 384], replicated, may hold values from -0.3125 to 0.3125
- w_up: bfloat16 [1536, 384], replicated, may hold values from -0.3125 to 0.3125
- w_down: bfloat16 [384, 1536], replicated, may hold values from -0.15625 to 0.15625
Outputs:
- grad_tokens: bfloat16 [8, 224, 56, 384], P('dp', 'ha', 'wa')
- grad_qkv: float32 [1152, 384], P('ha', 'wa')
- grad_proj: float32 [384, 384], P('ha', 'wa')
- grad_up: float32 [1536, 384], P('ha', 'wa')
- grad_down: float32 [384, 1536], P('ha', 'wa')
- grad_gain_first: float32 [384], replicated
- grad_gain_second: float32 [384], replicated
All inputs are finite; a program needn't handle non-finite values.
Results may differ from a plain program's by a relative error of at most 0.033.
Values may be sent and summed in bfloat16 or wider, within the bound.
No kernel may reach another device: no remote copies, remote signals or barrier semaphores. Data moves between devices by JAX's collectives and lax.ppermute only.
A program may use at most 64 MiB of HBM per device.

v0:
```python
import jax
import jax.numpy as jnp
from jax import lax
from jax.sharding import PartitionSpec as P

HEADS = 12
GRID = 7


EPSILON = 1e-05


def contract(form, left, right):
    return jnp.einsum(form, left, right, preferred_element_type=jnp.float32)


def norm_forward(values, gain):
    values_f = values.astype(jnp.float32)
    centered = values_f - jnp.mean(values_f, axis=-1, keepdims=True)
    inv_std = lax.rsqrt(jnp.mean(centered * centered, axis=-1, keepdims=True) + EPSILON)
    normal_hat = centered * inv_std
    return ((normal_hat * gain).astype(jnp.bfloat16), normal_hat, inv_std)


def norm_backward(grad_norm, normal_hat, inv_std, gain):
    grad_float = grad_norm.astype(jnp.float32)
    grad_hat = grad_float * gain
    first_mean = jnp.mean(grad_hat, axis=-1, keepdims=True)
    second_mean = jnp.mean(grad_hat * normal_hat, axis=-1, keepdims=True)
    return (
        inv_std * (grad_hat - first_mean - normal_hat * second_mean),
        jnp.sum(grad_float * normal_hat, axis=0),
    )


def linear(activations, weight):
    return jnp.dot(activations, weight.T, preferred_element_type=jnp.float32)


def linear_back(gradient, weight):
    return jnp.dot(gradient, weight, preferred_element_type=jnp.float32)


def weight_grad(gradient, activations):
    return jnp.dot(gradient.T, activations, preferred_element_type=jnp.float32)


def split_heads(qkv_rows):
    token_count, triple = qkv_rows.shape
    return qkv_rows.reshape(
        token_count // (GRID * GRID), GRID * GRID, 3, HEADS, triple // (3 * HEADS)
    )


def attention_forward(normed, w_qkv):
    token_count, channels = normed.shape
    qkv_rows = linear(normed, w_qkv).astype(jnp.bfloat16)
    heads_view = split_heads(qkv_rows)
    scale = (channels // HEADS) ** (-0.5)
    scores = contract("gqhd,gkhd->ghqk", heads_view[:, :, 0], heads_view[:, :, 1]) * scale
    expo_scores = jnp.exp(scores)
    probs_float = expo_scores / jnp.sum(expo_scores, axis=-1, keepdims=True)
    probs_round = probs_float.astype(jnp.bfloat16)
    mixed = contract("ghqk,gkhd->gqhd", probs_round, heads_view[:, :, 2])
    return (
        qkv_rows,
        probs_float,
        probs_round,
        mixed.astype(jnp.bfloat16).reshape(token_count, channels),
    )


def attention_backward(
    grad_resid, normed, qkv_rows, probs_float, probs_round, mixed, w_qkv, w_proj
):
    token_count, channels = grad_resid.shape
    grad_mixed = linear_back(grad_resid, w_proj).astype(jnp.bfloat16)
    heads_view = split_heads(qkv_rows)
    scale = (channels // HEADS) ** (-0.5)
    grad_heads = grad_mixed.reshape(
        token_count // (GRID * GRID), GRID * GRID, HEADS, channels // HEADS
    )
    grad_probs = contract("gqhd,gkhd->ghqk", grad_heads, heads_view[:, :, 2])
    grad_value = contract("ghqk,gqhd->gkhd", probs_round, grad_heads)
    centre = jnp.sum(grad_probs * probs_float, axis=-1, keepdims=True)
    grad_scores = (probs_float * (grad_probs - centre) * scale).astype(jnp.bfloat16)
    grad_query = contract("ghqk,gkhd->gqhd", grad_scores, heads_view[:, :, 1])
    grad_key = contract("ghqk,gqhd->gkhd", grad_scores, heads_view[:, :, 0])
    grad_rows = (
        jnp.stack([grad_query, grad_key, grad_value], axis=2)
        .astype(jnp.bfloat16)
        .reshape(token_count, 3 * channels)
    )
    grad_normed = linear_back(grad_rows, w_qkv).astype(jnp.bfloat16)
    return (grad_normed, weight_grad(grad_rows, normed), weight_grad(grad_resid, mixed))


def mlp_backward(resid, grad_out, gain_second, w_up, w_down):
    normed, normal_hat, inv_std = norm_forward(resid, gain_second)
    hidden = linear(normed, w_up)
    activated, gelu_back = jax.vjp(jax.nn.gelu, hidden)
    activated = activated.astype(jnp.bfloat16)
    grad_act = linear_back(grad_out, w_down)
    grad_hidden = gelu_back(grad_act)[0].astype(jnp.bfloat16)
    grad_normed = linear_back(grad_hidden, w_up)
    grad_float, grad_gain = norm_backward(grad_normed, normal_hat, inv_std, gain_second)
    grad_resid = (grad_out.astype(jnp.float32) + grad_float).astype(jnp.bfloat16)
    return (
        grad_resid,
        weight_grad(grad_hidden, normed),
        weight_grad(grad_out, activated),
        grad_gain,
    )


def padded_size(line_count, device_count):
    return device_count * -(-line_count // device_count)


def slot_lines(values, dim_axis, device_count, position):
    line_count = values.shape[dim_axis]
    padded = padded_size(line_count, device_count)
    pad_widths = [(0, 0)] * values.ndim
    pad_widths[dim_axis] = (0, padded - line_count)
    shifted = jnp.roll(jnp.pad(values, pad_widths), line_count * position % padded, axis=dim_axis)
    new_shape = (
        values.shape[:dim_axis]
        + (padded // device_count, device_count)
        + values.shape[dim_axis + 1 :]
    )
    return shifted.reshape(new_shape)


def unslot_lines(values, dim_axis, line_count, position):
    padded = values.shape[dim_axis] * values.shape[dim_axis + 1]
    merged = values.reshape(values.shape[:dim_axis] + (padded,) + values.shape[dim_axis + 2 :])
    merged = jnp.roll(merged, -(line_count * position % padded), axis=dim_axis)
    return lax.slice_in_dim(merged, 0, line_count, axis=dim_axis)


def group_lookup(line_count, device_count, position):
    padded = padded_size(line_count, device_count)
    spacing = line_count * device_count // GRID
    per_device = line_count // GRID
    group_line = jnp.arange(per_device, dtype=jnp.int32)[:, None]
    member_band = jnp.arange(GRID, dtype=jnp.int32)[None, :]
    global_line = position + device_count * group_line + spacing * member_band
    source_dev = global_line // line_count
    local_line = global_line % line_count
    slot_pos = (line_count * source_dev % padded + local_line) % padded
    return (slot_pos // device_count * device_count + source_dev).reshape(-1)


def slot_lookup(line_count, device_count, position):
    padded = padded_size(line_count, device_count)
    spacing = line_count * device_count // GRID
    per_device = line_count // GRID
    slot_level = jnp.arange(padded // device_count, dtype=jnp.int32)[:, None]
    source_dev = jnp.arange(device_count, dtype=jnp.int32)[None, :]
    slot_pos = slot_level * device_count + position
    local_line = (slot_pos - line_count * source_dev % padded) % padded
    global_line = line_count * source_dev + local_line
    group_line = (global_line % spacing - position) // device_count
    member_band = global_line // spacing
    return jnp.clip(group_line * GRID + member_band, 0, per_device * GRID - 1).reshape(-1)


def route_in(slots):
    dims = slots.shape
    joined = slots.transpose(0, 1, 2, 4, 3, 5, 6).reshape(
        dims[0], dims[1], dims[2], dims[4], dims[3] * dims[5], dims[6]
    )
    arrived = lax.all_to_all(joined, ("ha", "wa"), split_axis=4, concat_axis=4, tiled=True)
    return arrived.reshape(dims[0], dims[1], dims[2], dims[4], dims[3], dims[5], dims[6]).transpose(
        0, 1, 2, 4, 3, 5, 6
    )


def route_out(slots):
    dims = slots.shape
    joined = slots.transpose(0, 1, 2, 4, 3, 5, 6).reshape(
        dims[0], dims[1], dims[2], dims[4], dims[3] * dims[5], dims[6]
    )
    arrived = lax.all_to_all(joined, ("ha", "wa"), split_axis=4, concat_axis=4, tiled=True)
    return arrived.reshape(dims[0], dims[1], dims[2], dims[4], dims[3], dims[5], dims[6]).transpose(
        0, 1, 2, 4, 3, 5, 6
    )


def to_groups(values):
    row_devices = lax.axis_size("ha")
    col_devices = lax.axis_size("wa")
    row_position = lax.axis_index("ha")
    col_position = lax.axis_index("wa")
    stacks, crop_count, row_count, col_count, channels = values.shape
    slots = slot_lines(
        slot_lines(values, 2, row_devices, row_position), 4, col_devices, col_position
    )
    arrived = route_in(slots)
    dims = arrived.shape
    merged = arrived.reshape(stacks, crop_count, dims[2] * dims[3], dims[4] * dims[5], channels)
    picked = jnp.take(merged, group_lookup(row_count, row_devices, row_position), axis=2)
    picked = jnp.take(picked, group_lookup(col_count, col_devices, col_position), axis=3)
    grouped = picked.reshape(
        stacks, crop_count, row_count // GRID, GRID, col_count // GRID, GRID, channels
    )
    return grouped.transpose(0, 1, 2, 4, 3, 5, 6).reshape(stacks, -1, channels)


def from_groups(values, crop_count, row_count, col_count):
    row_devices = lax.axis_size("ha")
    col_devices = lax.axis_size("wa")
    row_position = lax.axis_index("ha")
    col_position = lax.axis_index("wa")
    stacks, token_count, channels = values.shape
    grouped = values.reshape(
        stacks, crop_count, row_count // GRID, col_count // GRID, GRID, GRID, channels
    )
    grouped = grouped.transpose(0, 1, 2, 4, 3, 5, 6).reshape(
        stacks, crop_count, row_count, col_count, channels
    )
    slots = jnp.take(grouped, slot_lookup(row_count, row_devices, row_position), axis=2)
    slots = jnp.take(slots, slot_lookup(col_count, col_devices, col_position), axis=3)
    row_depth = padded_size(row_count, row_devices) // row_devices
    col_depth = padded_size(col_count, col_devices) // col_devices
    slots = slots.reshape(
        stacks, crop_count, row_depth, row_devices, col_depth, col_devices, channels
    )
    returned = route_out(slots)
    tiled = unslot_lines(returned, 2, row_count, row_position)
    return unslot_lines(tiled, 3, col_count, col_position)


def body(tokens, grad_out, gain_first, gain_second, w_qkv, w_proj, w_up, w_down):
    crop_count, row_count, col_count, channels = tokens.shape
    flat_tokens = tokens.reshape(-1, channels)
    normed, normal_hat, inv_std = norm_forward(flat_tokens, gain_first)
    grid_normed = to_groups(normed.reshape(1, crop_count, row_count, col_count, channels))[0]
    qkv_rows, probs_float, probs_round, mixed = attention_forward(grid_normed, w_qkv)
    branch = linear(mixed, w_proj).astype(jnp.bfloat16)
    branch_tile = from_groups(branch[None], crop_count, row_count, col_count).reshape(-1, channels)
    resid = (flat_tokens.astype(jnp.float32) + branch_tile.astype(jnp.float32)).astype(jnp.bfloat16)
    grad_resid, grad_up, grad_down, gain_two = mlp_backward(
        resid, grad_out.reshape(-1, channels), gain_second, w_up, w_down
    )
    grid_grad = to_groups(grad_resid.reshape(1, crop_count, row_count, col_count, channels))[0]
    grad_normed, grad_qkv, grad_proj = attention_backward(
        grid_grad, grid_normed, qkv_rows, probs_float, probs_round, mixed, w_qkv, w_proj
    )
    normed_tile = from_groups(grad_normed[None], crop_count, row_count, col_count).reshape(
        -1, channels
    )
    grad_float, gain_one = norm_backward(normed_tile, normal_hat, inv_std, gain_first)
    grad_tokens = (
        (grad_resid.astype(jnp.float32) + grad_float)
        .astype(jnp.bfloat16)
        .reshape(crop_count, row_count, col_count, channels)
    )
    partial_value = (grad_qkv, grad_proj, grad_up, grad_down, gain_one, gain_two)
    weights = partial_value[:4]
    row_sums = (
        lax.psum_scatter(
            weights[0].astype(jnp.bfloat16), "ha", scatter_dimension=0, tiled=True
        ).astype(jnp.float32),
        lax.psum_scatter(
            weights[1].astype(jnp.bfloat16), "ha", scatter_dimension=0, tiled=True
        ).astype(jnp.float32),
        lax.psum_scatter(
            weights[2].astype(jnp.bfloat16), "ha", scatter_dimension=0, tiled=True
        ).astype(jnp.float32),
        lax.psum_scatter(
            weights[3].astype(jnp.bfloat16), "ha", scatter_dimension=0, tiled=True
        ).astype(jnp.float32),
    )
    col_sums = (
        lax.psum_scatter(
            row_sums[0].astype(jnp.bfloat16), "wa", scatter_dimension=1, tiled=True
        ).astype(jnp.float32),
        lax.psum_scatter(
            row_sums[1].astype(jnp.bfloat16), "wa", scatter_dimension=1, tiled=True
        ).astype(jnp.float32),
        lax.psum_scatter(
            row_sums[2].astype(jnp.bfloat16), "wa", scatter_dimension=1, tiled=True
        ).astype(jnp.float32),
        lax.psum_scatter(
            row_sums[3].astype(jnp.bfloat16), "wa", scatter_dimension=1, tiled=True
        ).astype(jnp.float32),
    )
    totals = (
        lax.psum(col_sums[0].astype(jnp.bfloat16), "dp").astype(jnp.float32),
        lax.psum(col_sums[1].astype(jnp.bfloat16), "dp").astype(jnp.float32),
        lax.psum(col_sums[2].astype(jnp.bfloat16), "dp").astype(jnp.float32),
        lax.psum(col_sums[3].astype(jnp.bfloat16), "dp").astype(jnp.float32),
    )
    gain_sums = lax.psum((partial_value[4], partial_value[5]), ("ha", "wa", "dp"))
    token_total = (
        crop_count
        * row_count
        * col_count
        * lax.axis_size("ha")
        * lax.axis_size("wa")
        * lax.axis_size("dp")
    )
    factor = token_total ** (-0.5)
    return (
        grad_tokens,
        totals[0] * factor,
        totals[1] * factor,
        totals[2] * factor,
        totals[3] * factor,
        gain_sums[0] * factor,
        gain_sums[1] * factor,
    )


def solution(mesh):
    in_specs = (P("dp", "ha", "wa", None), P("dp", "ha", "wa", None), P(), P(), P(), P(), P(), P())
    out_specs = (
        P("dp", "ha", "wa", None),
        P("ha", "wa"),
        P("ha", "wa"),
        P("ha", "wa"),
        P("ha", "wa"),
        P(),
        P(),
    )
    return jax.shard_map(body, mesh=mesh, in_specs=in_specs, out_specs=out_specs, check_vma=False)
```

profile of v0, /device:TPU:2, one launch (start us, length us, event | category | flops | bytes accessed | tf_op | source)
XLA Modules:
  0.0 552.2 jit_solution(7281656922644171538)
XLA Ops:
  13.2 14.4 %all-to-all-start = ((bf16[1,4,1,1,128,384]{5,1,3,2,0,4:T(4,128)(2,1)}), bf16[1,4,1,1,128,384]{5,1,3,2,0,4:T(4,128)(2,1)S(1)}, u32[]{:S(2)}, u32[]{:S(2)}) async-start(bf16[1,4,1,1,128,384]{5,1,3,2,0,4:T(4,128)(2,1)} %bitcast.2), calls=%async_computation | async-start | bytes 786432 | tf_op jit(solution)/shard_map/all_to_all | solution.py:173
  29.5 14.2 %all-to-all-done = bf16[1,4,1,1,128,384]{5,1,3,2,0,4:T(4,128)(2,1)S(1)} async-done(((bf16[1,4,1,1,128,384]{5,1,3,2,0,4:T(4,128)(2,1)}), bf16[1,4,1,1,128,384]{5,1,3,2,0,4:T(4,128)(2,1)S(1)}, u32[]{:S(2)}, u32[]{:S(2)}) %all-to-all-start) | async-done | bytes 393248 | tf_op jit(solution)/shard_map/all_to_all | solution.py:173
  48.4 3.7 reshape.498
  60.0 7.6 %all-to-all-start.1 = ((bf16[1,4,1,1,128,384]{5,1,3,2,0,4:T(4,128)(2,1)}), bf16[1,4,1,1,128,384]{5,1,3,2,0,4:T(4,128)(2,1)}, u32[]{:S(2)}, u32[]{:S(2)}) async-start(bf16[1,4,1,1,128,384]{5,1,3,2,0,4:T(4,128)(2,1)} %copy.155), calls=%async_computation.1 | async-start | bytes 786432 | tf_op jit(solution)/shard_map/all_to_all | solution.py:184
  69.5 3.5 fusion.97
  73.0 10.5 %all-to-all-done.1 = bf16[1,4,1,1,128,384]{5,1,3,2,0,4:T(4,128)(2,1)} async-done(((bf16[1,4,1,1,128,384]{5,1,3,2,0,4:T(4,128)(2,1)}), bf16[1,4,1,1,128,384]{5,1,3,2,0,4:T(4,128)(2,1)}, u32[]{:S(2)}, u32[]{:S(2)}) %all-to-all-start.1) | async-done | bytes 393248 | tf_op jit(solution)/shard_map/all_to_all | solution.py:184
  88.8 4.9 fusion.11
  96.2 22.1 %all_to_all.20 = bf16[1,4,1,1,128,384]{5,1,3,2,0,4:T(4,128)(2,1)S(1)} all-to-all(bf16[1,4,1,1,128,384]{5,1,3,2,0,4:T(4,128)(2,1)S(1)} %bitcast.172), channel_id=1, replica_groups=mesh['ha'=16,'wa'=8,'dp'=2] {'ha','wa'}, dimensions={4} | all-to-all | bytes 786432 | tf_op jit(solution)/shard_map/all_to_all | solution.py:173
  123.5 55.0 %reduce-scatter.37.cloned.1.call-done = bf16[24,384]{1,0:T(8,128)(2,1)} async-done(((bf16[384,384]{1,0:T(8,128)(2,1)}), bf16[24,384]{1,0:T(8,128)(2,1)}) %reduce-scatter.37.cloned.1.call-update) | async-done | bytes 18448
  180.0 3.5 convolution_convert_fusion.2
  190.4 3.7 fusion.33
  194.1 6.9 %fusion.23 = bf16[8,49,1,12,32]{1,4,3,0,2:T(8,128)(2,1)} fusion(f32[8,12,49,49]{2,3,1,0:T(8,128)} %fusion.33, bf16[8,49,1,12,32]{1,0,4,3,2:T(8,128)(2,1)} %copy-done.4, f32[8,12,49,49]{2,3,1,0:T(8,128)} %copy-done.7, f32[8,12,49]{2,1,0:T(8,128)S(1)} %copy-done.23), kind=kOutput, calls=%fused_computation.34 | convolution fusion | flops 16830960 | bytes 2464896 | tf_op jit(solution)/shard_map/ghqk,gqhd->gkhd/dot_general | solution.py:14
  201.0 6.8 %fusion.20 = bf16[8,49,1,12,32]{1,4,3,0,2:T(8,128)(2,1)} fusion(f32[8,12,49,49]{2,3,1,0:T(8,128)} %fusion.33, bf16[8,49,1,12,32]{1,0,4,3,2:T(8,128)(2,1)S(1)} %copy-done.3, f32[8,12,49,49]{2,3,1,0:T(8,128)} %copy-done.7, f32[8,12,49]{2,1,0:T(8,128)S(1)} %copy-done.23), kind=kOutput, calls=%fused_computation.33 | convolution fusion | flops 16830960 | bytes 2464896 | tf_op jit(solution)/shard_map/ghqk,gkhd->gqhd/dot_general | solution.py:14
  211.4 4.2 copy.174
  215.5 4.4 convert_element_type.196
  223.2 3.9 fusion.2
  236.8 12.6 %all-to-all-start.3 = ((bf16[1,4,1,1,128,384]{5,1,3,2,0,4:T(4,128)(2,1)}), bf16[1,4,1,1,128,384]{5,1,3,2,0,4:T(4,128)(2,1)S(1)}, u32[]{:S(2)}, u32[]{:S(2)}) async-start(bf16[1,4,1,1,128,384]{5,1,3,2,0,4:T(4,128)(2,1)} %copy.178), calls=%async_computation.3 | async-start | bytes 786432 | tf_op jit(solution)/shard_map/all_to_all | solution.py:184
  250.9 14.6 %all-to-all-done.3 = bf16[1,4,1,1,128,384]{5,1,3,2,0,4:T(4,128)(2,1)S(1)} async-done(((bf16[1,4,1,1,128,384]{5,1,3,2,0,4:T(4,128)(2,1)}), bf16[1,4,1,1,128,384]{5,1,3,2,0,4:T(4,128)(2,1)S(1)}, u32[]{:S(2)}, u32[]{:S(2)}) %all-to-all-start.3) | async-done | bytes 393248 | tf_op jit(solution)/shard_map/all_to_all | solution.py:184
  268.6 72.8 %all-reduce.6 = (f32[384]{0:T(512)S(1)}, f32[384]{0:T(512)S(1)}) all-reduce(f32[384]{0:T(512)S(1)} %get-tuple-element.52, f32[384]{0:T(512)S(1)} %get-tuple-element.50), channel_id=1, replica_groups=mesh['ha'=16,'wa'=8,'dp'=2] {'ha','wa','dp'}, use_global_device_ids=true, to_apply=%region_23.32 | all-reduce | flops 768 | bytes 6144 | tf_op jit(solution)/shard_map/psum | solution.py:295
  350.9 62.0 %reduce-scatter.33.cloned.1.call-done = bf16[24,1536]{1,0:T(8,128)(2,1)} async-done(((bf16[384,1536]{1,0:T(8,128)(2,1)}), bf16[24,1536]{1,0:T(8,128)(2,1)}) %reduce-scatter.33.cloned.1.call-update) | async-done | bytes 73744
  415.3 39.1 %reduce-scatter.31.cloned.1.call-done = bf16[48,96]{1,0:T(8,128)(2,1)} async-done(((bf16[384,96]{1,0:T(8,128)(2,1)}), bf16[48,96]{1,0:T(8,128)(2,1)}) %reduce-scatter.31.cloned.1.call-update) | async-done | bytes 9232
  455.1 37.1 %reduce-scatter.27.cloned.1.call-done = bf16[48,72]{1,0:T(8,128)(2,1)} async-done(((bf16[384,72]{1,0:T(8,128)(2,1)}), bf16[48,72]{1,0:T(8,128)(2,1)}) %reduce-scatter.27.cloned.1.call-update) | async-done | bytes 6928
  493.0 37.4 %reduce-scatter.25.cloned.1.call-done = bf16[24,192]{0,1:T(8,128)(2,1)} async-done(((bf16[24,1536]{0,1:T(8,128)(2,1)}), bf16[24,192]{0,1:T(8,128)(2,1)}) %reduce-scatter.25.cloned.1.call-update) | async-done | bytes 9232 | tf_op jit(solution)/shard_map/reduce_scatter | solution.py:285
  530.4 12.0 %all-reduce.7 = (bf16[72,48]{1,0:T(8,128)(2,1)S(1)}, bf16[24,48]{1,0:T(8,128)(2,1)S(1)}, bf16[96,48]{1,0:T(8,128)(2,1)S(1)}, bf16[24,192]{0,1:T(8,128)(2,1)S(1)}) all-reduce(bf16[72,48]{1,0:T(8,128)(2,1)S(1)} %copy.194, bf16[24,48]{1,0:T(8,128)(2,1)S(1)} %copy.196, ...), channel_id=1, replica_groups=mesh['ha'=16,'wa'=8,'dp'=2] {'dp'}, use_global_device_ids=true, to_apply=%region_12.21 | all-reduce | flops 13824 | bytes 55296 | tf_op jit(solution)/shard_map/psum | solution.py:290
  (225 shorter events, 79.9 us)
Async XLA Ops:
  7.2 81.6 %copy-start = (bf16[1536,384]{1,0:T(8,128)(2,1)S(1)}, bf16[1536,384]{1,0:T(8,128)(2,1)}, u32[]{:S(2)}) copy-start(bf16[1536,384]{1,0:T(8,128)(2,1)} %param.30) | copy-start | bytes 3538948
  13.2 32.8 %copy-start.19 = (bf16[1152,384]{1,0:T(8,128)(2,1)S(1)}, bf16[1152,384]{1,0:T(8,128)(2,1)}, u32[]{:S(2)}) copy-start(bf16[1152,384]{1,0:T(8,128)(2,1)} %param.28) | copy-start | bytes 2654212
  13.2 30.5 %all-to-all-start = ((bf16[1,4,1,1,128,384]{5,1,3,2,0,4:T(4,128)(2,1)}), bf16[1,4,1,1,128,384]{5,1,3,2,0,4:T(4,128)(2,1)S(1)}, u32[]{:S(2)}, u32[]{:S(2)}) async-start(bf16[1,4,1,1,128,384]{5,1,3,2,0,4:T(4,128)(2,1)} %bitcast.2), calls=%async_computation | async-start | bytes 786432 | tf_op jit(solution)/shard_map/all_to_all | solution.py:173
  28.9 17.0 %copy-start.33 = (pred[7]{0:T(512)(128)(4,1)}, pred[7]{0:T(512)(128)(4,1)S(1)}, u32[]{:S(2)}) copy-start(pred[7]{0:T(512)(128)(4,1)S(1)} %compare_and_fusion.2) | copy-start | bytes 25
  29.4 16.5 %copy-start.25 = (pred[14]{0:T(512)(128)(4,1)}, pred[14]{0:T(512)(128)(4,1)S(1)}, u32[]{:S(2)}) copy-start(pred[14]{0:T(512)(128)(4,1)S(1)} %get-tuple-element.65) | copy-start | bytes 46
  57.9 10.4 %copy-start.1 = (bf16[4,14,7,384]{3,0,2,1:T(4,128)(2,1)S(1)}, bf16[4,14,7,384]{3,0,2,1:T(4,128)(2,1)}, u32[]{:S(2)}) copy-start(bf16[4,14,7,384]{3,0,2,1:T(4,128)(2,1)} %param.24) | copy-start | bytes 903172
  60.0 23.5 %all-to-all-start.1 = ((bf16[1,4,1,1,128,384]{5,1,3,2,0,4:T(4,128)(2,1)}), bf16[1,4,1,1,128,384]{5,1,3,2,0,4:T(4,128)(2,1)}, u32[]{:S(2)}, u32[]{:S(2)}) async-start(bf16[1,4,1,1,128,384]{5,1,3,2,0,4:T(4,128)(2,1)} %copy.155), calls=%async_computation.1 | async-start | bytes 786432 | tf_op jit(solution)/shard_map/all_to_all | solution.py:184
  67.6 110.9 %reduce-scatter.37.cloned.1.call-start = ((), (), s32[]{:S(2)}) async-start(), calls=%async_computation.19 | async-start | bytes 313344
  95.0 23.3 %copy-start.8 = (bf16[392,384]{1,0:T(8,128)(2,1)}, bf16[392,384]{1,0:T(8,128)(2,1)S(1)}, u32[]{:S(2)}) copy-start(bf16[392,384]{1,0:T(8,128)(2,1)S(1)} %add_convert_fusion.1) | copy-start | bytes 903172
  95.5 24.3 %copy-start.26 = (pred[14]{0:T(512)(128)(4,1)S(1)}, pred[14]{0:T(512)(128)(4,1)}, u32[]{:S(2)}) copy-start(pred[14]{0:T(512)(128)(4,1)} %copy-done.25) | copy-start | bytes 46
  95.9 26.0 %copy-start.34 = (pred[7]{0:T(512)(128)(4,1)S(1)}, pred[7]{0:T(512)(128)(4,1)}, u32[]{:S(2)}) copy-start(pred[7]{0:T(512)(128)(4,1)} %copy-done.33) | copy-start | bytes 25
  120.9 59.1 %copy-start.28 = (f32[384]{0:T(512)S(1)}, f32[384]{0:T(512)}, u32[]{:S(2)}) copy-start(f32[384]{0:T(512)} %param.27) | copy-start | bytes 4612
  123.4 126.7 %reduce-scatter.29.cloned.1.call-start = ((), (), s32[]{:S(2)}) async-start(), calls=%async_computation.15 | async-start | bytes 110592
  180.0 161.5 %reduce-scatter.23.cloned.1.call-start = ((), (), s32[]{:S(2)}) async-start(), calls=%async_computation.12 | async-start | bytes 1253376 | tf_op jit(solution)/shard_map/reduce_scatter | solution.py:268
  183.6 164.2 %reduce-scatter.35.cloned.1.call-start = ((), (), s32[]{:S(2)}) async-start(), calls=%async_computation.18 | async-start | bytes 940032
  222.9 190.0 %reduce-scatter.33.cloned.1.call-start = ((), (), s32[]{:S(2)}) async-start(), calls=%async_computation.17 | async-start | bytes 1253376
  234.6 14.8 %copy-start.11 = (f32[4,14,7]{0,2,1:T(8,128)S(1)}, f32[4,14,7]{0,2,1:T(8,128)}, u32[]{:S(2)}) copy-start(f32[4,14,7]{0,2,1:T(8,128)} %copy-done.10) | copy-start | bytes 4708
  234.6 15.0 %copy-start.18 = (f32[4,14,7]{0,2,1:T(8,128)S(1)}, f32[4,14,7]{0,2,1:T(8,128)}, u32[]{:S(2)}) copy-start(f32[4,14,7]{0,2,1:T(8,128)} %copy-done.17) | copy-start | bytes 4708
  234.7 31.3 %copy-start.24 = (f32[384]{0:T(512)S(1)}, f32[384]{0:T(512)}, u32[]{:S(2)}) copy-start(f32[384]{0:T(512)} %param.26) | copy-start | bytes 4612
  236.8 28.7 %all-to-all-start.3 = ((bf16[1,4,1,1,128,384]{5,1,3,2,0,4:T(4,128)(2,1)}), bf16[1,4,1,1,128,384]{5,1,3,2,0,4:T(4,128)(2,1)S(1)}, u32[]{:S(2)}, u32[]{:S(2)}) async-start(bf16[1,4,1,1,128,384]{5,1,3,2,0,4:T(4,128)(2,1)} %copy.178), calls=%async_computation.3 | async-start | bytes 786432 | tf_op jit(solution)/shard_map/all_to_all | solution.py:184
  249.4 204.9 %reduce-scatter.31.cloned.1.call-start = ((), (), s32[]{:S(2)}) async-start(), calls=%async_computation.16 | async-start | bytes 110592
  265.5 77.6 %copy-start.9 = (bf16[392,384]{1,0:T(8,128)(2,1)S(1)}, bf16[392,384]{1,0:T(8,128)(2,1)}, u32[]{:S(2)}) copy-start(bf16[392,384]{1,0:T(8,128)(2,1)} %copy-done.8) | copy-start | bytes 903172
  343.1 149.1 %reduce-scatter.27.cloned.1.call-start = ((), (), s32[]{:S(2)}) async-start(), calls=%async_computation.14 | async-start | bytes 110592
  349.3 181.1 %reduce-scatter.25.cloned.1.call-start = ((), (), s32[]{:S(2)}) async-start(), calls=%async_computation.13 | async-start | bytes 442368 | tf_op jit(solution)/shard_map/reduce_scatter | solution.py:285
  (23 other events, 67.3 us)
Sparse Core Ops, SparseCore 0:
  123.6 54.8 reduce-scatter.36
  181.1 38.6 reduce-scatter.28
  222.4 60.3 reduce-scatter.22
  285.1 62.5 reduce-scatter.34
  350.1 62.6 reduce-scatter.32
  415.2 39.0 reduce-scatter.30
  457.0 35.1 reduce-scatter.26
  494.7 35.6 reduce-scatter.24
where the time goes:
time: 558 us; the launch traced here: 552 us
  waiting for transfers between devices  273 us (49%)
  blocking collectives  107 us (19%)
  local copies, waits for them, and re-layouts  53.9 us (10%)
  matrix products  48.9 us (9%)
  starting transfers between devices  35.8 us (6%)
  other arithmetic  17.9 us (3%)
  between operations  15.5 us (3%)
    unnamed x14, waiting for transfers between devices  196 us
    psum x1, blocking collectives, body(): lax.psum((partial_value[4], partial_value[5]), ('ha', 'wa', 'dp'))  72.8 us
    reduce_scatter x1, waiting for transfers between devices, body(): lax.psum_scatter(row_sums[3].astype(jnp.bfloat16), 'wa', scatter_dimensio...  37.4 us
    all_to_all x2, waiting for transfers between devices, route_out(): lax.all_to_all(joined, ('ha', 'wa'), split_axis=4, concat_axis=4, tiled=T...  25.1 us
    dot_general x6, matrix products, contract(): return jnp.einsum(form, left, right, preferred_element_type=jnp.float32)  22.2 us
    all_to_all x1, blocking collectives, route_in(): lax.all_to_all(joined, ('ha', 'wa'), split_axis=4, concat_axis=4, tiled=T...  22.1 us
    all_to_all x2, starting transfers between devices, route_out(): lax.all_to_all(joined, ('ha', 'wa'), split_axis=4, concat_axis=4, tiled=T...  20.1 us
    unnamed x85, local copies, waits for them, and re-layouts  16.2 us
  transfers between devices with their start and end apart: 11, of which 9 were waited for; matrix products, arithmetic and copies ran while one was open for 14% of the time, Pallas kernels for 0%

commit v1 on v0

v1 whole, which is shorter than its diff:
```python
import functools

import jax
import jax.numpy as jnp
from jax import lax
from jax.experimental import pallas as pl
from jax.experimental.pallas import tpu as pltpu
from jax.sharding import Mesh, PartitionSpec as P

HEADS = 12
GRID = 7
EPSILON = 1e-05
SLOTS = 128
ROWS = 64
LINES = 14
QUAD = 4
F32 = jnp.float32
BF16 = jnp.bfloat16
HA = ("y", "xl", "core")


def dot(left, right):
    return jnp.dot(left, right, preferred_element_type=F32)


def dot_nt(left, right):
    return lax.dot_general(left, right, (((1,), (1,)), ((), ())), preferred_element_type=F32)


def dot_tn(left, right):
    return lax.dot_general(left, right, (((0,), (0,)), ((), ())), preferred_element_type=F32)


def iota(shape, dim):
    return lax.broadcasted_iota(jnp.int32, shape, dim)


def position():
    rows = (lax.axis_index("y") * 2 + lax.axis_index("xl")) * 2 + lax.axis_index("core")
    return rows, lax.axis_index("wa")


def group_match(slot, member):
    row, col = position()
    parity, local = member >> 6, member & 63
    band_row = (local * 37) >> 8
    band_col = local - GRID * band_row
    offset_row = row + 16 * parity + 32 * band_row - LINES * (slot >> 3)
    offset_col = col + 8 * band_col - GRID * (slot & 7)
    hit = jnp.logical_and(offset_row >= 0, offset_row < LINES)
    hit = jnp.logical_and(hit, jnp.logical_and(offset_col >= 0, offset_col < GRID))
    return jnp.logical_and(hit, local < GRID * GRID)


def owner_slot(line, column):
    row, col = position()
    return ((LINES * row + line) & 15) * 8 + ((GRID * col + column) & 7)


def one_hot(hit):
    return jnp.where(hit, 1.0, 0.0).astype(BF16)


def norm_parts(values):
    centered = values - jnp.mean(values, axis=-1, keepdims=True)
    inv_std = lax.rsqrt(jnp.mean(centered * centered, axis=-1, keepdims=True) + EPSILON)
    return centered * inv_std, inv_std


def norm_back(grad, normal_hat, inv_std, gain):
    grad_hat = grad * gain
    first = jnp.mean(grad_hat, axis=-1, keepdims=True)
    second = jnp.mean(grad_hat * normal_hat, axis=-1, keepdims=True)
    return inv_std * (grad_hat - first - normal_hat * second)


def head_mask(shape):
    return (iota(shape, 0) >> 6) == (iota(shape, 1) >> 5)


def spread(values, mask):
    tiled = jnp.concatenate([values] * QUAD, axis=0)
    return jnp.where(mask, tiled, jnp.zeros_like(tiled))


def gather_heads(values):
    lanes = iota((ROWS, 128), 1) >> 5
    total = jnp.where(lanes == 0, values[:ROWS], 0.0)
    for head in range(1, QUAD):
        total = total + jnp.where(lanes == head, values[head * ROWS : (head + 1) * ROWS], 0.0)
    return total


def probabilities(key, query_spread, scale):
    scores = dot_nt(key, query_spread) * scale
    expo = jnp.where(iota(scores.shape, 0) < GRID * GRID, jnp.exp(scores), 0.0)
    return expo * (1.0 / jnp.sum(expo, axis=0, keepdims=True))


def load_every(ref, start, step):
    parts = [ref[part, pl.ds(start, SLOTS, stride=step), :] for part in range(3)]
    return jnp.concatenate(parts, axis=1).astype(BF16)


def store_every(ref, start, step, values):
    for part in range(3):
        ref[part, pl.ds(start, SLOTS, stride=step), :] = values[:, part * 128 : (part + 1) * 128]


def send_kernel(tokens_hbm, grad_hbm, out_ref, tokens_ref, grad_ref, sems):
    copies = [
        pltpu.make_async_copy(tokens_hbm, tokens_ref, sems.at[0]),
        pltpu.make_async_copy(grad_hbm, grad_ref, sems.at[1]),
    ]
    for copy in copies:
        copy.start()
    for copy in copies:
        copy.wait()
    for line in range(16):
        for column in range(8):
            slot = owner_slot(line, column)
            if line < LINES and column < GRID:
                unit = jnp.concatenate(
                    [tokens_ref[line, column].astype(F32), grad_ref[line, column].astype(F32)], axis=0
                ).astype(BF16)
            else:
                unit = jnp.zeros((8, 384), BF16)
            out_ref[slot] = unit


def return_kernel(recv_ref, out_ref):
    for line in range(LINES):
        for column in range(GRID):
            out_ref[line, column] = recv_ref[owner_slot(line, column)]


def gelu_parts(hidden, grad):
    inner = 0.7978845608028654
    square = hidden * hidden
    tanh = jnp.tanh(inner * (hidden + 0.044715 * (hidden * square)))
    half = 0.5 * (1.0 + tanh)
    slope = half + 0.5 * hidden * (1.0 - tanh * tanh) * (
        inner * (1.0 + 3 * 0.044715 * square)
    )
    return hidden * half, grad * slope


def forward_kernel(
    recv_ref, gain_one, w_qkv, w_proj,
    x_ref, qkv_ref, mixed_ref, resid_ref, grad_ref, arrived, normed,
):
    for part in range(3):
        arrived[part] = recv_ref[:, part * 128 : (part + 1) * 128].astype(F32)
    match = one_hot(group_match(iota((SLOTS, SLOTS), 1), iota((SLOTS, SLOTS), 0)))
    for crop in range(4):
        rows = pl.ds(crop * SLOTS, SLOTS)
        x = dot(match, load_every(arrived, crop, 8))
        x_ref[rows, :] = x.astype(BF16)
        normal_hat, _ = norm_parts(x)
        normed[rows, :] = (normal_hat * gain_one[...]).astype(BF16)
        grad_ref[rows, :] = dot(match, load_every(arrived, crop + 4, 8)).astype(BF16)
    for part in range(3):
        cols = pl.ds(part * 384, 384)
        qkv_ref[:, cols] = dot_nt(normed[...], w_qkv[cols, :]).astype(BF16)
    mask = head_mask((QUAD * ROWS, 128))
    scale = 32.0 ** -0.5

    @pl.loop(0, 4)
    def _(pair):
        units = unit_places(pair)
        query = [spread(qkv_ref[rows, pl.ds(lane, 128)], mask) for rows, lane in units]
        probs = [
            probabilities(qkv_ref[rows, pl.ds(384 + lane, 128)], query[n], scale).astype(BF16)
            for n, (rows, lane) in enumerate(units)
        ]
        mixed = [
            dot_tn(probs[n], qkv_ref[rows, pl.ds(768 + lane, 128)])
            for n, (rows, lane) in enumerate(units)
        ]
        for n, (rows, lane) in enumerate(units):
            mixed_ref[rows, pl.ds(lane, 128)] = gather_heads(mixed[n]).astype(BF16)

    for crop in range(4):
        rows = pl.ds(crop * SLOTS, SLOTS)
        branch = dot_nt(mixed_ref[rows, :], w_proj[...]).astype(BF16)
        resid_ref[rows, :] = (x_ref[rows, :].astype(F32) + branch.astype(F32)).astype(BF16)


def unit_places(pair):
    places = []
    for half in range(2):
        rows = pl.ds(pl.multiple_of(pair * 2 * ROWS + half * ROWS, ROWS), ROWS)
        places.extend((rows, quad * 128) for quad in range(3))
    return places


def mlp_kernel(
    grad_out, resid, gain_two, w_up, w_down,
    resid_grad_ref, keep_ref, send_ref, gain_ref,
    normed, hidden_grad, grad_turned, up_total, down_total, back, piece_rows,
):
    for crop in range(4):
        rows = pl.ds(crop * SLOTS, SLOTS)
        normal_hat, _ = norm_parts(resid[rows, :].astype(F32))
        normed[rows, :] = (normal_hat * gain_two[...]).astype(BF16)
        grad_turned[:, rows] = grad_out[rows, :].astype(F32).T.astype(BF16)
    back[...] = jnp.zeros_like(back)

    @pl.loop(0, 4)
    def _(chunk):
        cols = pl.ds(pl.multiple_of(chunk * 384, 384), 384)
        hidden = dot_nt(normed[...], w_up[cols, :])
        grad_act = dot(grad_out[...], w_down[:, cols])
        activated, grad_hidden = gelu_parts(hidden, grad_act)
        hidden_grad[...] = grad_hidden.astype(BF16)
        down_total[:, cols] = dot(grad_turned[...], activated.astype(BF16))
        up_total[cols, :] = dot_tn(hidden_grad[...], normed[...])
        back[...] += dot(hidden_grad[...], w_up[cols, :])

    for ref, side in piece_sides(keep_ref, send_ref):
        for piece in range(8):
            owner = 2 * piece + side
            piece_rows[:96, :] = up_total[pl.ds(pl.multiple_of(owner * 96, 8), 96), :]
            for part in range(4):
                piece_rows[96 + 24 * part : 120 + 24 * part, :] = down_total[
                    pl.ds(pl.multiple_of(owner * 24, 8), 24), part * 384 : (part + 1) * 384
                ]
            ref[piece] = piece_rows[...].astype(BF16)
    gain = jnp.zeros((1, 384), F32)
    for crop in range(4):
        rows = pl.ds(crop * SLOTS, SLOTS)
        normal_hat, inv_std = norm_parts(resid[rows, :].astype(F32))
        grad = back[rows, :]
        gain = gain + jnp.sum(grad * normal_hat, axis=0, keepdims=True)
        resid_grad_ref[rows, :] = (
            grad_out[rows, :].astype(F32) + norm_back(grad, normal_hat, inv_std, gain_two[...])
        ).astype(BF16)
    gain_ref[...] = gain


def piece_sides(keep_ref, send_ref):
    core = lax.axis_index("core")
    return (keep_ref, core), (send_ref, 1 - core)


def attention_kernel(
    x_ref, qkv_ref, resid_grad_ref, gain_one, w_qkv, w_proj,
    out_ref, rows_grad, normed_ref, gain_ref, grad_mixed, slots,
):
    grad_mixed[...] = dot(resid_grad_ref[...], w_proj[...]).astype(BF16)
    mask = head_mask((QUAD * ROWS, 128))
    scale = 32.0 ** -0.5

    @pl.loop(0, 4)
    def _(pair):
        units = unit_places(pair)
        count = range(len(units))
        query = [spread(qkv_ref[rows, pl.ds(lane, 128)], mask) for rows, lane in units]
        grad = [spread(grad_mixed[rows, pl.ds(lane, 128)], mask) for rows, lane in units]
        key = [qkv_ref[rows, pl.ds(384 + lane, 128)] for rows, lane in units]
        probs = [probabilities(key[n], query[n], scale) for n in count]
        grad_probs = [
            dot_nt(qkv_ref[rows, pl.ds(768 + lane, 128)], grad[n])
            for n, (rows, lane) in enumerate(units)
        ]
        grad_scores = []
        for n in count:
            centre = jnp.sum(grad_probs[n] * probs[n], axis=0, keepdims=True)
            grad_scores.append((probs[n] * (grad_probs[n] - centre) * scale).astype(BF16))
        for n, (rows, lane) in enumerate(units):
            rows_grad[rows, pl.ds(768 + lane, 128)] = dot(probs[n].astype(BF16), grad[n]).astype(BF16)
            rows_grad[rows, pl.ds(384 + lane, 128)] = dot(grad_scores[n], query[n]).astype(BF16)
            rows_grad[rows, pl.ds(lane, 128)] = gather_heads(
                dot_tn(grad_scores[n], key[n])
            ).astype(BF16)

    match = one_hot(group_match(iota((SLOTS, SLOTS), 0), iota((SLOTS, SLOTS), 1)))
    gain = jnp.zeros((1, 384), F32)
    for crop in range(4):
        rows = pl.ds(crop * SLOTS, SLOTS)
        grad = dot(rows_grad[rows, :], w_qkv[...]).astype(BF16).astype(F32)
        normal_hat, inv_std = norm_parts(x_ref[rows, :].astype(F32))
        normed_ref[rows, :] = (normal_hat * gain_one[...]).astype(BF16)
        gain = gain + jnp.sum(grad * normal_hat, axis=0, keepdims=True)
        grad_x = resid_grad_ref[rows, :].astype(F32) + norm_back(
            grad, normal_hat, inv_std, gain_one[...]
        )
        store_every(slots, crop, 4, dot(match, grad_x.astype(BF16)))
    for slot in range(SLOTS):
        for part in range(3):
            out_ref[slot, :, part * 128 : (part + 1) * 128] = slots[
                part, slot * 4 : slot * 4 + 4, :
            ].astype(BF16)
    gain_ref[...] = gain


def weight_kernel(
    rows_grad, normed, resid_grad, mixed, first, second, keep_ref, send_ref,
    qkv_total, proj_total, piece_rows,
):
    for part in range(3):
        cols = pl.ds(part * 384, 384)
        qkv_total[cols, :] = dot_tn(rows_grad[:, cols], normed[...])
    proj_total[...] = dot_tn(resid_grad[...], mixed[...])
    piece_rows[96:, :] = jnp.zeros((16, 384), F32)
    piece_rows[96:97, :] = first[...]
    piece_rows[97:98, :] = second[...]
    for ref, side in piece_sides(keep_ref, send_ref):
        for piece in range(8):
            owner = 2 * piece + side
            piece_rows[:72, :] = qkv_total[pl.ds(pl.multiple_of(owner * 72, 8), 72), :]
            piece_rows[72:96, :] = proj_total[pl.ds(pl.multiple_of(owner * 24, 8), 24), :]
            ref[piece] = piece_rows[...].astype(BF16)


def core_kernel(early_keep, early_recv, late_keep, late_recv, *outs):
    row = lax.axis_index("y")
    for step in range(4):
        place = (row + step) & 3
        for col in range(2):
            piece = place * 2 + col
            outs[step][col, :192] = (
                early_keep[piece].astype(F32) + early_recv[piece].astype(F32)
            ).astype(BF16)
            outs[step][col, 192:] = (
                late_keep[piece].astype(F32) + late_recv[piece].astype(F32)
            ).astype(BF16)


def pack_columns(rows, col):
    low = pltpu.roll(rows[:48], (384 - 48 * col) % 384, 1)[:, :128]
    high = pltpu.roll(rows[48:96], (384 + 64 - 48 * col) % 384, 1)[:, :128]
    return jnp.where(iota((48, 128), 1) < 64, low, high)


def pack_kernel(own, one, two, three, out_ref, gains):
    row = lax.axis_index("y")
    for step, ref in enumerate((own, one, two, three)):
        gains[(row - step) & 3] = ref[0, 288:].astype(F32)
    gain = (gains[0] + gains[1]) + (gains[2] + gains[3])
    gain_rows = [
        gain[which : which + 1, part * 128 : (part + 1) * 128]
        for which in range(2)
        for part in range(3)
    ]
    gain_rows.append(jnp.zeros((2, 128), F32))
    for side in range(2):
        total = own[side, :288].astype(F32) + one[side, :288].astype(F32)
        total = total + (two[side, :288].astype(F32) + three[side, :288].astype(F32))
        for col in range(8):
            start = 96 + 24 * (col // 2)
            block = total[start : start + 24]
            if col % 2:
                block = pltpu.roll(block, 192, 1)
            out_ref[side * 8 + col] = jnp.concatenate(
                [pack_columns(total[:96], col), block[:, :128], block[:, 128:256]]
                + [pack_columns(total[192:], col)] + gain_rows,
                axis=0,
            ).astype(BF16)


def block_sum(recv_ref, out_ref):
    total = recv_ref[0].astype(F32)
    for place in range(1, 16):
        total = total + recv_ref[place].astype(F32)
    out_ref[...] = total.astype(BF16)


def unpack_columns(packed):
    low = packed[:, :48]
    high = pltpu.roll(packed, 64, 1)[:, :48]
    wide = jnp.concatenate([low, high], axis=0)
    wide = jnp.concatenate([wide, jnp.zeros((96, 80), F32)], axis=1)
    wide = jnp.concatenate([wide, jnp.zeros((32, 128), F32)], axis=0)
    return wide.T[:48]


def final_weights(
    own_ref, other_ref,
    qkv_ref, proj_ref, up_ref, down_ref, first_ref, second_ref, factor,
):
    total = (own_ref[...].astype(F32) + other_ref[...].astype(F32)) * factor
    early, late = total[:96], total[96:]
    up_ref[...] = unpack_columns(early[:48])[:, :96]
    down_ref[:, :128] = early[48:72]
    down_ref[:, 128:] = early[72:96, :64]
    qkv_ref[...] = unpack_columns(late[:48])[:, :72]
    proj_ref[...] = pltpu.roll(late[:48], 64, 1)[24:48, :48]
    for part in range(3):
        lane = pl.ds(part * 128, 128)
        first_ref[lane] = late[48 + part]
        second_ref[lane] = late[51 + part]


def call(kernel, outs, scratch=(), flops=0, nbytes=0, space=pltpu.VMEM):
    vmem = pl.BlockSpec(memory_space=pltpu.VMEM)
    scratch = [pltpu.VMEM(*item) if isinstance(item, tuple) else item for item in scratch]

    def run(*args):
        return pl.pallas_call(
            kernel,
            out_shape=[jax.ShapeDtypeStruct(shape, dtype) for shape, dtype in outs],
            in_specs=[pl.BlockSpec(memory_space=space)] * len(args),
            out_specs=[vmem] * len(outs),
            scratch_shapes=scratch,
            compiler_params=pltpu.CompilerParams(vmem_limit_bytes=24 << 20),
            cost_estimate=pl.CostEstimate(flops=flops, bytes_accessed=nbytes, transcendentals=0),
        )(*args)

    return run


def exchange(values, axes):
    return lax.all_to_all(values, axes, split_axis=0, concat_axis=0, tiled=True)


def swap(values, axis):
    return lax.ppermute(values, axis, [(0, 1), (1, 0)])


def body(tokens, grad_out, gain_first, gain_second, w_qkv, w_proj, w_up, w_down):
    gain_one, gain_two = gain_first.reshape(1, 384), gain_second.reshape(1, 384)
    factor = (8 * 224 * 56) ** -0.5
    tile = pltpu.VMEM((LINES, GRID, 4, 384), BF16)
    (sent,) = call(
        send_kernel,
        [((SLOTS, 8, 384), BF16)],
        [tile, tile, pltpu.SemaphoreType.DMA((2,))],
        nbytes=2 * 10**6,
        space=pltpu.HBM,
    )(
        tokens.transpose(1, 2, 0, 3), grad_out.transpose(1, 2, 0, 3)
    )
    arrived = exchange(sent, HA + ("wa",)).reshape(SLOTS * 8, 384)
    rows = ((512, 384), BF16)
    x, qkv, mixed, resid, grad_rows = call(
        forward_kernel,
        [rows, ((512, 1152), BF16), rows, rows, rows],
        [((3, 1024, 128), F32), rows],
        flops=10**9, nbytes=4 * 10**6,
    )(arrived, gain_one, w_qkv, w_proj)
    resid_grad, early_keep, early_send, gain_sum_two = call(
        mlp_kernel,
        [rows, ((8, 192, 384), BF16), ((8, 192, 384), BF16), ((1, 384), F32)],
        [
            rows, rows, ((384, 512), BF16), ((1536, 384), F32), ((384, 1536), F32),
            ((512, 384), F32), ((192, 384), F32),
        ],
        flops=3 * 10**9, nbytes=6 * 10**6,
    )(grad_rows, resid, gain_two, w_up, w_down)
    slots, rows_grad, normed, gain_sum_one = call(
        attention_kernel,
        [((SLOTS, 4, 384), BF16), ((512, 1152), BF16), rows, ((1, 384), F32)],
        [rows, ((3, 512, 128), F32)],
        flops=6 * 10**9, nbytes=20 * 10**6,
    )(x, qkv, resid_grad, gain_one, w_qkv, w_proj)
    returned = exchange(slots, HA + ("wa",))
    late_keep, late_send = call(
        weight_kernel,
        [((8, 112, 384), BF16), ((8, 112, 384), BF16)],
        [((1152, 384), F32), ((384, 384), F32), ((112, 384), F32)],
        flops=10**9, nbytes=5 * 10**6,
    )(rows_grad, normed, resid_grad, mixed, gain_sum_one, gain_sum_two)
    piece = ((2, 304, 384), BF16)
    own, *others = call(core_kernel, [piece] * 4, nbytes=10**7)(
        early_keep, swap(early_send, "core"), late_keep, swap(late_send, "core")
    )
    arrived = [
        lax.ppermute(values, "y", [(place, (place + step) % 4) for place in range(4)])
        for step, values in zip((1, 2, 3), others)
    ]
    (blocks,) = call(
        pack_kernel, [((16, 152, 128), BF16)], [((4, 16, 384), F32)], nbytes=3 * 10**6
    )(own, *arrived)
    blocks, returned = lax.optimization_barrier((blocks, returned))
    (total,) = call(block_sum, [((152, 128), BF16)], nbytes=10**6)(exchange(blocks, ("xl", "wa")))
    other = swap(total, "dp")
    grad_qkv, grad_proj, grad_up, grad_down, first, second = call(
        functools.partial(final_weights, factor=factor),
        [
            ((48, 72), F32), ((24, 48), F32), ((48, 96), F32), ((24, 192), F32),
            ((384,), F32), ((384,), F32),
        ],
        nbytes=10**6,
    )(total, other)
    (grad_tile,) = call(return_kernel, [((LINES, GRID, 4, 384), BF16)], nbytes=10**6)(returned)
    return (
        grad_tile.transpose(2, 0, 1, 3), grad_qkv.T, grad_proj, grad_up.T, grad_down, first, second,
    )


def solution(mesh):
    fine = Mesh(mesh.devices.reshape(4, 2, 2, 8, 2), HA + ("wa", "dp"))
    tile = P("dp", HA, "wa", None)
    block = P(HA, "wa")
    return jax.shard_map(
        body,
        mesh=fine,
        in_specs=(tile, tile, P(), P(), P(), P(), P(), P()),
        out_specs=(tile, block, block, block, block, P(), P()),
        check_vma=False,
    )
```

time: 558 us -> 136 us (0.24)
  waiting for transfers between devices: 273 us -> 48.2 us
  blocking collectives: 107 us -> 25.3 us
  local copies, waits for them, and re-layouts: 53.9 us -> 3.9 us
  matrix products: 48.9 us -> 0 us
  Pallas kernels: 0 us -> 26.3 us
  other arithmetic: 17.9 us -> 0 us
  between operations: 15.5 us -> 0.8 us
    unnamed x14 -> x0, waiting for transfers between devices: 196 us -> none
    psum x2 -> x0, blocking collectives: 84.8 us -> none  [the longest x1 72.8 us: body(): lax.psum((partial_value[4], partial_value[5]), ('ha', 'wa', 'dp'))]
    dot_general x17 -> x0, matrix products: 48.9 us -> none  [the longest x6 22.2 us: contract(): return jnp.einsum(form, left, right, preferred_element_type=jnp.float32)]
    reduce_scatter x2 -> x0, waiting for transfers between devices: 37.4 us -> none  [the longest x1 37.4 us: body(): lax.psum_scatter(row_sums[3].astype(jnp.bfloat16), 'wa', scatter_dimensio...]
    pallas_call x0 -> x10, Pallas kernels: none -> 26.3 us  [run(): pl.pallas_call(kernel, out_shape=[jax.ShapeDtypeStruct(shape, dtype) for...]
    ppermute x0 -> x6, waiting for transfers between devices: none -> 24.5 us  [the longest x3 22 us: body(): lax.ppermute(values, 'y', [(place, (place + step) % 4) for place in range...]
    convert_element_type x11 -> x0, local copies, waits for them, and re-layouts: 15.8 us -> none  [the longest x2 8.52 us: attention_backward(): grad_rows = jnp.stack([grad_query, grad_key, grad_value], axis=2).astype(...]
    all_to_all x3 -> x2, waiting for transfers between devices: 39.4 us -> 23.7 us  [exchange(): return lax.all_to_all(values, axes, split_axis=0, concat_axis=0, tiled=True)]
  transfers between devices with their start and end apart: 11 -> 8, of which waited for: 9 -> 4; matrix products, arithmetic and copies ran while one was open for 14% -> 0% of each run, Pallas kernels for 0% -> 9%
where the time goes in v1:
time: 136 us; the launch traced here: 135 us
  waiting for transfers between devices  48.2 us (35%)
  starting transfers between devices  30.3 us (22%)
  Pallas kernels  26.3 us (19%)
  blocking collectives  25.3 us (19%)
  local copies, waits for them, and re-layouts  3.9 us (3%)
    pallas_call x10, Pallas kernels, run(): pl.pallas_call(kernel, out_shape=[jax.ShapeDtypeStruct(shape, dtype) for...  26.3 us
    all_to_all x1, blocking collectives, exchange(): return lax.all_to_all(values, axes, split_axis=0, concat_axis=0, tiled=True)  25.3 us
    all_to_all x2, waiting for transfers between devices, exchange(): return lax.all_to_all(values, axes, split_axis=0, concat_axis=0, tiled=True)  23.7 us
    ppermute x3, waiting for transfers between devices, body(): lax.ppermute(values, 'y', [(place, (place + step) % 4) for place in range...  22 us
    all_to_all x2, starting transfers between devices, exchange(): return lax.all_to_all(values, axes, split_axis=0, concat_axis=0, tiled=True)  21.4 us
    ppermute x3, starting transfers between devices, body(): lax.ppermute(values, 'y', [(place, (place + step) % 4) for place in range...  6.11 us
    unnamed x24, local copies, waits for them, and re-layouts  3.9 us
    ppermute x3, starting transfers between devices, swap(): return lax.ppermute(values, axis, [(0, 1), (1, 0)])  2.79 us
  transfers between devices with their start and end apart: 8, of which 4 were waited for; matrix products, arithmetic and copies ran while one was open for 0% of the time, Pallas kernels for 9%

profile of v1, /device:TPU:2, one launch (start us, length us, event | category | flops | bytes accessed | tf_op | source)
XLA Modules:
  0.0 134.8 jit_solution(17819190632450066200)
XLA Ops:
  0.6 1.0 copy-done.2
  1.6 1.0 copy-done.3
  2.6 1.2 shard_map.135
  3.8 13.9 %all-to-all-start = ((bf16[128,8,384]{2,1,0:T(8,128)(2,1)}), bf16[128,8,384]{2,1,0:T(8,128)(2,1)S(1)}, u32[]{:S(2)}, u32[]{:S(2)}) async-start(bf16[128,8,384]{2,1,0:T(8,128)(2,1)} %shard_map.135), calls=%async_computation | async-start | bytes 1572864 | tf_op jit(solution)/shard_map/all_to_all | solution.py:414
  17.8 23.7 %all-to-all-done = bf16[128,8,384]{2,1,0:T(8,128)(2,1)S(1)} async-done(((bf16[128,8,384]{2,1,0:T(8,128)(2,1)}), bf16[128,8,384]{2,1,0:T(8,128)(2,1)S(1)}, u32[]{:S(2)}, u32[]{:S(2)}) %all-to-all-start) | async-done | bytes 786464 | tf_op jit(solution)/shard_map/all_to_all | solution.py:414
  41.5 4.2 %shard_map.136 = (bf16[512,384]{1,0:T(8,128)(2,1)S(1)}, bf16[512,1152]{1,0:T(8,128)(2,1)S(1)}, bf16[512,384]{1,0:T(8,128)(2,1)S(1)}, bf16[512,384]{1,0:T(8,128)(2,1)S(1)}, bf16[512,384]{1,0:T(8,128)(2,1)S(1)}) custom-call(bf16[1024,384]{1,0:T(8,128)(2,1)S(1)} %bitcast.6, f32[1,384]{1,0:T(1,128)S(1)} %reshape.24.gain_one, bf16[1152,384]{1,0:T(8,128)(2,1)S(1)} %copy-done.6, ...), custom_call_target="tpu_custom_call" | custom-call | flops 1000000000 | bytes 4000000 | tf_op jit(solution)/shard_map/pallas_call | solution.py:400
  45.8 8.4 %shard_map.137 = (bf16[512,384]{1,0:T(8,128)(2,1)S(1)}, bf16[8,192,384]{2,1,0:T(8,128)(2,1)S(1)}, bf16[8,192,384]{2,1,0:T(8,128)(2,1)}, f32[1,384]{1,0:T(1,128)S(1)}) custom-call(bf16[512,384]{1,0:T(8,128)(2,1)S(1)} %get-tuple-element.34.grad_out, bf16[512,384]{1,0:T(8,128)(2,1)S(1)} %get-tuple-element.35.resid, f32[1,384]{1,0:T(1,128)S(1)} %reshape.25.gain_two, ...), custom_call_target="tpu_custom_call" | custom-call | flops 3000000000 | bytes 6000000 | tf_op jit(solution)/shard_map/pallas_call | solution.py:400
  54.2 6.2 %shard_map.138 = (bf16[128,4,384]{2,1,0:T(4,128)(2,1)}, bf16[512,1152]{1,0:T(8,128)(2,1)S(1)}, bf16[512,384]{1,0:T(8,128)(2,1)S(1)}, f32[1,384]{1,0:T(1,128)S(1)}) custom-call(bf16[512,384]{1,0:T(8,128)(2,1)S(1)} %get-tuple-element.38.x_ref, bf16[512,1152]{1,0:T(8,128)(2,1)S(1)} %get-tuple-element.39.qkv_ref, ...), custom_call_target="tpu_custom_call" | custom-call | flops 6000000000 | bytes 20000000 | tf_op jit(solution)/shard_map/pallas_call | solution.py:400
  60.4 2.5 %shard_map.139 = (bf16[8,112,384]{2,1,0:T(8,128)(2,1)S(1)}, bf16[8,112,384]{2,1,0:T(8,128)(2,1)}) custom-call(bf16[512,1152]{1,0:T(8,128)(2,1)S(1)} %get-tuple-element.41.rows_grad, bf16[512,384]{1,0:T(8,128)(2,1)S(1)} %get-tuple-element.42.normed, bf16[512,384]{1,0:T(8,128)(2,1)S(1)} %get-tuple-element.40.resid_grad_ref.resid_grad, ...), custom_call_target="tpu_custom_call" | custom-call | flops 1000000000 | bytes 5000000 | tf_op jit(solution)/shard_map/pallas_call | solution.py:400
  62.9 0.8 copy-done
  63.7 0.5 collective-permute-start.1
  64.2 7.5 %all-to-all-start.1 = ((bf16[128,4,384]{2,1,0:T(4,128)(2,1)}), bf16[128,4,384]{2,1,0:T(4,128)(2,1)S(1)}, u32[]{:S(2)}, u32[]{:S(2)}) async-start(bf16[128,4,384]{2,1,0:T(4,128)(2,1)} %get-tuple-element.52), calls=%async_computation.1 | async-start | bytes 786432 | tf_op jit(solution)/shard_map/all_to_all | solution.py:414
  71.8 1.1 copy-done.1
  72.9 1.5 %shard_map.140 = (bf16[2,304,384]{2,1,0:T(8,128)(2,1)S(1)}, bf16[2,304,384]{2,1,0:T(8,128)(2,1)S(1)}, bf16[2,304,384]{2,1,0:T(8,128)(2,1)S(1)}, bf16[2,304,384]{2,1,0:T(8,128)(2,1)S(1)}) custom-call(bf16[8,192,384]{2,1,0:T(8,128)(2,1)S(1)} %get-tuple-element.36.early_keep, bf16[8,192,384]{2,1,0:T(8,128)(2,1)S(1)} %collective-permute-done.early_recv, ...), custom_call_target="tpu_custom_call" | custom-call | bytes 10000000 | tf_op jit(solution)/shard_map/pallas_call | solution.py:400
  74.4 1.8 %collective-permute-start.2 = (bf16[2,304,384]{2,1,0:T(8,128)(2,1)S(1)}, bf16[2,304,384]{2,1,0:T(8,128)(2,1)S(1)}, u32[]{:S(2)}, u32[]{:S(2)}) collective-permute-start(bf16[2,304,384]{2,1,0:T(8,128)(2,1)S(1)} %get-tuple-element.49), channel_id=1, source_target_pairs={{0,64},{64,128},{128,192},{192,0},{1,65},{65,129},{129,193},{193,1... | collective-permute-start | bytes 1400840 | tf_op jit(solution)/shard_map/ppermute | solution.py:469
  76.2 3.1 %collective-permute-start.3 = (bf16[2,304,384]{2,1,0:T(8,128)(2,1)S(1)}, bf16[2,304,384]{2,1,0:T(8,128)(2,1)S(1)}, u32[]{:S(2)}, u32[]{:S(2)}) collective-permute-start(bf16[2,304,384]{2,1,0:T(8,128)(2,1)S(1)} %get-tuple-element.50), channel_id=1, source_target_pairs={{0,128},{64,192},{128,0},{192,64},{1,129},{65,193},{129,1},{193,65... | collective-permute-start | bytes 1400840 | tf_op jit(solution)/shard_map/ppermute | solution.py:469
  79.3 1.2 collective-permute-start.4
  80.5 11.4 %collective-permute-done.2.one = bf16[2,304,384]{2,1,0:T(8,128)(2,1)S(1)} collective-permute-done((bf16[2,304,384]{2,1,0:T(8,128)(2,1)S(1)}, bf16[2,304,384]{2,1,0:T(8,128)(2,1)S(1)}, u32[]{:S(2)}, u32[]{:S(2)}) %collective-permute-start.2) | collective-permute-done | bytes 466976 | tf_op jit(solution)/shard_map/ppermute | solution.py:469
  91.9 10.6 %collective-permute-done.3.two = bf16[2,304,384]{2,1,0:T(8,128)(2,1)S(1)} collective-permute-done((bf16[2,304,384]{2,1,0:T(8,128)(2,1)S(1)}, bf16[2,304,384]{2,1,0:T(8,128)(2,1)S(1)}, u32[]{:S(2)}, u32[]{:S(2)}) %collective-permute-start.3) | collective-permute-done | bytes 466976 | tf_op jit(solution)/shard_map/ppermute | solution.py:469
  103.1 25.3 %all_to_all.15.recv_ref = bf16[16,152,128]{2,1,0:T(8,128)(2,1)S(1)} all-to-all(bf16[16,152,128]{2,1,0:T(8,128)(2,1)S(1)} %shard_map.141), channel_id=1, replica_groups=mesh['y'=4,'xl'=2,'core'=2,'wa'=8,'dp'=2] {'xl','wa'}, dimensions={0} | all-to-all | bytes 1245184 | tf_op jit(solution)/shard_map/all_to_all | solution.py:414
  128.5 2.2 %collective-permute-start.5 = (bf16[152,128]{1,0:T(8,128)(2,1)S(1)}, bf16[152,128]{1,0:T(8,128)(2,1)S(1)}, u32[]{:S(2)}, u32[]{:S(2)}) collective-permute-start(bf16[152,128]{1,0:T(8,128)(2,1)S(1)} %shard_map.143.own_ref), channel_id=1, source_target_pairs={{0,1},{1,0},{2,3},{3,2},{4,5},{5,4},{6,7},{7,6},{8,9},{9,8},{10,11... | collective-permute-start | bytes 116744 | tf_op jit(solution)/shard_map/ppermute | solution.py:418
  130.8 0.8 shard_map.142
  131.6 2.5 %collective-permute-done.5.other_ref = bf16[152,128]{1,0:T(8,128)(2,1)S(1)} collective-permute-done((bf16[152,128]{1,0:T(8,128)(2,1)S(1)}, bf16[152,128]{1,0:T(8,128)(2,1)S(1)}, u32[]{:S(2)}, u32[]{:S(2)}) %collective-permute-start.5) | collective-permute-done | bytes 38944 | tf_op jit(solution)/shard_map/ppermute | solution.py:418
  134.1 0.8 shard_map.144
  (29 shorter events, 0.7 us)
Async XLA Ops:
  0.6 1.0 copy-start.2
  1.6 1.0 copy-start.3
  2.6 15.2 %copy-start.10 = (f32[384]{0:T(512)S(1)}, f32[384]{0:T(512)}, u32[]{:S(2)}) copy-start(f32[384]{0:T(512)} %param.10) | copy-start | bytes 4612
  2.6 15.2 %copy-start.11 = (f32[384]{0:T(512)S(1)}, f32[384]{0:T(512)}, u32[]{:S(2)}) copy-start(f32[384]{0:T(512)} %param.11) | copy-start | bytes 4612
  2.6 38.9 %copy-start.6 = (bf16[1152,384]{1,0:T(8,128)(2,1)S(1)}, bf16[1152,384]{1,0:T(8,128)(2,1)}, u32[]{:S(2)}) copy-start(bf16[1152,384]{1,0:T(8,128)(2,1)} %w_qkv.3) | copy-start | bytes 2654212
  2.6 38.9 %copy-start.8 = (bf16[384,384]{1,0:T(8,128)(2,1)S(1)}, bf16[384,384]{1,0:T(8,128)(2,1)}, u32[]{:S(2)}) copy-start(bf16[384,384]{1,0:T(8,128)(2,1)} %w_proj.3) | copy-start | bytes 884740
  3.8 37.7 %all-to-all-start = ((bf16[128,8,384]{2,1,0:T(8,128)(2,1)}), bf16[128,8,384]{2,1,0:T(8,128)(2,1)S(1)}, u32[]{:S(2)}, u32[]{:S(2)}) async-start(bf16[128,8,384]{2,1,0:T(8,128)(2,1)} %shard_map.135), calls=%async_computation | async-start | bytes 1572864 | tf_op jit(solution)/shard_map/all_to_all | solution.py:414
  41.5 4.3 %copy-start.4 = (bf16[1536,384]{1,0:T(8,128)(2,1)S(1)}, bf16[1536,384]{1,0:T(8,128)(2,1)}, u32[]{:S(2)}) copy-start(bf16[1536,384]{1,0:T(8,128)(2,1)} %w_up.1) | copy-start | bytes 3538948
  41.5 4.3 %copy-start.5 = (bf16[384,1536]{1,0:T(8,128)(2,1)S(1)}, bf16[384,1536]{1,0:T(8,128)(2,1)}, u32[]{:S(2)}) copy-start(bf16[384,1536]{1,0:T(8,128)(2,1)} %w_down.1) | copy-start | bytes 3538948
  45.7 8.5 %copy-start.7 = (bf16[1152,384]{1,0:T(8,128)(2,1)S(1)}, bf16[1152,384]{1,0:T(8,128)(2,1)}, u32[]{:S(2)}) copy-start(bf16[1152,384]{1,0:T(8,128)(2,1)} %w_qkv.3) | copy-start | bytes 2654212
  45.7 8.4 %copy-start.9 = (bf16[384,384]{1,0:T(8,128)(2,1)S(1)}, bf16[384,384]{1,0:T(8,128)(2,1)}, u32[]{:S(2)}) copy-start(bf16[384,384]{1,0:T(8,128)(2,1)} %w_proj.3) | copy-start | bytes 884740
  54.2 17.6 %collective-permute-start = (bf16[8,192,384]{2,1,0:T(8,128)(2,1)}, bf16[8,192,384]{2,1,0:T(8,128)(2,1)S(1)}, u32[]{:S(2)}, u32[]{:S(2)}) collective-permute-start(bf16[8,192,384]{2,1,0:T(8,128)(2,1)} %get-tuple-element.37), channel_id=1, source_target_pairs={{0,16},{16,0},{1,17},{17,1},{2,18},{18,2},{3,19},{19,3},{4,20},{20... | collective-permute-start | bytes 3538952 | tf_op jit(solution)/shard_map/ppermute | solution.py:418
  62.9 0.9 copy-start
  63.7 8.0 %collective-permute-start.1 = (bf16[8,112,384]{2,1,0:T(8,128)(2,1)}, bf16[8,112,384]{2,1,0:T(8,128)(2,1)}, u32[]{:S(2)}, u32[]{:S(2)}) collective-permute-start(bf16[8,112,384]{2,1,0:T(8,128)(2,1)} %get-tuple-element.47), channel_id=1, source_target_pairs={{0,16},{16,0},{1,17},{17,1},{2,18},{18,2},{3,19},{19,3},{4,20},{20... | collective-permute-start | bytes 2064392 | tf_op jit(solution)/shard_map/ppermute | solution.py:418
  64.2 38.8 %all-to-all-start.1 = ((bf16[128,4,384]{2,1,0:T(4,128)(2,1)}), bf16[128,4,384]{2,1,0:T(4,128)(2,1)S(1)}, u32[]{:S(2)}, u32[]{:S(2)}) async-start(bf16[128,4,384]{2,1,0:T(4,128)(2,1)} %get-tuple-element.52), calls=%async_computation.1 | async-start | bytes 786432 | tf_op jit(solution)/shard_map/all_to_all | solution.py:414
  71.8 1.1 copy-start.1
  74.4 17.5 %collective-permute-start.2 = (bf16[2,304,384]{2,1,0:T(8,128)(2,1)S(1)}, bf16[2,304,384]{2,1,0:T(8,128)(2,1)S(1)}, u32[]{:S(2)}, u32[]{:S(2)}) collective-permute-start(bf16[2,304,384]{2,1,0:T(8,128)(2,1)S(1)} %get-tuple-element.49), channel_id=1, source_target_pairs={{0,64},{64,128},{128,192},{192,0},{1,65},{65,129},{129,193},{193,1... | collective-permute-start | bytes 1400840 | tf_op jit(solution)/shard_map/ppermute | solution.py:469
  76.2 26.4 %collective-permute-start.3 = (bf16[2,304,384]{2,1,0:T(8,128)(2,1)S(1)}, bf16[2,304,384]{2,1,0:T(8,128)(2,1)S(1)}, u32[]{:S(2)}, u32[]{:S(2)}) collective-permute-start(bf16[2,304,384]{2,1,0:T(8,128)(2,1)S(1)} %get-tuple-element.50), channel_id=1, source_target_pairs={{0,128},{64,192},{128,0},{192,64},{1,129},{65,193},{129,1},{193,65... | collective-permute-start | bytes 1400840 | tf_op jit(solution)/shard_map/ppermute | solution.py:469
  79.3 23.2 %collective-permute-start.4 = (bf16[2,304,384]{2,1,0:T(8,128)(2,1)S(1)}, bf16[2,304,384]{2,1,0:T(8,128)(2,1)S(1)}, u32[]{:S(2)}, u32[]{:S(2)}) collective-permute-start(bf16[2,304,384]{2,1,0:T(8,128)(2,1)S(1)} %get-tuple-element.51), channel_id=1, source_target_pairs={{0,192},{64,0},{128,64},{192,128},{1,193},{65,1},{129,65},{193,129... | collective-permute-start | bytes 1400840 | tf_op jit(solution)/shard_map/ppermute | solution.py:469
  128.5 5.6 %collective-permute-start.5 = (bf16[152,128]{1,0:T(8,128)(2,1)S(1)}, bf16[152,128]{1,0:T(8,128)(2,1)S(1)}, u32[]{:S(2)}, u32[]{:S(2)}) collective-permute-start(bf16[152,128]{1,0:T(8,128)(2,1)S(1)} %shard_map.143.own_ref), channel_id=1, source_target_pairs={{0,1},{1,0},{2,3},{3,2},{4,5},{5,4},{6,7},{7,6},{8,9},{9,8},{10,11... | collective-permute-start | bytes 116744 | tf_op jit(solution)/shard_map/ppermute | solution.py:418

commit v2 on v1

--- a/solution.py
+++ b/solution.py
@@ -100,11 +100,6 @@
 def load_every(ref, start, step):
     parts = [ref[part, pl.ds(start, SLOTS, stride=step), :] for part in range(3)]
     return jnp.concatenate(parts, axis=1).astype(BF16)
-
-
-def store_every(ref, start, step, values):
-    for part in range(3):
-        ref[part, pl.ds(start, SLOTS, stride=step), :] = values[:, part * 128 : (part + 1) * 128]
 
 
 def send_kernel(tokens_hbm, grad_hbm, out_ref, tokens_ref, grad_ref, sems):
@@ -131,7 +126,11 @@
 def return_kernel(recv_ref, out_ref):
     for line in range(LINES):
         for column in range(GRID):
-            out_ref[line, column] = recv_ref[owner_slot(line, column)]
+            unit = recv_ref[owner_slot(line, column), :16].astype(F32)
+            for part in range(3):
+                out_ref[line, column, :, part * 128 : (part + 1) * 128] = unit[
+                    part * 4 : part * 4 + 4
+                ].astype(BF16)
 
 
 def gelu_parts(hidden, grad):
@@ -285,46 +284,65 @@
         grad_x = resid_grad_ref[rows, :].astype(F32) + norm_back(
             grad, normal_hat, inv_std, gain_one[...]
         )
-        store_every(slots, crop, 4, dot(match, grad_x.astype(BF16)))
-    for slot in range(SLOTS):
+        returned = dot(match, grad_x.astype(BF16))
         for part in range(3):
-            out_ref[slot, :, part * 128 : (part + 1) * 128] = slots[
-                part, slot * 4 : slot * 4 + 4, :
-            ].astype(BF16)
+            slots[pl.ds(part * 4 + crop, SLOTS, stride=16), :] = returned[
+                :, part * 128 : (part + 1) * 128
+            ]
+    for spare in range(12, 16):
+        slots[pl.ds(spare, SLOTS, stride=16), :] = jnp.zeros((SLOTS, 128), F32)
+    out_ref[...] = slots[...].astype(BF16)
     gain_ref[...] = gain
 
 
 def weight_kernel(
-    rows_grad, normed, resid_grad, mixed, first, second, keep_ref, send_ref,
-    qkv_total, proj_total, piece_rows,
+    rows_grad, normed, resid_grad, mixed, first, second, keep_ref, send_ref, total, piece_rows,
 ):
     for part in range(3):
-        cols = pl.ds(part * 384, 384)
-        qkv_total[cols, :] = dot_tn(rows_grad[:, cols], normed[...])
-    proj_total[...] = dot_tn(resid_grad[...], mixed[...])
-    piece_rows[96:, :] = jnp.zeros((16, 384), F32)
-    piece_rows[96:97, :] = first[...]
-    piece_rows[97:98, :] = second[...]
+        grad = dot_tn(rows_grad[:, pl.ds(part * 384, 384)], normed[...])
+        start, stop = part * 384, part * 384 + 384
+        for owner in range(16):
+            low, high = max(start, owner * 72), min(stop, owner * 72 + 72)
+            if low < high:
+                place = owner * 96 + low - owner * 72
+                total[place : place + high - low, :] = grad[low - start : high - start]
+    grad = dot_tn(resid_grad[...], mixed[...])
+    for owner in range(16):
+        total[owner * 96 + 72 : owner * 96 + 96, :] = grad[owner * 24 : owner * 24 + 24]
     for ref, side in piece_sides(keep_ref, send_ref):
-        for piece in range(8):
-            owner = 2 * piece + side
-            piece_rows[:72, :] = qkv_total[pl.ds(pl.multiple_of(owner * 72, 8), 72), :]
-            piece_rows[72:96, :] = proj_total[pl.ds(pl.multiple_of(owner * 24, 8), 24), :]
-            ref[piece] = piece_rows[...].astype(BF16)
-
-
-def core_kernel(early_keep, early_recv, late_keep, late_recv, *outs):
-    row = lax.axis_index("y")
-    for step in range(4):
-        place = (row + step) & 3
-        for col in range(2):
-            piece = place * 2 + col
-            outs[step][col, :192] = (
-                early_keep[piece].astype(F32) + early_recv[piece].astype(F32)
-            ).astype(BF16)
-            outs[step][col, 192:] = (
-                late_keep[piece].astype(F32) + late_recv[piece].astype(F32)
-            ).astype(BF16)
+        piece_rows[...] = jnp.zeros_like(piece_rows)
+        for owner in range(16):
+            for half in range(2):
+                start = pl.multiple_of(owner * 96 + side * 48 + half * 24, 8)
+                piece_rows[half, owner * 24 : owner * 24 + 24, :] = total[pl.ds(start, 24), :]
+        piece_rows[0, 384:385, :] = jnp.where(side == 0, first[...], second[...])
+        ref[...] = piece_rows[...].astype(BF16)
+
+
+def column_spread(half):
+    source, target = iota((384, 1024), 0), iota((384, 1024), 1)
+    lane = (target & 127) - 64 * half
+    hit = jnp.logical_and(source == (target >> 7) * 48 + lane, lane >= 0)
+    return one_hot(jnp.logical_and(hit, lane < 48))
+
+
+def out_kernel(keep_ref, recv_ref, slots_ref, out_ref):
+    total = keep_ref[...].astype(F32) + recv_ref[...].astype(F32)
+    packed = dot(total[0, :384].astype(BF16), column_spread(0))
+    packed = packed + dot(total[1, :384].astype(BF16), column_spread(1))
+    gain = jnp.concatenate(
+        [jnp.zeros((12, 128), F32)]
+        + [total[0, 384:385, part * 128 : (part + 1) * 128] for part in range(3)]
+        + [jnp.zeros((1, 128), F32)],
+        axis=0,
+    )
+    for row in range(16):
+        for col in range(8):
+            owner = row * 8 + col
+            block = packed[row * 24 : row * 24 + 24, col * 128 : (col + 1) * 128]
+            token = slots_ref[owner * 16 : owner * 16 + 16, :].astype(F32) + gain
+            out_ref[owner, :16] = token.astype(BF16)
+            out_ref[owner, 16:] = block.astype(BF16)
 
 
 def pack_columns(rows, col):
@@ -333,37 +351,73 @@
     return jnp.where(iota((48, 128), 1) < 64, low, high)
 
 
-def pack_kernel(own, one, two, three, out_ref, gains):
+def core_kernel(keep_ref, recv_ref, own, near, back, far_low, far_high):
     row = lax.axis_index("y")
-    for step, ref in enumerate((own, one, two, three)):
-        gains[(row - step) & 3] = ref[0, 288:].astype(F32)
-    gain = (gains[0] + gains[1]) + (gains[2] + gains[3])
-    gain_rows = [
-        gain[which : which + 1, part * 128 : (part + 1) * 128]
-        for which in range(2)
-        for part in range(3)
-    ]
-    gain_rows.append(jnp.zeros((2, 128), F32))
-    for side in range(2):
-        total = own[side, :288].astype(F32) + one[side, :288].astype(F32)
-        total = total + (two[side, :288].astype(F32) + three[side, :288].astype(F32))
-        for col in range(8):
-            start = 96 + 24 * (col // 2)
-            block = total[start : start + 24]
-            if col % 2:
-                block = pltpu.roll(block, 192, 1)
-            out_ref[side * 8 + col] = jnp.concatenate(
-                [pack_columns(total[:96], col), block[:, :128], block[:, 128:256]]
-                + [pack_columns(total[192:], col)] + gain_rows,
-                axis=0,
-            ).astype(BF16)
-
-
-def block_sum(recv_ref, out_ref):
-    total = recv_ref[0].astype(F32)
-    for place in range(1, 16):
-        total = total + recv_ref[place].astype(F32)
-    out_ref[...] = total.astype(BF16)
+
+    def total(step, col):
+        piece = ((row + step) & 3) * 2 + col
+        return (keep_ref[piece].astype(F32) + recv_ref[piece].astype(F32)).astype(BF16)
+
+    for ref, step in ((own, 0), (near, 1), (back, 3)):
+        for col in range(2):
+            ref[col] = total(step, col)
+    far_low[...] = total(2, 0)
+    far_high[...] = total(2, 1)
+
+
+def ring_kernel(near, back, far_low, far_high, out_near, out_back):
+    out_near[0] = (near[0].astype(F32) + far_low[...].astype(F32)).astype(BF16)
+    out_near[1] = near[1]
+    out_back[0] = back[0]
+    out_back[1] = (back[1].astype(F32) + far_high[...].astype(F32)).astype(BF16)
+
+
+def row_kernel(own, near, back, keep_ref, send_ref):
+    col = lax.axis_index("xl")
+    for ref, side in ((keep_ref, col), (send_ref, 1 - col)):
+        total = own[side].astype(F32) + near[side].astype(F32) + back[side].astype(F32)
+        ref[...] = total.astype(BF16)
+
+
+def column_split(packed, keep_ref, send_ref, bit, count):
+    own = (lax.axis_index("wa") >> bit) & 1
+    for ref, side in ((keep_ref, own), (send_ref, 1 - own)):
+        for piece in range(count):
+            ref[piece] = packed(2 * piece + side).astype(BF16)
+
+
+def early_pack(keep_ref, recv_ref, out_keep, out_send, packed):
+    total = keep_ref[...].astype(F32) + recv_ref[...].astype(F32)
+    for col in range(8):
+        start = 96 + 24 * (col // 2)
+        block = total[start : start + 24]
+        if col % 2:
+            block = pltpu.roll(block, 192, 1)
+        packed[col, :48] = pack_columns(total[:96], col)
+        packed[col, 48:72] = block[:, :128]
+        packed[col, 72:] = block[:, 128:256]
+    column_split(lambda piece: packed[piece], out_keep, out_send, 0, 4)
+
+
+def early_halve(keep_ref, recv_ref, out_keep, out_send, bit, count):
+    column_split(
+        lambda piece: keep_ref[piece].astype(F32) + recv_ref[piece].astype(F32),
+        out_keep, out_send, bit, count,
+    )
+
+
+def block_sum(early_keep, early_recv, recv_ref, out_ref):
+    early = early_keep[0].astype(F32) + early_recv[0].astype(F32)
+    out_ref[:96, :] = early.astype(BF16)
+    gains = []
+    for core in range(2):
+        total = jnp.zeros((40, 128), F32)
+        for plane in range(8):
+            for col in range(8):
+                total = total + recv_ref[(plane * 2 + core) * 8 + col].astype(F32)
+        out_ref[96 + 24 * core : 120 + 24 * core, :] = total[16:].astype(BF16)
+        gains.append(total[8:16])
+    out_ref[144:, :] = jnp.concatenate(gains, axis=0).astype(BF16)
 
 
 def unpack_columns(packed):
@@ -380,19 +434,21 @@
     qkv_ref, proj_ref, up_ref, down_ref, first_ref, second_ref, factor,
 ):
     total = (own_ref[...].astype(F32) + other_ref[...].astype(F32)) * factor
-    early, late = total[:96], total[96:]
-    up_ref[...] = unpack_columns(early[:48])[:, :96]
-    down_ref[:, :128] = early[48:72]
-    down_ref[:, 128:] = early[72:96, :64]
-    qkv_ref[...] = unpack_columns(late[:48])[:, :72]
-    proj_ref[...] = pltpu.roll(late[:48], 64, 1)[24:48, :48]
+    up_ref[...] = unpack_columns(total[:48])[:, :96]
+    down_ref[:, :128] = total[48:72]
+    down_ref[:, 128:] = total[72:96, :64]
+    late = total[96:144]
+    high = pltpu.roll(late, 64, 1)
+    proj_ref[...] = high[24:, :48]
+    wide = jnp.concatenate([late[:24], high[:24], late[24:], jnp.zeros((56, 128), F32)], axis=0)
+    qkv_ref[...] = wide.T[:48, :72]
     for part in range(3):
         lane = pl.ds(part * 128, 128)
-        first_ref[lane] = late[48 + part]
-        second_ref[lane] = late[51 + part]
-
-
-def call(kernel, outs, scratch=(), flops=0, nbytes=0, space=pltpu.VMEM):
+        first_ref[lane] = total[148 + part]
+        second_ref[lane] = total[156 + part]
+
+
+def call(kernel, outs, scratch=(), flops=0, nbytes=0, space=pltpu.VMEM, limit=24):
     vmem = pl.BlockSpec(memory_space=pltpu.VMEM)
     scratch = [pltpu.VMEM(*item) if isinstance(item, tuple) else item for item in scratch]
 
@@ -403,7 +459,7 @@
             in_specs=[pl.BlockSpec(memory_space=space)] * len(args),
             out_specs=[vmem] * len(outs),
             scratch_shapes=scratch,
-            compiler_params=pltpu.CompilerParams(vmem_limit_bytes=24 << 20),
+            compiler_params=pltpu.CompilerParams(vmem_limit_bytes=limit << 20),
             cost_estimate=pl.CostEstimate(flops=flops, bytes_accessed=nbytes, transcendentals=0),
         )(*args)
 
@@ -414,8 +470,38 @@
     return lax.all_to_all(values, axes, split_axis=0, concat_axis=0, tiled=True)
 
 
-def swap(values, axis):
-    return lax.ppermute(values, axis, [(0, 1), (1, 0)])
+def swap(values, axis, size, bit):
+    return lax.ppermute(values, axis, [(place, place ^ bit) for place in range(size)])
+
+
+def shift(values, step):
+    return lax.ppermute(values, "y", [(place, (place + step) % 4) for place in range(4)])
+
+
+def early_ring(keep, arrived):
+    part, half = ((2, 192, 384), BF16), ((192, 384), BF16)
+    own, near, back, low, high = call(
+        core_kernel, [part, part, part, half, half], nbytes=4 * 10**6
+    )(keep, arrived)
+    near, back = call(ring_kernel, [part, part], nbytes=3 * 10**6)(
+        near, back, shift(low, 1), shift(high, 3)
+    )
+    return own, near, back
+
+
+def early_sums(own, near, back):
+    piece = ((192, 384), BF16)
+    keep, send = call(row_kernel, [piece] * 2, nbytes=2 * 10**6)(own, shift(near, 1), shift(back, 3))
+    keep, send = call(
+        early_pack, [((4, 96, 128), BF16)] * 2, [((8, 96, 128), F32)], nbytes=10**6
+    )(keep, swap(send, "xl", 2, 1))
+    for bit, count in ((1, 2), (2, 1)):
+        keep, send = call(
+            functools.partial(early_halve, bit=bit, count=count),
+            [((count, 96, 128), BF16)] * 2,
+            nbytes=3 * 10**5,
+        )(keep, swap(send, "wa", 8, bit))
+    return keep, swap(send, "wa", 8, 4)
 
 
 def body(tokens, grad_out, gain_first, gain_second, w_qkv, w_proj, w_up, w_down):
@@ -427,7 +513,8 @@
         [((SLOTS, 8, 384), BF16)],
         [tile, tile, pltpu.SemaphoreType.DMA((2,))],
         nbytes=2 * 10**6,
-        space=pltpu.HBM,
+        space=pl.ANY,
+        limit=60,
     )(
         tokens.transpose(1, 2, 0, 3), grad_out.transpose(1, 2, 0, 3)
     )
@@ -448,33 +535,30 @@
         ],
         flops=3 * 10**9, nbytes=6 * 10**6,
     )(grad_rows, resid, gain_two, w_up, w_down)
+    early_arrived = swap(early_send, "core", 2, 1)
     slots, rows_grad, normed, gain_sum_one = call(
         attention_kernel,
-        [((SLOTS, 4, 384), BF16), ((512, 1152), BF16), rows, ((1, 384), F32)],
-        [rows, ((3, 512, 128), F32)],
+        [((SLOTS * 16, 128), BF16), ((512, 1152), BF16), rows, ((1, 384), F32)],
+        [rows, ((SLOTS * 16, 128), F32)],
         flops=6 * 10**9, nbytes=20 * 10**6,
     )(x, qkv, resid_grad, gain_one, w_qkv, w_proj)
-    returned = exchange(slots, HA + ("wa",))
+    early_keep, rows_grad = lax.optimization_barrier((early_keep, rows_grad))
+    own, near, back = early_ring(early_keep, early_arrived)
+    late = ((2, 400, 384), BF16)
     late_keep, late_send = call(
         weight_kernel,
-        [((8, 112, 384), BF16), ((8, 112, 384), BF16)],
-        [((1152, 384), F32), ((384, 384), F32), ((112, 384), F32)],
+        [late, late],
+        [((1536, 384), F32), ((2, 400, 384), F32)],
         flops=10**9, nbytes=5 * 10**6,
     )(rows_grad, normed, resid_grad, mixed, gain_sum_one, gain_sum_two)
-    piece = ((2, 304, 384), BF16)
-    own, *others = call(core_kernel, [piece] * 4, nbytes=10**7)(
-        early_keep, swap(early_send, "core"), late_keep, swap(late_send, "core")
-    )
-    arrived = [
-        lax.ppermute(values, "y", [(place, (place + step) % 4) for place in range(4)])
-        for step, values in zip((1, 2, 3), others)
-    ]
-    (blocks,) = call(
-        pack_kernel, [((16, 152, 128), BF16)], [((4, 16, 384), F32)], nbytes=3 * 10**6
-    )(own, *arrived)
-    blocks, returned = lax.optimization_barrier((blocks, returned))
-    (total,) = call(block_sum, [((152, 128), BF16)], nbytes=10**6)(exchange(blocks, ("xl", "wa")))
-    other = swap(total, "dp")
+    near, back, slots = lax.optimization_barrier((near, back, slots))
+    (sent,) = call(out_kernel, [((SLOTS, 40, 128), BF16)], flops=10**9, nbytes=5 * 10**6)(
+        late_keep, swap(late_send, "core", 2, 1), slots
+    )
+    returned = exchange(sent, HA + ("wa",))
+    early = early_sums(own, near, back)
+    (total,) = call(block_sum, [((160, 128), BF16)], nbytes=10**6)(*early, returned)
+    other = lax.ppermute(total, "dp", [(0, 1), (1, 0)])
     grad_qkv, grad_proj, grad_up, grad_down, first, second = call(
         functools.partial(final_weights, factor=factor),
         [

time: 136 us -> 131 us (0.963)
  blocking collectives: 25.3 us -> 0 us
  starting transfers between devices: 30.3 us -> 44.1 us
  waiting for transfers between devices: 48.2 us -> 59.7 us
  local copies, waits for them, and re-layouts: 3.9 us -> 0.03 us
    all_to_all x1 -> x0, blocking collectives: 25.3 us -> none  [exchange(): return lax.all_to_all(values, axes, split_axis=0, concat_axis=0, tiled=True)]
    ppermute x6 -> x11, starting transfers between devices: 8.9 us -> 21.5 us  [the longest x6 12.5 us: swap(): lax.ppermute(values, axis, [(place, place ^ bit) for place in range(size)])]
    ppermute x6 -> x11, waiting for transfers between devices: 24.5 us -> 36 us  [the longest x4 17.2 us: shift(): lax.ppermute(values, 'y', [(place, (place + step) % 4) for place in range...]
    unnamed x24 -> x12, local copies, waits for them, and re-layouts: 3.9 us -> 0.02 us
    pallas_call x10 -> x15, Pallas kernels: 26.3 us -> 25.6 us  [run(): pl.pallas_call(kernel, out_shape=[jax.ShapeDtypeStruct(shape, dtype) for...]
  transfers between devices with their start and end apart: 8 -> 13, of which waited for: 4 -> 8; matrix products, arithmetic and copies ran while one was open for 0% -> 0% of each run, Pallas kernels for 9% -> 7%
where the time goes in v2:
time: 131 us; the launch traced here: 130 us
  waiting for transfers between devices  59.7 us (46%)
  starting transfers between devices  44.1 us (34%)
  Pallas kernels  25.6 us (20%)
    pallas_call x15, Pallas kernels, run(): pl.pallas_call(kernel, out_shape=[jax.ShapeDtypeStruct(shape, dtype) for...  25.6 us
    all_to_all x2, waiting for transfers between devices, exchange(): return lax.all_to_all(values, axes, split_axis=0, concat_axis=0, tiled=True)  23.7 us
    all_to_all x2, starting transfers between devices, exchange(): return lax.all_to_all(values, axes, split_axis=0, concat_axis=0, tiled=True)  22.6 us
    ppermute x4, waiting for transfers between devices, shift(): lax.ppermute(values, 'y', [(place, (place + step) % 4) for place in range...  17.2 us
    ppermute x6, waiting for transfers between devices, swap(): lax.ppermute(values, axis, [(place, place ^ bit) for place in range(size)])  16.2 us
    ppermute x6, starting transfers between devices, swap(): lax.ppermute(values, axis, [(place, place ^ bit) for place in range(size)])  12.5 us
    ppermute x4, starting transfers between devices, shift(): lax.ppermute(values, 'y', [(place, (place + step) % 4) for place in range...  6.79 us
  transfers between devices with their start and end apart: 13, of which 8 were waited for; matrix products, arithmetic and copies ran while one was open for 0% of the time, Pallas kernels for 7%

profile of v2, /device:TPU:2, one launch (start us, length us, event | category | flops | bytes accessed | tf_op | source)
XLA Modules:
  0.0 130.2 jit_solution(2833643100684132358)
XLA Ops:
  0.7 2.2 %shard_map.135 = bf16[128,8,384]{2,1,0:T(8,128)(2,1)} custom-call(bf16[14,7,4,384]{3,2,1,0:T(4,128)(2,1)} %bitcast.7, bf16[14,7,4,384]{3,2,1,0:T(4,128)(2,1)} %bitcast.8), custom_call_target="tpu_custom_call" | custom-call | bytes 2000000 | tf_op jit(solution)/shard_map/pallas_call | solution.py:456
  2.9 13.9 %all-to-all-start = ((bf16[128,8,384]{2,1,0:T(8,128)(2,1)}), bf16[128,8,384]{2,1,0:T(8,128)(2,1)S(1)}, u32[]{:S(2)}, u32[]{:S(2)}) async-start(bf16[128,8,384]{2,1,0:T(8,128)(2,1)} %shard_map.135), calls=%async_computation | async-start | bytes 1572864 | tf_op jit(solution)/shard_map/all_to_all | solution.py:470
  16.9 23.7 %all-to-all-done = bf16[128,8,384]{2,1,0:T(8,128)(2,1)S(1)} async-done(((bf16[128,8,384]{2,1,0:T(8,128)(2,1)}), bf16[128,8,384]{2,1,0:T(8,128)(2,1)S(1)}, u32[]{:S(2)}, u32[]{:S(2)}) %all-to-all-start) | async-done | bytes 786464 | tf_op jit(solution)/shard_map/all_to_all | solution.py:470
  40.6 4.2 %shard_map.136 = (bf16[512,384]{1,0:T(8,128)(2,1)S(1)}, bf16[512,1152]{1,0:T(8,128)(2,1)S(1)}, bf16[512,384]{1,0:T(8,128)(2,1)S(1)}, bf16[512,384]{1,0:T(8,128)(2,1)S(1)}, bf16[512,384]{1,0:T(8,128)(2,1)S(1)}) custom-call(bf16[1024,384]{1,0:T(8,128)(2,1)S(1)} %bitcast.6, f32[1,384]{1,0:T(1,128)S(1)} %reshape.24.gain_one, bf16[1152,384]{1,0:T(8,128)(2,1)S(1)} %copy-done.2, ...), custom_call_target="tpu_custom_call" | custom-call | flops 1000000000 | bytes 4000000 | tf_op jit(solution)/shard_map/pallas_call | solution.py:456
  44.9 7.4 %shard_map.137 = (bf16[512,384]{1,0:T(8,128)(2,1)S(1)}, bf16[8,192,384]{2,1,0:T(8,128)(2,1)S(1)}, bf16[8,192,384]{2,1,0:T(8,128)(2,1)S(1)}, f32[1,384]{1,0:T(1,128)S(1)}) custom-call(bf16[512,384]{1,0:T(8,128)(2,1)S(1)} %get-tuple-element.48.grad_out, bf16[512,384]{1,0:T(8,128)(2,1)S(1)} %get-tuple-element.49.resid, f32[1,384]{1,0:T(1,128)S(1)} %reshape.25.gain_two, ...), custom_call_target="tpu_custom_call" | custom-call | flops 3000000000 | bytes 6000000 | tf_op jit(solution)/shard_map/pallas_call | solution.py:456
  52.3 5.7 %shard_map.138 = (bf16[2048,128]{1,0:T(8,128)(2,1)S(1)}, bf16[512,1152]{1,0:T(8,128)(2,1)S(1)}, bf16[512,384]{1,0:T(8,128)(2,1)S(1)}, f32[1,384]{1,0:T(1,128)S(1)}) custom-call(bf16[512,384]{1,0:T(8,128)(2,1)S(1)} %get-tuple-element.51.x_ref, bf16[512,1152]{1,0:T(8,128)(2,1)S(1)} %get-tuple-element.52.qkv_ref, ...), custom_call_target="tpu_custom_call" | custom-call | flops 6000000000 | bytes 20000000 | tf_op jit(solution)/shard_map/pallas_call | solution.py:456
  58.0 1.3 %shard_map.139 = (bf16[2,400,384]{2,1,0:T(8,128)(2,1)S(1)}, bf16[2,400,384]{2,1,0:T(8,128)(2,1)S(1)}) custom-call(bf16[512,1152]{1,0:T(8,128)(2,1)S(1)} %get-tuple-element.55.rows_grad, bf16[512,384]{1,0:T(8,128)(2,1)S(1)} %get-tuple-element.56.normed, bf16[512,384]{1,0:T(8,128)(2,1)S(1)} %get-tuple-element.53.resid_grad_ref.resid_grad, ...), custom_call_target="tpu_custom_call" | custom-call | flops 1000000000 | bytes 5000000 | tf_op jit(solution)/shard_map/pallas_call | solution.py:456
  61.2 2.5 %collective-permute-start.3 = (bf16[192,384]{1,0:T(8,128)(2,1)S(1)}, bf16[192,384]{1,0:T(8,128)(2,1)S(1)}, u32[]{:S(2)}, u32[]{:S(2)}) collective-permute-start(bf16[192,384]{1,0:T(8,128)(2,1)S(1)} %get-tuple-element.67), channel_id=1, source_target_pairs={{0,192},{64,0},{128,64},{192,128},{1,193},{65,1},{129,65},{193,129... | collective-permute-start | bytes 442376 | tf_op jit(solution)/shard_map/ppermute | solution.py:478
  63.7 3.8 %collective-permute-done.2.far_low = bf16[192,384]{1,0:T(8,128)(2,1)S(1)} collective-permute-done((bf16[192,384]{1,0:T(8,128)(2,1)S(1)}, bf16[192,384]{1,0:T(8,128)(2,1)S(1)}, u32[]{:S(2)}, u32[]{:S(2)}) %collective-permute-start.2) | collective-permute-done | bytes 147488 | tf_op jit(solution)/shard_map/ppermute | solution.py:478
  67.6 2.1 %shard_map.142 = bf16[128,40,128]{2,1,0:T(8,128)(2,1)} custom-call(bf16[2,400,384]{2,1,0:T(8,128)(2,1)S(1)} %get-tuple-element.60.keep_ref, bf16[2,400,384]{2,1,0:T(8,128)(2,1)S(1)} %collective-permute-done.recv_ref, bf16[2048,128]{1,0:T(8,128)(2,1)S(1)} %get-tuple-element.71.slots_ref), custom_call_target="tpu_custom_call" | custom-call | flops 1000000000 | bytes 5000000 | tf_op jit(solution)/shard_map/pallas_call | solution.py:456
  69.7 8.7 %all-to-all-start.1 = ((bf16[128,40,128]{2,1,0:T(8,128)(2,1)}), bf16[128,40,128]{2,1,0:T(8,128)(2,1)S(1)}, u32[]{:S(2)}, u32[]{:S(2)}) async-start(bf16[128,40,128]{2,1,0:T(8,128)(2,1)} %shard_map.142), calls=%async_computation.1 | async-start | bytes 2621440 | tf_op jit(solution)/shard_map/all_to_all | solution.py:470
  78.4 1.7 %collective-permute-start.4 = (bf16[2,192,384]{2,1,0:T(8,128)(2,1)S(1)}, bf16[2,192,384]{2,1,0:T(8,128)(2,1)S(1)}, u32[]{:S(2)}, u32[]{:S(2)}) collective-permute-start(bf16[2,192,384]{2,1,0:T(8,128)(2,1)S(1)} %get-tuple-element.73), channel_id=1, source_target_pairs={{0,64},{64,128},{128,192},{192,0},{1,65},{65,129},{129,193},{193,1... | collective-permute-start | bytes 884744 | tf_op jit(solution)/shard_map/ppermute | solution.py:478
  80.1 1.7 %collective-permute-start.5 = (bf16[2,192,384]{2,1,0:T(8,128)(2,1)S(1)}, bf16[2,192,384]{2,1,0:T(8,128)(2,1)S(1)}, u32[]{:S(2)}, u32[]{:S(2)}) collective-permute-start(bf16[2,192,384]{2,1,0:T(8,128)(2,1)S(1)} %get-tuple-element.74), channel_id=1, source_target_pairs={{0,192},{64,0},{128,64},{192,128},{1,193},{65,1},{129,65},{193,129... | collective-permute-start | bytes 884744 | tf_op jit(solution)/shard_map/ppermute | solution.py:478
  81.9 13.5 %collective-permute-done.4.near = bf16[2,192,384]{2,1,0:T(8,128)(2,1)S(1)} collective-permute-done((bf16[2,192,384]{2,1,0:T(8,128)(2,1)S(1)}, bf16[2,192,384]{2,1,0:T(8,128)(2,1)S(1)}, u32[]{:S(2)}, u32[]{:S(2)}) %collective-permute-start.4) | collective-permute-done | bytes 294944 | tf_op jit(solution)/shard_map/ppermute | solution.py:478
  96.0 7.7 %collective-permute-done.6.recv_ref = bf16[192,384]{1,0:T(8,128)(2,1)S(1)} collective-permute-done((bf16[192,384]{1,0:T(8,128)(2,1)S(1)}, bf16[192,384]{1,0:T(8,128)(2,1)S(1)}, u32[]{:S(2)}, u32[]{:S(2)}) %collective-permute-start.6) | collective-permute-done | bytes 147488 | tf_op jit(solution)/shard_map/ppermute | solution.py:474
  104.0 2.4 %collective-permute-start.7 = (bf16[4,96,128]{2,1,0:T(8,128)(2,1)S(1)}, bf16[4,96,128]{2,1,0:T(8,128)(2,1)S(1)}, u32[]{:S(2)}, u32[]{:S(2)}) collective-permute-start(bf16[4,96,128]{2,1,0:T(8,128)(2,1)S(1)} %get-tuple-element.78), channel_id=1, source_target_pairs={{0,2},{2,0},{4,6},{6,4},{8,10},{10,8},{12,14},{14,12},{1,3},{3,1},... | collective-permute-start | bytes 294920 | tf_op jit(solution)/shard_map/ppermute | solution.py:474
  106.4 4.0 %collective-permute-done.7.recv_ref = bf16[4,96,128]{2,1,0:T(8,128)(2,1)S(1)} collective-permute-done((bf16[4,96,128]{2,1,0:T(8,128)(2,1)S(1)}, bf16[4,96,128]{2,1,0:T(8,128)(2,1)S(1)}, u32[]{:S(2)}, u32[]{:S(2)}) %collective-permute-start.7) | collective-permute-done | bytes 98336 | tf_op jit(solution)/shard_map/ppermute | solution.py:474
  110.4 2.4 %collective-permute-start.8 = (bf16[2,96,128]{2,1,0:T(8,128)(2,1)S(1)}, bf16[2,96,128]{2,1,0:T(8,128)(2,1)S(1)}, u32[]{:S(2)}, u32[]{:S(2)}) collective-permute-start(bf16[2,96,128]{2,1,0:T(8,128)(2,1)S(1)} %get-tuple-element.80), channel_id=1, source_target_pairs={{0,4},{2,6},{4,0},{6,2},{8,12},{10,14},{12,8},{14,10},{1,5},{3,7},... | collective-permute-start | bytes 147464 | tf_op jit(solution)/shard_map/ppermute | solution.py:474
  112.8 2.7 %collective-permute-done.8.recv_ref = bf16[2,96,128]{2,1,0:T(8,128)(2,1)S(1)} collective-permute-done((bf16[2,96,128]{2,1,0:T(8,128)(2,1)S(1)}, bf16[2,96,128]{2,1,0:T(8,128)(2,1)S(1)}, u32[]{:S(2)}, u32[]{:S(2)}) %collective-permute-start.8) | collective-permute-done | bytes 49184 | tf_op jit(solution)/shard_map/ppermute | solution.py:474
  115.5 6.3 %collective-permute-start.9 = (bf16[1,96,128]{2,1,0:T(8,128)(2,1)S(1)}, bf16[1,96,128]{2,1,0:T(8,128)(2,1)S(1)}, u32[]{:S(2)}, u32[]{:S(2)}) collective-permute-start(bf16[1,96,128]{2,1,0:T(8,128)(2,1)S(1)} %get-tuple-element.82), channel_id=1, source_target_pairs={{0,8},{2,10},{4,12},{6,14},{8,0},{10,2},{12,4},{14,6},{1,9},{3,11}... | collective-permute-start | bytes 73736 | tf_op jit(solution)/shard_map/ppermute | solution.py:474
  121.8 1.8 %collective-permute-done.9.early_recv = bf16[1,96,128]{2,1,0:T(8,128)(2,1)S(1)} collective-permute-done((bf16[1,96,128]{2,1,0:T(8,128)(2,1)S(1)}, bf16[1,96,128]{2,1,0:T(8,128)(2,1)S(1)}, u32[]{:S(2)}, u32[]{:S(2)}) %collective-permute-start.9) | collective-permute-done | bytes 24608 | tf_op jit(solution)/shard_map/ppermute | solution.py:474
  123.8 2.2 %collective-permute-start.10 = (bf16[160,128]{1,0:T(8,128)(2,1)S(1)}, bf16[160,128]{1,0:T(8,128)(2,1)S(1)}, u32[]{:S(2)}, u32[]{:S(2)}) collective-permute-start(bf16[160,128]{1,0:T(8,128)(2,1)S(1)} %shard_map.148.own_ref), channel_id=1, source_target_pairs={{0,1},{1,0},{2,3},{3,2},{4,5},{5,4},{6,7},{7,6},{8,9},{9,8},{10,11... | collective-permute-start | bytes 122888 | tf_op jit(solution)/shard_map/ppermute | solution.py:561
  126.0 0.8 shard_map.143
  126.9 2.5 %collective-permute-done.10.other_ref = bf16[160,128]{1,0:T(8,128)(2,1)S(1)} collective-permute-done((bf16[160,128]{1,0:T(8,128)(2,1)S(1)}, bf16[160,128]{1,0:T(8,128)(2,1)S(1)}, u32[]{:S(2)}, u32[]{:S(2)}) %collective-permute-start.10) | collective-permute-done | bytes 40992 | tf_op jit(solution)/shard_map/ppermute | solution.py:561
  (31 shorter events, 4.1 us)
Async XLA Ops:
  0.6 16.2 %copy-start.4 = (f32[384]{0:T(512)S(1)}, f32[384]{0:T(512)}, u32[]{:S(2)}) copy-start(f32[384]{0:T(512)} %param.10) | copy-start | bytes 4612
  0.6 16.2 %copy-start.5 = (f32[384]{0:T(512)S(1)}, f32[384]{0:T(512)}, u32[]{:S(2)}) copy-start(f32[384]{0:T(512)} %param.11) | copy-start | bytes 4612
  0.7 39.9 %copy-start.2 = (bf16[1152,384]{1,0:T(8,128)(2,1)S(1)}, bf16[1152,384]{1,0:T(8,128)(2,1)}, u32[]{:S(2)}) copy-start(bf16[1152,384]{1,0:T(8,128)(2,1)} %w_qkv.3) | copy-start | bytes 2654212
  0.7 39.9 %copy-start.3 = (bf16[384,384]{1,0:T(8,128)(2,1)S(1)}, bf16[384,384]{1,0:T(8,128)(2,1)}, u32[]{:S(2)}) copy-start(bf16[384,384]{1,0:T(8,128)(2,1)} %w_proj.3) | copy-start | bytes 884740
  2.9 37.7 %all-to-all-start = ((bf16[128,8,384]{2,1,0:T(8,128)(2,1)}), bf16[128,8,384]{2,1,0:T(8,128)(2,1)S(1)}, u32[]{:S(2)}, u32[]{:S(2)}) async-start(bf16[128,8,384]{2,1,0:T(8,128)(2,1)} %shard_map.135), calls=%async_computation | async-start | bytes 1572864 | tf_op jit(solution)/shard_map/all_to_all | solution.py:470
  40.6 4.3 %copy-start = (bf16[1536,384]{1,0:T(8,128)(2,1)S(1)}, bf16[1536,384]{1,0:T(8,128)(2,1)}, u32[]{:S(2)}) copy-start(bf16[1536,384]{1,0:T(8,128)(2,1)} %w_up.1) | copy-start | bytes 3538948
  40.6 4.3 %copy-start.1 = (bf16[384,1536]{1,0:T(8,128)(2,1)S(1)}, bf16[384,1536]{1,0:T(8,128)(2,1)}, u32[]{:S(2)}) copy-start(bf16[384,1536]{1,0:T(8,128)(2,1)} %w_down.1) | copy-start | bytes 3538948
  52.2 7.9 %collective-permute-start.1 = (bf16[8,192,384]{2,1,0:T(8,128)(2,1)S(1)}, bf16[8,192,384]{2,1,0:T(8,128)(2,1)S(1)}, u32[]{:S(2)}, u32[]{:S(2)}) collective-permute-start(bf16[8,192,384]{2,1,0:T(8,128)(2,1)S(1)} %get-tuple-element.63), channel_id=1, source_target_pairs={{0,16},{16,0},{1,17},{17,1},{2,18},{18,2},{3,19},{19,3},{4,20},{20... | collective-permute-start | bytes 3538952 | tf_op jit(solution)/shard_map/ppermute | solution.py:474
  59.3 8.2 %collective-permute-start = (bf16[2,400,384]{2,1,0:T(8,128)(2,1)S(1)}, bf16[2,400,384]{2,1,0:T(8,128)(2,1)S(1)}, u32[]{:S(2)}, u32[]{:S(2)}) collective-permute-start(bf16[2,400,384]{2,1,0:T(8,128)(2,1)S(1)} %get-tuple-element.61), channel_id=1, source_target_pairs={{0,16},{16,0},{1,17},{17,1},{2,18},{18,2},{3,19},{19,3},{4,20},{20... | collective-permute-start | bytes 1843208 | tf_op jit(solution)/shard_map/ppermute | solution.py:474
  60.4 7.1 %collective-permute-start.2 = (bf16[192,384]{1,0:T(8,128)(2,1)S(1)}, bf16[192,384]{1,0:T(8,128)(2,1)S(1)}, u32[]{:S(2)}, u32[]{:S(2)}) collective-permute-start(bf16[192,384]{1,0:T(8,128)(2,1)S(1)} %get-tuple-element.66), channel_id=1, source_target_pairs={{0,64},{64,128},{128,192},{192,0},{1,65},{65,129},{129,193},{193,1... | collective-permute-start | bytes 442376 | tf_op jit(solution)/shard_map/ppermute | solution.py:478
  61.2 6.3 %collective-permute-start.3 = (bf16[192,384]{1,0:T(8,128)(2,1)S(1)}, bf16[192,384]{1,0:T(8,128)(2,1)S(1)}, u32[]{:S(2)}, u32[]{:S(2)}) collective-permute-start(bf16[192,384]{1,0:T(8,128)(2,1)S(1)} %get-tuple-element.67), channel_id=1, source_target_pairs={{0,192},{64,0},{128,64},{192,128},{1,193},{65,1},{129,65},{193,129... | collective-permute-start | bytes 442376 | tf_op jit(solution)/shard_map/ppermute | solution.py:478
  69.7 53.9 %all-to-all-start.1 = ((bf16[128,40,128]{2,1,0:T(8,128)(2,1)}), bf16[128,40,128]{2,1,0:T(8,128)(2,1)S(1)}, u32[]{:S(2)}, u32[]{:S(2)}) async-start(bf16[128,40,128]{2,1,0:T(8,128)(2,1)} %shard_map.142), calls=%async_computation.1 | async-start | bytes 2621440 | tf_op jit(solution)/shard_map/all_to_all | solution.py:470
  78.4 16.9 %collective-permute-start.4 = (bf16[2,192,384]{2,1,0:T(8,128)(2,1)S(1)}, bf16[2,192,384]{2,1,0:T(8,128)(2,1)S(1)}, u32[]{:S(2)}, u32[]{:S(2)}) collective-permute-start(bf16[2,192,384]{2,1,0:T(8,128)(2,1)S(1)} %get-tuple-element.73), channel_id=1, source_target_pairs={{0,64},{64,128},{128,192},{192,0},{1,65},{65,129},{129,193},{193,1... | collective-permute-start | bytes 884744 | tf_op jit(solution)/shard_map/ppermute | solution.py:478
  80.1 15.2 %collective-permute-start.5 = (bf16[2,192,384]{2,1,0:T(8,128)(2,1)S(1)}, bf16[2,192,384]{2,1,0:T(8,128)(2,1)S(1)}, u32[]{:S(2)}, u32[]{:S(2)}) collective-permute-start(bf16[2,192,384]{2,1,0:T(8,128)(2,1)S(1)} %get-tuple-element.74), channel_id=1, source_target_pairs={{0,192},{64,0},{128,64},{192,128},{1,193},{65,1},{129,65},{193,129... | collective-permute-start | bytes 884744 | tf_op jit(solution)/shard_map/ppermute | solution.py:478
  95.5 8.3 %collective-permute-start.6 = (bf16[192,384]{1,0:T(8,128)(2,1)S(1)}, bf16[192,384]{1,0:T(8,128)(2,1)S(1)}, u32[]{:S(2)}, u32[]{:S(2)}) collective-permute-start(bf16[192,384]{1,0:T(8,128)(2,1)S(1)} %get-tuple-element.76), channel_id=1, source_target_pairs={{0,32},{32,0},{1,33},{33,1},{2,34},{34,2},{3,35},{35,3},{4,36},{36... | collective-permute-start | bytes 442376 | tf_op jit(solution)/shard_map/ppermute | solution.py:474
  104.0 6.4 %collective-permute-start.7 = (bf16[4,96,128]{2,1,0:T(8,128)(2,1)S(1)}, bf16[4,96,128]{2,1,0:T(8,128)(2,1)S(1)}, u32[]{:S(2)}, u32[]{:S(2)}) collective-permute-start(bf16[4,96,128]{2,1,0:T(8,128)(2,1)S(1)} %get-tuple-element.78), channel_id=1, source_target_pairs={{0,2},{2,0},{4,6},{6,4},{8,10},{10,8},{12,14},{14,12},{1,3},{3,1},... | collective-permute-start | bytes 294920 | tf_op jit(solution)/shard_map/ppermute | solution.py:474
  110.4 5.1 %collective-permute-start.8 = (bf16[2,96,128]{2,1,0:T(8,128)(2,1)S(1)}, bf16[2,96,128]{2,1,0:T(8,128)(2,1)S(1)}, u32[]{:S(2)}, u32[]{:S(2)}) collective-permute-start(bf16[2,96,128]{2,1,0:T(8,128)(2,1)S(1)} %get-tuple-element.80), channel_id=1, source_target_pairs={{0,4},{2,6},{4,0},{6,2},{8,12},{10,14},{12,8},{14,10},{1,5},{3,7},... | collective-permute-start | bytes 147464 | tf_op jit(solution)/shard_map/ppermute | solution.py:474
  115.5 8.1 %collective-permute-start.9 = (bf16[1,96,128]{2,1,0:T(8,128)(2,1)S(1)}, bf16[1,96,128]{2,1,0:T(8,128)(2,1)S(1)}, u32[]{:S(2)}, u32[]{:S(2)}) collective-permute-start(bf16[1,96,128]{2,1,0:T(8,128)(2,1)S(1)} %get-tuple-element.82), channel_id=1, source_target_pairs={{0,8},{2,10},{4,12},{6,14},{8,0},{10,2},{12,4},{14,6},{1,9},{3,11}... | collective-permute-start | bytes 73736 | tf_op jit(solution)/shard_map/ppermute | solution.py:474
  123.8 5.6 %collective-permute-start.10 = (bf16[160,128]{1,0:T(8,128)(2,1)S(1)}, bf16[160,128]{1,0:T(8,128)(2,1)S(1)}, u32[]{:S(2)}, u32[]{:S(2)}) collective-permute-start(bf16[160,128]{1,0:T(8,128)(2,1)S(1)} %shard_map.148.own_ref), channel_id=1, source_target_pairs={{0,1},{1,0},{2,3},{3,2},{4,5},{5,4},{6,7},{7,6},{8,9},{9,8},{10,11... | collective-permute-start | bytes 122888 | tf_op jit(solution)/shard_map/ppermute | solution.py:561

commit v3 on v1

--- a/solution.py
+++ b/solution.py
@@ -204,18 +204,15 @@
         normal_hat, _ = norm_parts(resid[rows, :].astype(F32))
         normed[rows, :] = (normal_hat * gain_two[...]).astype(BF16)
         grad_turned[:, rows] = grad_out[rows, :].astype(F32).T.astype(BF16)
-    back[...] = jnp.zeros_like(back)
-
-    @pl.loop(0, 4)
-    def _(chunk):
-        cols = pl.ds(pl.multiple_of(chunk * 384, 384), 384)
+    for chunk in range(4):
+        cols = pl.ds(chunk * 384, 384)
         hidden = dot_nt(normed[...], w_up[cols, :])
         grad_act = dot(grad_out[...], w_down[:, cols])
         activated, grad_hidden = gelu_parts(hidden, grad_act)
-        hidden_grad[...] = grad_hidden.astype(BF16)
+        hidden_grad[:, cols] = grad_hidden.astype(BF16)
         down_total[:, cols] = dot(grad_turned[...], activated.astype(BF16))
-        up_total[cols, :] = dot_tn(hidden_grad[...], normed[...])
-        back[...] += dot(hidden_grad[...], w_up[cols, :])
+        up_total[cols, :] = dot_tn(hidden_grad[:, cols], normed[...])
+    back[...] = dot(hidden_grad[...], w_up[...])
 
     for ref, side in piece_sides(keep_ref, send_ref):
         for piece in range(8):
@@ -313,18 +310,46 @@
             ref[piece] = piece_rows[...].astype(BF16)
 
 
-def core_kernel(early_keep, early_recv, late_keep, late_recv, *outs):
+def core_kernel(
+    early_keep, early_recv, late_keep, late_recv, own, near, back, far_low, far_high,
+):
     row = lax.axis_index("y")
-    for step in range(4):
-        place = (row + step) & 3
+
+    def put(ref, step, col):
+        piece = ((row + step) & 3) * 2 + col
+        early = early_keep[piece].astype(F32) + early_recv[piece].astype(F32)
+        late = late_keep[piece].astype(F32) + late_recv[piece].astype(F32)
+        ref[:192] = early.astype(BF16)
+        if step == 2:
+            late = jnp.concatenate([late[:96], pltpu.roll(late[96:], 2, 0)], axis=0)
+        ref[192:] = late.astype(BF16)
+
+    for ref, step in ((own, 0), (near, 1), (back, 3)):
         for col in range(2):
-            piece = place * 2 + col
-            outs[step][col, :192] = (
-                early_keep[piece].astype(F32) + early_recv[piece].astype(F32)
-            ).astype(BF16)
-            outs[step][col, 192:] = (
-                late_keep[piece].astype(F32) + late_recv[piece].astype(F32)
-            ).astype(BF16)
+            put(ref.at[col], step, col)
+    put(far_low, 2, 0)
+    put(far_high, 2, 1)
+
+
+def ring_kernel(near, back, far_low, far_high, out_near, out_back):
+    out_near[0] = (near[0].astype(F32) + far_low[...].astype(F32)).astype(BF16)
+    out_near[1] = near[1]
+    out_back[0] = back[0]
+    out_back[1] = (back[1].astype(F32) + far_high[...].astype(F32)).astype(BF16)
+
+
+def row_kernel(own, near, back, keep_ref, send_ref, gains):
+    row, col = lax.axis_index("y"), lax.axis_index("xl")
+    first, second, third = (ref[0, 288:].astype(F32) for ref in (own, near, back))
+    gains[row] = first
+    gains[(row + 3) & 3] = second
+    gains[(row + 1) & 3] = third
+    gains[(row + 2) & 3] = pltpu.roll(second, 14, 0)
+    gain = ((gains[0] + gains[1]) + (gains[2] + gains[3])).astype(BF16)
+    for ref, side in ((keep_ref, col), (send_ref, 1 - col)):
+        total = own[side, :288].astype(F32) + near[side, :288].astype(F32)
+        ref[:288] = (total + back[side, :288].astype(F32)).astype(BF16)
+        ref[288:] = gain
 
 
 def pack_columns(rows, col):
@@ -333,35 +358,29 @@
     return jnp.where(iota((48, 128), 1) < 64, low, high)
 
 
-def pack_kernel(own, one, two, three, out_ref, gains):
-    row = lax.axis_index("y")
-    for step, ref in enumerate((own, one, two, three)):
-        gains[(row - step) & 3] = ref[0, 288:].astype(F32)
-    gain = (gains[0] + gains[1]) + (gains[2] + gains[3])
+def pack_kernel(keep_ref, recv_ref, out_ref):
+    total = keep_ref[...].astype(F32) + recv_ref[...].astype(F32)
     gain_rows = [
-        gain[which : which + 1, part * 128 : (part + 1) * 128]
+        total[288 + which : 289 + which, part * 128 : (part + 1) * 128]
         for which in range(2)
         for part in range(3)
     ]
     gain_rows.append(jnp.zeros((2, 128), F32))
-    for side in range(2):
-        total = own[side, :288].astype(F32) + one[side, :288].astype(F32)
-        total = total + (two[side, :288].astype(F32) + three[side, :288].astype(F32))
-        for col in range(8):
-            start = 96 + 24 * (col // 2)
-            block = total[start : start + 24]
-            if col % 2:
-                block = pltpu.roll(block, 192, 1)
-            out_ref[side * 8 + col] = jnp.concatenate(
-                [pack_columns(total[:96], col), block[:, :128], block[:, 128:256]]
-                + [pack_columns(total[192:], col)] + gain_rows,
-                axis=0,
-            ).astype(BF16)
+    for col in range(8):
+        start = 96 + 24 * (col // 2)
+        block = total[start : start + 24]
+        if col % 2:
+            block = pltpu.roll(block, 192, 1)
+        out_ref[col] = jnp.concatenate(
+            [pack_columns(total[:96], col), block[:, :128], block[:, 128:256]]
+            + [pack_columns(total[192:288], col)] + gain_rows,
+            axis=0,
+        ).astype(BF16)
 
 
 def block_sum(recv_ref, out_ref):
     total = recv_ref[0].astype(F32)
-    for place in range(1, 16):
+    for place in range(1, 8):
         total = total + recv_ref[place].astype(F32)
     out_ref[...] = total.astype(BF16)
 
@@ -392,7 +411,7 @@
         second_ref[lane] = late[51 + part]
 
 
-def call(kernel, outs, scratch=(), flops=0, nbytes=0, space=pltpu.VMEM):
+def call(kernel, outs, scratch=(), flops=0, nbytes=0, space=pltpu.VMEM, limit=16):
     vmem = pl.BlockSpec(memory_space=pltpu.VMEM)
     scratch = [pltpu.VMEM(*item) if isinstance(item, tuple) else item for item in scratch]
 
@@ -403,7 +422,7 @@
             in_specs=[pl.BlockSpec(memory_space=space)] * len(args),
             out_specs=[vmem] * len(outs),
             scratch_shapes=scratch,
-            compiler_params=pltpu.CompilerParams(vmem_limit_bytes=24 << 20),
+            compiler_params=pltpu.CompilerParams(vmem_limit_bytes=limit << 20),
             cost_estimate=pl.CostEstimate(flops=flops, bytes_accessed=nbytes, transcendentals=0),
         )(*args)
 
@@ -416,6 +435,10 @@
 
 def swap(values, axis):
     return lax.ppermute(values, axis, [(0, 1), (1, 0)])
+
+
+def shift(values, step):
+    return lax.ppermute(values, "y", [(place, (place + step) % 4) for place in range(4)])
 
 
 def body(tokens, grad_out, gain_first, gain_second, w_qkv, w_proj, w_up, w_down):
@@ -427,7 +450,8 @@
         [((SLOTS, 8, 384), BF16)],
         [tile, tile, pltpu.SemaphoreType.DMA((2,))],
         nbytes=2 * 10**6,
-        space=pltpu.HBM,
+        space=pl.ANY,
+        limit=60,
     )(
         tokens.transpose(1, 2, 0, 3), grad_out.transpose(1, 2, 0, 3)
     )
@@ -443,7 +467,7 @@
         mlp_kernel,
         [rows, ((8, 192, 384), BF16), ((8, 192, 384), BF16), ((1, 384), F32)],
         [
-            rows, rows, ((384, 512), BF16), ((1536, 384), F32), ((384, 1536), F32),
+            rows, ((512, 1536), BF16), ((384, 512), BF16), ((1536, 384), F32), ((384, 1536), F32),
             ((512, 384), F32), ((192, 384), F32),
         ],
         flops=3 * 10**9, nbytes=6 * 10**6,
@@ -454,26 +478,27 @@
         [rows, ((3, 512, 128), F32)],
         flops=6 * 10**9, nbytes=20 * 10**6,
     )(x, qkv, resid_grad, gain_one, w_qkv, w_proj)
-    returned = exchange(slots, HA + ("wa",))
     late_keep, late_send = call(
         weight_kernel,
         [((8, 112, 384), BF16), ((8, 112, 384), BF16)],
         [((1152, 384), F32), ((384, 384), F32), ((112, 384), F32)],
         flops=10**9, nbytes=5 * 10**6,
     )(rows_grad, normed, resid_grad, mixed, gain_sum_one, gain_sum_two)
-    piece = ((2, 304, 384), BF16)
-    own, *others = call(core_kernel, [piece] * 4, nbytes=10**7)(
+    whole, half = ((2, 304, 384), BF16), ((304, 384), BF16)
+    own, near, back, low, high = call(core_kernel, [whole, whole, whole, half, half], nbytes=10**7)(
         early_keep, swap(early_send, "core"), late_keep, swap(late_send, "core")
     )
-    arrived = [
-        lax.ppermute(values, "y", [(place, (place + step) % 4) for place in range(4)])
-        for step, values in zip((1, 2, 3), others)
-    ]
-    (blocks,) = call(
-        pack_kernel, [((16, 152, 128), BF16)], [((4, 16, 384), F32)], nbytes=3 * 10**6
-    )(own, *arrived)
+    slots, low, high = lax.optimization_barrier((slots, low, high))
+    returned = exchange(slots, HA + ("wa",))
+    near, back = call(ring_kernel, [whole, whole], nbytes=4 * 10**6)(
+        near, back, shift(low, 1), shift(high, 3)
+    )
+    keep, send = call(row_kernel, [half, half], [((4, 16, 384), F32)], nbytes=3 * 10**6)(
+        own, shift(near, 1), shift(back, 3)
+    )
+    (blocks,) = call(pack_kernel, [((8, 152, 128), BF16)], nbytes=10**6)(keep, swap(send, "xl"))
     blocks, returned = lax.optimization_barrier((blocks, returned))
-    (total,) = call(block_sum, [((152, 128), BF16)], nbytes=10**6)(exchange(blocks, ("xl", "wa")))
+    (total,) = call(block_sum, [((152, 128), BF16)], nbytes=10**6)(exchange(blocks, "wa"))
     other = swap(total, "dp")
     grad_qkv, grad_proj, grad_up, grad_down, first, second = call(
         functools.partial(final_weights, factor=factor),

time: 136 us -> 125 us (0.919)
  blocking collectives: 25.3 us -> 18.6 us
  local copies, waits for them, and re-layouts: 3.9 us -> 0.03 us
  Pallas kernels: 26.3 us -> 23.9 us
  starting transfers between devices: 30.3 us -> 32.1 us
  waiting for transfers between devices: 48.2 us -> 49.6 us
    ppermute x3 -> x4, waiting for transfers between devices: 2.53 us -> 11.1 us  [swap(): return lax.ppermute(values, axis, [(0, 1), (1, 0)])]
    ppermute x3 -> x4, waiting for transfers between devices: 22 us -> 14.8 us  [shift(): lax.ppermute(values, 'y', [(place, (place + step) % 4) for place in range...]
    all_to_all x1, blocking collectives: 25.3 us -> 18.6 us  [exchange(): return lax.all_to_all(values, axes, split_axis=0, concat_axis=0, tiled=True)]
    unnamed x24 -> x12, local copies, waits for them, and re-layouts: 3.9 us -> 0.02 us
    pallas_call x10 -> x12, Pallas kernels: 26.3 us -> 23.9 us  [run(): pl.pallas_call(kernel, out_shape=[jax.ShapeDtypeStruct(shape, dtype) for...]
    ppermute x3 -> x4, starting transfers between devices: 2.79 us -> 3.82 us  [swap(): return lax.ppermute(values, axis, [(0, 1), (1, 0)])]
    ppermute x3 -> x4, starting transfers between devices: 6.11 us -> 6.83 us  [shift(): lax.ppermute(values, 'y', [(place, (place + step) % 4) for place in range...]
  transfers between devices with their start and end apart: 8 -> 10, of which waited for: 4 -> 5; matrix products, arithmetic and copies ran while one was open for 0% -> 0% of each run, Pallas kernels for 9% -> 7%
where the time goes in v3:
time: 125 us
  waiting for transfers between devices  49.6 us (40%)
  starting transfers between devices  32.1 us (26%)
  Pallas kernels  23.9 us (19%)
  blocking collectives  18.6 us (15%)
    pallas_call x12, Pallas kernels, run(): pl.pallas_call(kernel, out_shape=[jax.ShapeDtypeStruct(shape, dtype) for...  23.9 us
    all_to_all x2, waiting for transfers between devices, exchange(): return lax.all_to_all(values, axes, split_axis=0, concat_axis=0, tiled=True)  23.7 us
    all_to_all x2, starting transfers between devices, exchange(): return lax.all_to_all(values, axes, split_axis=0, concat_axis=0, tiled=True)  21.4 us
    all_to_all x1, blocking collectives, exchange(): return lax.all_to_all(values, axes, split_axis=0, concat_axis=0, tiled=True)  18.6 us
    ppermute x4, waiting for transfers between devices, shift(): lax.ppermute(values, 'y', [(place, (place + step) % 4) for place in range...  14.8 us
    ppermute x4, waiting for transfers between devices, swap(): return lax.ppermute(values, axis, [(0, 1), (1, 0)])  11.1 us
    ppermute x4, starting transfers between devices, shift(): lax.ppermute(values, 'y', [(place, (place + step) % 4) for place in range...  6.83 us
    ppermute x4, starting transfers between devices, swap(): return lax.ppermute(values, axis, [(0, 1), (1, 0)])  3.82 us
  transfers between devices with their start and end apart: 10, of which 5 were waited for; matrix products, arithmetic and copies ran while one was open for 0% of the time, Pallas kernels for 7%

profile of v3, /device:TPU:2, one launch (start us, length us, event | category | flops | bytes accessed | tf_op | source)
XLA Modules:
  0.0 124.9 jit_solution(13329137465952982949)
XLA Ops:
  0.7 2.2 %shard_map.135 = bf16[128,8,384]{2,1,0:T(8,128)(2,1)} custom-call(bf16[14,7,4,384]{3,2,1,0:T(4,128)(2,1)} %bitcast.7, bf16[14,7,4,384]{3,2,1,0:T(4,128)(2,1)} %bitcast.8), custom_call_target="tpu_custom_call" | custom-call | bytes 2000000 | tf_op jit(solution)/shard_map/pallas_call | solution.py:419
  2.9 13.9 %all-to-all-start = ((bf16[128,8,384]{2,1,0:T(8,128)(2,1)}), bf16[128,8,384]{2,1,0:T(8,128)(2,1)S(1)}, u32[]{:S(2)}, u32[]{:S(2)}) async-start(bf16[128,8,384]{2,1,0:T(8,128)(2,1)} %shard_map.135), calls=%async_computation | async-start | bytes 1572864 | tf_op jit(solution)/shard_map/all_to_all | solution.py:433
  16.9 23.7 %all-to-all-done = bf16[128,8,384]{2,1,0:T(8,128)(2,1)S(1)} async-done(((bf16[128,8,384]{2,1,0:T(8,128)(2,1)}), bf16[128,8,384]{2,1,0:T(8,128)(2,1)S(1)}, u32[]{:S(2)}, u32[]{:S(2)}) %all-to-all-start) | async-done | bytes 786464 | tf_op jit(solution)/shard_map/all_to_all | solution.py:433
  40.6 4.2 %shard_map.136 = (bf16[512,384]{1,0:T(8,128)(2,1)S(1)}, bf16[512,1152]{1,0:T(8,128)(2,1)S(1)}, bf16[512,384]{1,0:T(8,128)(2,1)S(1)}, bf16[512,384]{1,0:T(8,128)(2,1)S(1)}, bf16[512,384]{1,0:T(8,128)(2,1)S(1)}) custom-call(bf16[1024,384]{1,0:T(8,128)(2,1)S(1)} %bitcast.6, f32[1,384]{1,0:T(1,128)S(1)} %reshape.24.gain_one, bf16[1152,384]{1,0:T(8,128)(2,1)S(1)} %copy-done.2, ...), custom_call_target="tpu_custom_call" | custom-call | flops 1000000000 | bytes 4000000 | tf_op jit(solution)/shard_map/pallas_call | solution.py:419
  44.8 6.9 %shard_map.137 = (bf16[512,384]{1,0:T(8,128)(2,1)S(1)}, bf16[8,192,384]{2,1,0:T(8,128)(2,1)S(1)}, bf16[8,192,384]{2,1,0:T(8,128)(2,1)S(1)}, f32[1,384]{1,0:T(1,128)S(1)}) custom-call(bf16[512,384]{1,0:T(8,128)(2,1)S(1)} %get-tuple-element.42.grad_out, bf16[512,384]{1,0:T(8,128)(2,1)S(1)} %get-tuple-element.43.resid, f32[1,384]{1,0:T(1,128)S(1)} %reshape.25.gain_two, ...), custom_call_target="tpu_custom_call" | custom-call | flops 3000000000 | bytes 6000000 | tf_op jit(solution)/shard_map/pallas_call | solution.py:419
  52.0 6.2 %shard_map.138 = (bf16[128,4,384]{2,1,0:T(4,128)(2,1)}, bf16[512,1152]{1,0:T(8,128)(2,1)S(1)}, bf16[512,384]{1,0:T(8,128)(2,1)S(1)}, f32[1,384]{1,0:T(1,128)S(1)}) custom-call(bf16[512,384]{1,0:T(8,128)(2,1)S(1)} %get-tuple-element.46.x_ref, bf16[512,1152]{1,0:T(8,128)(2,1)S(1)} %get-tuple-element.47.qkv_ref, ...), custom_call_target="tpu_custom_call" | custom-call | flops 6000000000 | bytes 20000000 | tf_op jit(solution)/shard_map/pallas_call | solution.py:419
  58.2 1.6 %shard_map.139 = (bf16[8,112,384]{2,1,0:T(8,128)(2,1)S(1)}, bf16[8,112,384]{2,1,0:T(8,128)(2,1)S(1)}) custom-call(bf16[512,1152]{1,0:T(8,128)(2,1)S(1)} %get-tuple-element.49.rows_grad, bf16[512,384]{1,0:T(8,128)(2,1)S(1)} %get-tuple-element.50.normed, bf16[512,384]{1,0:T(8,128)(2,1)S(1)} %get-tuple-element.48.resid_grad_ref.resid_grad, ...), custom_call_target="tpu_custom_call" | custom-call | flops 1000000000 | bytes 5000000 | tf_op jit(solution)/shard_map/pallas_call | solution.py:419
  59.8 0.6 collective-permute-start.1
  60.4 1.8 %collective-permute-done.1.late_recv = bf16[8,112,384]{2,1,0:T(8,128)(2,1)S(1)} collective-permute-done((bf16[8,112,384]{2,1,0:T(8,128)(2,1)S(1)}, bf16[8,112,384]{2,1,0:T(8,128)(2,1)S(1)}, u32[]{:S(2)}, u32[]{:S(2)}) %collective-permute-start.1) | collective-permute-done | bytes 688160 | tf_op jit(solution)/shard_map/ppermute | solution.py:437
  62.2 0.5 shard_map.140
  62.6 0.8 collective-permute-start.2
  63.5 2.5 %collective-permute-start.3 = (bf16[304,384]{1,0:T(8,128)(2,1)S(1)}, bf16[304,384]{1,0:T(8,128)(2,1)S(1)}, u32[]{:S(2)}, u32[]{:S(2)}) collective-permute-start(bf16[304,384]{1,0:T(8,128)(2,1)S(1)} %get-tuple-element.63), channel_id=1, source_target_pairs={{0,192},{64,0},{128,64},{192,128},{1,193},{65,1},{129,65},{193,129... | collective-permute-start | bytes 700424 | tf_op jit(solution)/shard_map/ppermute | solution.py:441
  65.9 7.5 %all-to-all-start.1 = ((bf16[128,4,384]{2,1,0:T(4,128)(2,1)}), bf16[128,4,384]{2,1,0:T(4,128)(2,1)S(1)}, u32[]{:S(2)}, u32[]{:S(2)}) async-start(bf16[128,4,384]{2,1,0:T(4,128)(2,1)} %get-tuple-element.68), calls=%async_computation.1 | async-start | bytes 786432 | tf_op jit(solution)/shard_map/all_to_all | solution.py:433
  73.6 1.8 %collective-permute-start.4 = (bf16[2,304,384]{2,1,0:T(8,128)(2,1)S(1)}, bf16[2,304,384]{2,1,0:T(8,128)(2,1)S(1)}, u32[]{:S(2)}, u32[]{:S(2)}) collective-permute-start(bf16[2,304,384]{2,1,0:T(8,128)(2,1)S(1)} %get-tuple-element.64), channel_id=1, source_target_pairs={{0,64},{64,128},{128,192},{192,0},{1,65},{65,129},{129,193},{193,1... | collective-permute-start | bytes 1400840 | tf_op jit(solution)/shard_map/ppermute | solution.py:441
  75.4 1.7 %collective-permute-start.5 = (bf16[2,304,384]{2,1,0:T(8,128)(2,1)S(1)}, bf16[2,304,384]{2,1,0:T(8,128)(2,1)S(1)}, u32[]{:S(2)}, u32[]{:S(2)}) collective-permute-start(bf16[2,304,384]{2,1,0:T(8,128)(2,1)S(1)} %get-tuple-element.65), channel_id=1, source_target_pairs={{0,192},{64,0},{128,64},{192,128},{1,193},{65,1},{129,65},{193,129... | collective-permute-start | bytes 1400840 | tf_op jit(solution)/shard_map/ppermute | solution.py:441
  77.1 14.8 %collective-permute-done.4.near = bf16[2,304,384]{2,1,0:T(8,128)(2,1)S(1)} collective-permute-done((bf16[2,304,384]{2,1,0:T(8,128)(2,1)S(1)}, bf16[2,304,384]{2,1,0:T(8,128)(2,1)S(1)}, u32[]{:S(2)}, u32[]{:S(2)}) %collective-permute-start.4) | collective-permute-done | bytes 466976 | tf_op jit(solution)/shard_map/ppermute | solution.py:441
  91.9 0.3 shard_map.142
  92.2 0.7 collective-permute-start.6
  92.9 6.8 %collective-permute-done.6.recv_ref = bf16[304,384]{1,0:T(8,128)(2,1)S(1)} collective-permute-done((bf16[304,384]{1,0:T(8,128)(2,1)S(1)}, bf16[304,384]{1,0:T(8,128)(2,1)S(1)}, u32[]{:S(2)}, u32[]{:S(2)}) %collective-permute-start.6) | collective-permute-done | bytes 233504 | tf_op jit(solution)/shard_map/ppermute | solution.py:437
  100.0 18.6 %all_to_all.15.recv_ref = bf16[8,152,128]{2,1,0:T(8,128)(2,1)S(1)} all-to-all(bf16[8,152,128]{2,1,0:T(8,128)(2,1)S(1)} %shard_map.143), channel_id=1, replica_groups=mesh['y'=4,'xl'=2,'core'=2,'wa'=8,'dp'=2] {'wa'}, dimensions={0} | all-to-all | bytes 622592 | tf_op jit(solution)/shard_map/all_to_all | solution.py:433
  118.6 2.2 %collective-permute-start.7 = (bf16[152,128]{1,0:T(8,128)(2,1)S(1)}, bf16[152,128]{1,0:T(8,128)(2,1)S(1)}, u32[]{:S(2)}, u32[]{:S(2)}) collective-permute-start(bf16[152,128]{1,0:T(8,128)(2,1)S(1)} %shard_map.145.own_ref), channel_id=1, source_target_pairs={{0,1},{1,0},{2,3},{3,2},{4,5},{5,4},{6,7},{7,6},{8,9},{9,8},{10,11... | collective-permute-start | bytes 116744 | tf_op jit(solution)/shard_map/ppermute | solution.py:437
  120.8 0.8 shard_map.144
  121.6 2.6 %collective-permute-done.7.other_ref = bf16[152,128]{1,0:T(8,128)(2,1)S(1)} collective-permute-done((bf16[152,128]{1,0:T(8,128)(2,1)S(1)}, bf16[152,128]{1,0:T(8,128)(2,1)S(1)}, u32[]{:S(2)}, u32[]{:S(2)}) %collective-permute-start.7) | collective-permute-done | bytes 38944 | tf_op jit(solution)/shard_map/ppermute | solution.py:437
  124.2 0.8 shard_map.146
  (23 shorter events, 0.8 us)
Async XLA Ops:
  0.6 16.2 %copy-start.4 = (f32[384]{0:T(512)S(1)}, f32[384]{0:T(512)}, u32[]{:S(2)}) copy-start(f32[384]{0:T(512)} %param.10) | copy-start | bytes 4612
  0.6 16.2 %copy-start.5 = (f32[384]{0:T(512)S(1)}, f32[384]{0:T(512)}, u32[]{:S(2)}) copy-start(f32[384]{0:T(512)} %param.11) | copy-start | bytes 4612
  0.7 39.9 %copy-start.2 = (bf16[1152,384]{1,0:T(8,128)(2,1)S(1)}, bf16[1152,384]{1,0:T(8,128)(2,1)}, u32[]{:S(2)}) copy-start(bf16[1152,384]{1,0:T(8,128)(2,1)} %w_qkv.3) | copy-start | bytes 2654212
  0.7 39.9 %copy-start.3 = (bf16[384,384]{1,0:T(8,128)(2,1)S(1)}, bf16[384,384]{1,0:T(8,128)(2,1)}, u32[]{:S(2)}) copy-start(bf16[384,384]{1,0:T(8,128)(2,1)} %w_proj.3) | copy-start | bytes 884740
  2.9 37.7 %all-to-all-start = ((bf16[128,8,384]{2,1,0:T(8,128)(2,1)}), bf16[128,8,384]{2,1,0:T(8,128)(2,1)S(1)}, u32[]{:S(2)}, u32[]{:S(2)}) async-start(bf16[128,8,384]{2,1,0:T(8,128)(2,1)} %shard_map.135), calls=%async_computation | async-start | bytes 1572864 | tf_op jit(solution)/shard_map/all_to_all | solution.py:433
  40.6 4.2 %copy-start = (bf16[1536,384]{1,0:T(8,128)(2,1)S(1)}, bf16[1536,384]{1,0:T(8,128)(2,1)}, u32[]{:S(2)}) copy-start(bf16[1536,384]{1,0:T(8,128)(2,1)} %w_up.1) | copy-start | bytes 3538948
  40.6 4.3 %copy-start.1 = (bf16[384,1536]{1,0:T(8,128)(2,1)S(1)}, bf16[384,1536]{1,0:T(8,128)(2,1)}, u32[]{:S(2)}) copy-start(bf16[384,1536]{1,0:T(8,128)(2,1)} %w_down.1) | copy-start | bytes 3538948
  51.7 10.4 %collective-permute-start = (bf16[8,192,384]{2,1,0:T(8,128)(2,1)S(1)}, bf16[8,192,384]{2,1,0:T(8,128)(2,1)S(1)}, u32[]{:S(2)}, u32[]{:S(2)}) collective-permute-start(bf16[8,192,384]{2,1,0:T(8,128)(2,1)S(1)} %get-tuple-element.45), channel_id=1, source_target_pairs={{0,16},{16,0},{1,17},{17,1},{2,18},{18,2},{3,19},{19,3},{4,20},{20... | collective-permute-start | bytes 3538952 | tf_op jit(solution)/shard_map/ppermute | solution.py:437
  59.8 2.4 %collective-permute-start.1 = (bf16[8,112,384]{2,1,0:T(8,128)(2,1)S(1)}, bf16[8,112,384]{2,1,0:T(8,128)(2,1)S(1)}, u32[]{:S(2)}, u32[]{:S(2)}) collective-permute-start(bf16[8,112,384]{2,1,0:T(8,128)(2,1)S(1)} %get-tuple-element.55), channel_id=1, source_target_pairs={{0,16},{16,0},{1,17},{17,1},{2,18},{18,2},{3,19},{19,3},{4,20},{20... | collective-permute-start | bytes 2064392 | tf_op jit(solution)/shard_map/ppermute | solution.py:437
  62.6 10.8 %collective-permute-start.2 = (bf16[304,384]{1,0:T(8,128)(2,1)S(1)}, bf16[304,384]{1,0:T(8,128)(2,1)S(1)}, u32[]{:S(2)}, u32[]{:S(2)}) collective-permute-start(bf16[304,384]{1,0:T(8,128)(2,1)S(1)} %get-tuple-element.62), channel_id=1, source_target_pairs={{0,64},{64,128},{128,192},{192,0},{1,65},{65,129},{129,193},{193,1... | collective-permute-start | bytes 700424 | tf_op jit(solution)/shard_map/ppermute | solution.py:441
  63.5 10.0 %collective-permute-start.3 = (bf16[304,384]{1,0:T(8,128)(2,1)S(1)}, bf16[304,384]{1,0:T(8,128)(2,1)S(1)}, u32[]{:S(2)}, u32[]{:S(2)}) collective-permute-start(bf16[304,384]{1,0:T(8,128)(2,1)S(1)} %get-tuple-element.63), channel_id=1, source_target_pairs={{0,192},{64,0},{128,64},{192,128},{1,193},{65,1},{129,65},{193,129... | collective-permute-start | bytes 700424 | tf_op jit(solution)/shard_map/ppermute | solution.py:441
  65.9 34.0 %all-to-all-start.1 = ((bf16[128,4,384]{2,1,0:T(4,128)(2,1)}), bf16[128,4,384]{2,1,0:T(4,128)(2,1)S(1)}, u32[]{:S(2)}, u32[]{:S(2)}) async-start(bf16[128,4,384]{2,1,0:T(4,128)(2,1)} %get-tuple-element.68), calls=%async_computation.1 | async-start | bytes 786432 | tf_op jit(solution)/shard_map/all_to_all | solution.py:433
  73.6 18.3 %collective-permute-start.4 = (bf16[2,304,384]{2,1,0:T(8,128)(2,1)S(1)}, bf16[2,304,384]{2,1,0:T(8,128)(2,1)S(1)}, u32[]{:S(2)}, u32[]{:S(2)}) collective-permute-start(bf16[2,304,384]{2,1,0:T(8,128)(2,1)S(1)} %get-tuple-element.64), channel_id=1, source_target_pairs={{0,64},{64,128},{128,192},{192,0},{1,65},{65,129},{129,193},{193,1... | collective-permute-start | bytes 1400840 | tf_op jit(solution)/shard_map/ppermute | solution.py:441
  75.4 16.5 %collective-permute-start.5 = (bf16[2,304,384]{2,1,0:T(8,128)(2,1)S(1)}, bf16[2,304,384]{2,1,0:T(8,128)(2,1)S(1)}, u32[]{:S(2)}, u32[]{:S(2)}) collective-permute-start(bf16[2,304,384]{2,1,0:T(8,128)(2,1)S(1)} %get-tuple-element.65), channel_id=1, source_target_pairs={{0,192},{64,0},{128,64},{192,128},{1,193},{65,1},{129,65},{193,129... | collective-permute-start | bytes 1400840 | tf_op jit(solution)/shard_map/ppermute | solution.py:441
  92.2 7.5 %collective-permute-start.6 = (bf16[304,384]{1,0:T(8,128)(2,1)S(1)}, bf16[304,384]{1,0:T(8,128)(2,1)S(1)}, u32[]{:S(2)}, u32[]{:S(2)}) collective-permute-start(bf16[304,384]{1,0:T(8,128)(2,1)S(1)} %get-tuple-element.67), channel_id=1, source_target_pairs={{0,32},{32,0},{1,33},{33,1},{2,34},{34,2},{3,35},{35,3},{4,36},{36... | collective-permute-start | bytes 700424 | tf_op jit(solution)/shard_map/ppermute | solution.py:437
  118.6 5.6 %collective-permute-start.7 = (bf16[152,128]{1,0:T(8,128)(2,1)S(1)}, bf16[152,128]{1,0:T(8,128)(2,1)S(1)}, u32[]{:S(2)}, u32[]{:S(2)}) collective-permute-start(bf16[152,128]{1,0:T(8,128)(2,1)S(1)} %shard_map.145.own_ref), channel_id=1, source_target_pairs={{0,1},{1,0},{2,3},{3,2},{4,5},{5,4},{6,7},{7,6},{8,9},{9,8},{10,11... | collective-permute-start | bytes 116744 | tf_op jit(solution)/shard_map/ppermute | solution.py:437

commit v4 on v3

--- a/solution.py
+++ b/solution.py
@@ -100,11 +100,6 @@
 def load_every(ref, start, step):
     parts = [ref[part, pl.ds(start, SLOTS, stride=step), :] for part in range(3)]
     return jnp.concatenate(parts, axis=1).astype(BF16)
-
-
-def store_every(ref, start, step, values):
-    for part in range(3):
-        ref[part, pl.ds(start, SLOTS, stride=step), :] = values[:, part * 128 : (part + 1) * 128]
 
 
 def send_kernel(tokens_hbm, grad_hbm, out_ref, tokens_ref, grad_ref, sems):
@@ -131,18 +126,18 @@
 def return_kernel(recv_ref, out_ref):
     for line in range(LINES):
         for column in range(GRID):
-            out_ref[line, column] = recv_ref[owner_slot(line, column)]
+            slot = owner_slot(line, column)
+            for part in range(3):
+                out_ref[line, column, :, part * 128 : (part + 1) * 128] = recv_ref[slot, part]
 
 
 def gelu_parts(hidden, grad):
-    inner = 0.7978845608028654
+    inner, cubic = 0.7978845608028654, 0.7978845608028654 * 0.044715
     square = hidden * hidden
-    tanh = jnp.tanh(inner * (hidden + 0.044715 * (hidden * square)))
-    half = 0.5 * (1.0 + tanh)
-    slope = half + 0.5 * hidden * (1.0 - tanh * tanh) * (
-        inner * (1.0 + 3 * 0.044715 * square)
-    )
-    return hidden * half, grad * slope
+    part = 0.5 * jnp.tanh(hidden * (inner + cubic * square)) + 0.5
+    twice = hidden * (2 * inner + 6 * cubic * square)
+    slope = part * (1.0 + (1.0 - part) * twice)
+    return hidden * part, grad * slope
 
 
 def forward_kernel(
@@ -282,12 +277,15 @@
         grad_x = resid_grad_ref[rows, :].astype(F32) + norm_back(
             grad, normal_hat, inv_std, gain_one[...]
         )
-        store_every(slots, crop, 4, dot(match, grad_x.astype(BF16)))
+        returned = dot(match, grad_x.astype(BF16))
+        for part in range(3):
+            slots[pl.ds(part * 4 + crop, SLOTS, stride=12), :] = returned[
+                :, part * 128 : (part + 1) * 128
+            ]
     for slot in range(SLOTS):
         for part in range(3):
-            out_ref[slot, :, part * 128 : (part + 1) * 128] = slots[
-                part, slot * 4 : slot * 4 + 4, :
-            ].astype(BF16)
+            start = slot * 12 + part * 4
+            out_ref[slot, part] = slots[start : start + 4, :].astype(BF16)
     gain_ref[...] = gain
 
 
@@ -474,8 +472,8 @@
     )(grad_rows, resid, gain_two, w_up, w_down)
     slots, rows_grad, normed, gain_sum_one = call(
         attention_kernel,
-        [((SLOTS, 4, 384), BF16), ((512, 1152), BF16), rows, ((1, 384), F32)],
-        [rows, ((3, 512, 128), F32)],
+        [((SLOTS, 3, 4, 128), BF16), ((512, 1152), BF16), rows, ((1, 384), F32)],
+        [rows, ((SLOTS * 12, 128), F32)],
         flops=6 * 10**9, nbytes=20 * 10**6,
     )(x, qkv, resid_grad, gain_one, w_qkv, w_proj)
     late_keep, late_send = call(
@@ -488,11 +486,11 @@
     own, near, back, low, high = call(core_kernel, [whole, whole, whole, half, half], nbytes=10**7)(
         early_keep, swap(early_send, "core"), late_keep, swap(late_send, "core")
     )
-    slots, low, high = lax.optimization_barrier((slots, low, high))
-    returned = exchange(slots, HA + ("wa",))
     near, back = call(ring_kernel, [whole, whole], nbytes=4 * 10**6)(
         near, back, shift(low, 1), shift(high, 3)
     )
+    slots, near, back = lax.optimization_barrier((slots, near, back))
+    returned = exchange(slots, HA + ("wa",))
     keep, send = call(row_kernel, [half, half], [((4, 16, 384), F32)], nbytes=3 * 10**6)(
         own, shift(near, 1), shift(back, 3)
     )

time: 125 us -> 132 us (1.056)
  waiting for transfers between devices: 49.6 us -> 55.6 us
    ppermute x4, waiting for transfers between devices: 14.8 us -> 20.8 us  [shift(): lax.ppermute(values, 'y', [(place, (place + step) % 4) for place in range...]
  transfers between devices with their start and end apart: 10 -> 10, of which waited for: 5 -> 6; matrix products, arithmetic and copies ran while one was open for 0% -> 0% of each run, Pallas kernels for 7% -> 7%
where the time goes in v4:
time: 132 us
  waiting for transfers between devices  55.6 us (42%)
  starting transfers between devices  33.1 us (25%)
  Pallas kernels  23.8 us (18%)
  blocking collectives  18.7 us (14%)
    pallas_call x12, Pallas kernels, run(): pl.pallas_call(kernel, out_shape=[jax.ShapeDtypeStruct(shape, dtype) for...  23.8 us
    all_to_all x2, waiting for transfers between devices, exchange(): return lax.all_to_all(values, axes, split_axis=0, concat_axis=0, tiled=True)  23.7 us
    all_to_all x2, starting transfers between devices, exchange(): return lax.all_to_all(values, axes, split_axis=0, concat_axis=0, tiled=True)  22.5 us
    ppermute x4, waiting for transfers between devices, shift(): lax.ppermute(values, 'y', [(place, (place + step) % 4) for place in range...  20.8 us
    all_to_all x1, blocking collectives, exchange(): return lax.all_to_all(values, axes, split_axis=0, concat_axis=0, tiled=True)  18.7 us
    ppermute x4, waiting for transfers between devices, swap(): return lax.ppermute(values, axis, [(0, 1), (1, 0)])  11.2 us
    ppermute x4, starting transfers between devices, shift(): lax.ppermute(values, 'y', [(place, (place + step) % 4) for place in range...  6.81 us
    ppermute x4, starting transfers between devices, swap(): return lax.ppermute(values, axis, [(0, 1), (1, 0)])  3.75 us
  transfers between devices with their start and end apart: 10, of which 6 were waited for; matrix products, arithmetic and copies ran while one was open for 0% of the time, Pallas kernels for 7%

profile of v4, /device:TPU:2, one launch (start us, length us, event | category | flops | bytes accessed | tf_op | source)
XLA Modules:
  0.0 132.0 jit_solution(16456312249374825971)
XLA Ops:
  0.7 2.2 %shard_map.135 = bf16[128,8,384]{2,1,0:T(8,128)(2,1)} custom-call(bf16[14,7,4,384]{3,2,1,0:T(4,128)(2,1)} %bitcast.7, bf16[14,7,4,384]{3,2,1,0:T(4,128)(2,1)} %bitcast.8), custom_call_target="tpu_custom_call" | custom-call | bytes 2000000 | tf_op jit(solution)/shard_map/pallas_call | solution.py:417
  2.9 13.9 %all-to-all-start = ((bf16[128,8,384]{2,1,0:T(8,128)(2,1)}), bf16[128,8,384]{2,1,0:T(8,128)(2,1)S(1)}, u32[]{:S(2)}, u32[]{:S(2)}) async-start(bf16[128,8,384]{2,1,0:T(8,128)(2,1)} %shard_map.135), calls=%async_computation | async-start | bytes 1572864 | tf_op jit(solution)/shard_map/all_to_all | solution.py:431
  16.9 23.7 %all-to-all-done = bf16[128,8,384]{2,1,0:T(8,128)(2,1)S(1)} async-done(((bf16[128,8,384]{2,1,0:T(8,128)(2,1)}), bf16[128,8,384]{2,1,0:T(8,128)(2,1)S(1)}, u32[]{:S(2)}, u32[]{:S(2)}) %all-to-all-start) | async-done | bytes 786464 | tf_op jit(solution)/shard_map/all_to_all | solution.py:431
  40.6 4.2 %shard_map.136 = (bf16[512,384]{1,0:T(8,128)(2,1)S(1)}, bf16[512,1152]{1,0:T(8,128)(2,1)S(1)}, bf16[512,384]{1,0:T(8,128)(2,1)S(1)}, bf16[512,384]{1,0:T(8,128)(2,1)S(1)}, bf16[512,384]{1,0:T(8,128)(2,1)S(1)}) custom-call(bf16[1024,384]{1,0:T(8,128)(2,1)S(1)} %bitcast.6, f32[1,384]{1,0:T(1,128)S(1)} %reshape.24.gain_one, bf16[1152,384]{1,0:T(8,128)(2,1)S(1)} %copy-done.2, ...), custom_call_target="tpu_custom_call" | custom-call | flops 1000000000 | bytes 4000000 | tf_op jit(solution)/shard_map/pallas_call | solution.py:417
  44.8 6.8 %shard_map.137 = (bf16[512,384]{1,0:T(8,128)(2,1)S(1)}, bf16[8,192,384]{2,1,0:T(8,128)(2,1)S(1)}, bf16[8,192,384]{2,1,0:T(8,128)(2,1)S(1)}, f32[1,384]{1,0:T(1,128)S(1)}) custom-call(bf16[512,384]{1,0:T(8,128)(2,1)S(1)} %get-tuple-element.42.grad_out, bf16[512,384]{1,0:T(8,128)(2,1)S(1)} %get-tuple-element.43.resid, f32[1,384]{1,0:T(1,128)S(1)} %reshape.25.gain_two, ...), custom_call_target="tpu_custom_call" | custom-call | flops 3000000000 | bytes 6000000 | tf_op jit(solution)/shard_map/pallas_call | solution.py:417
  51.9 6.2 %shard_map.138 = (bf16[128,3,4,128]{3,2,1,0:T(4,128)(2,1)}, bf16[512,1152]{1,0:T(8,128)(2,1)S(1)}, bf16[512,384]{1,0:T(8,128)(2,1)S(1)}, f32[1,384]{1,0:T(1,128)S(1)}) custom-call(bf16[512,384]{1,0:T(8,128)(2,1)S(1)} %get-tuple-element.46.x_ref, bf16[512,1152]{1,0:T(8,128)(2,1)S(1)} %get-tuple-element.47.qkv_ref, ...), custom_call_target="tpu_custom_call" | custom-call | flops 6000000000 | bytes 20000000 | tf_op jit(solution)/shard_map/pallas_call | solution.py:417
  58.1 1.6 %shard_map.139 = (bf16[8,112,384]{2,1,0:T(8,128)(2,1)S(1)}, bf16[8,112,384]{2,1,0:T(8,128)(2,1)S(1)}) custom-call(bf16[512,1152]{1,0:T(8,128)(2,1)S(1)} %get-tuple-element.49.rows_grad, bf16[512,384]{1,0:T(8,128)(2,1)S(1)} %get-tuple-element.50.normed, bf16[512,384]{1,0:T(8,128)(2,1)S(1)} %get-tuple-element.48.resid_grad_ref.resid_grad, ...), custom_call_target="tpu_custom_call" | custom-call | flops 1000000000 | bytes 5000000 | tf_op jit(solution)/shard_map/pallas_call | solution.py:417
  59.7 0.6 collective-permute-start.1
  60.3 1.8 %collective-permute-done.1.late_recv = bf16[8,112,384]{2,1,0:T(8,128)(2,1)S(1)} collective-permute-done((bf16[8,112,384]{2,1,0:T(8,128)(2,1)S(1)}, bf16[8,112,384]{2,1,0:T(8,128)(2,1)S(1)}, u32[]{:S(2)}, u32[]{:S(2)}) %collective-permute-start.1) | collective-permute-done | bytes 688160 | tf_op jit(solution)/shard_map/ppermute | solution.py:435
  62.0 0.5 shard_map.140
  62.5 0.8 collective-permute-start.2
  63.3 2.5 %collective-permute-start.3 = (bf16[304,384]{1,0:T(8,128)(2,1)S(1)}, bf16[304,384]{1,0:T(8,128)(2,1)S(1)}, u32[]{:S(2)}, u32[]{:S(2)}) collective-permute-start(bf16[304,384]{1,0:T(8,128)(2,1)S(1)} %get-tuple-element.61), channel_id=1, source_target_pairs={{0,192},{64,0},{128,64},{192,128},{1,193},{65,1},{129,65},{193,129... | collective-permute-start | bytes 700424 | tf_op jit(solution)/shard_map/ppermute | solution.py:439
  65.8 5.9 %collective-permute-done.2.far_low = bf16[304,384]{1,0:T(8,128)(2,1)S(1)} collective-permute-done((bf16[304,384]{1,0:T(8,128)(2,1)S(1)}, bf16[304,384]{1,0:T(8,128)(2,1)S(1)}, u32[]{:S(2)}, u32[]{:S(2)}) %collective-permute-start.2) | collective-permute-done | bytes 233504 | tf_op jit(solution)/shard_map/ppermute | solution.py:439
  71.9 8.6 %all-to-all-start.1 = ((bf16[128,3,4,128]{3,2,1,0:T(4,128)(2,1)}), bf16[128,3,4,128]{3,2,1,0:T(4,128)(2,1)S(1)}, u32[]{:S(2)}, u32[]{:S(2)}) async-start(bf16[128,3,4,128]{3,2,1,0:T(4,128)(2,1)} %get-tuple-element.68), calls=%async_computation.1 | async-start | bytes 786432 | tf_op jit(solution)/shard_map/all_to_all | solution.py:431
  80.5 1.7 %collective-permute-start.4 = (bf16[2,304,384]{2,1,0:T(8,128)(2,1)S(1)}, bf16[2,304,384]{2,1,0:T(8,128)(2,1)S(1)}, u32[]{:S(2)}, u32[]{:S(2)}) collective-permute-start(bf16[2,304,384]{2,1,0:T(8,128)(2,1)S(1)} %get-tuple-element.64), channel_id=1, source_target_pairs={{0,64},{64,128},{128,192},{192,0},{1,65},{65,129},{129,193},{193,1... | collective-permute-start | bytes 1400840 | tf_op jit(solution)/shard_map/ppermute | solution.py:439
  82.3 1.7 %collective-permute-start.5 = (bf16[2,304,384]{2,1,0:T(8,128)(2,1)S(1)}, bf16[2,304,384]{2,1,0:T(8,128)(2,1)S(1)}, u32[]{:S(2)}, u32[]{:S(2)}) collective-permute-start(bf16[2,304,384]{2,1,0:T(8,128)(2,1)S(1)} %get-tuple-element.65), channel_id=1, source_target_pairs={{0,192},{64,0},{128,64},{192,128},{1,193},{65,1},{129,65},{193,129... | collective-permute-start | bytes 1400840 | tf_op jit(solution)/shard_map/ppermute | solution.py:439
  84.0 14.8 %collective-permute-done.4.near = bf16[2,304,384]{2,1,0:T(8,128)(2,1)S(1)} collective-permute-done((bf16[2,304,384]{2,1,0:T(8,128)(2,1)S(1)}, bf16[2,304,384]{2,1,0:T(8,128)(2,1)S(1)}, u32[]{:S(2)}, u32[]{:S(2)}) %collective-permute-start.4) | collective-permute-done | bytes 466976 | tf_op jit(solution)/shard_map/ppermute | solution.py:439
  99.1 0.7 collective-permute-start.6
  99.8 6.8 %collective-permute-done.6.recv_ref = bf16[304,384]{1,0:T(8,128)(2,1)S(1)} collective-permute-done((bf16[304,384]{1,0:T(8,128)(2,1)S(1)}, bf16[304,384]{1,0:T(8,128)(2,1)S(1)}, u32[]{:S(2)}, u32[]{:S(2)}) %collective-permute-start.6) | collective-permute-done | bytes 233504 | tf_op jit(solution)/shard_map/ppermute | solution.py:435
  106.9 18.7 %all_to_all.15.recv_ref = bf16[8,152,128]{2,1,0:T(8,128)(2,1)S(1)} all-to-all(bf16[8,152,128]{2,1,0:T(8,128)(2,1)S(1)} %shard_map.143), channel_id=1, replica_groups=mesh['y'=4,'xl'=2,'core'=2,'wa'=8,'dp'=2] {'wa'}, dimensions={0} | all-to-all | bytes 622592 | tf_op jit(solution)/shard_map/all_to_all | solution.py:431
  125.6 2.2 %collective-permute-start.7 = (bf16[152,128]{1,0:T(8,128)(2,1)S(1)}, bf16[152,128]{1,0:T(8,128)(2,1)S(1)}, u32[]{:S(2)}, u32[]{:S(2)}) collective-permute-start(bf16[152,128]{1,0:T(8,128)(2,1)S(1)} %shard_map.145.own_ref), channel_id=1, source_target_pairs={{0,1},{1,0},{2,3},{3,2},{4,5},{5,4},{6,7},{7,6},{8,9},{9,8},{10,11... | collective-permute-start | bytes 116744 | tf_op jit(solution)/shard_map/ppermute | solution.py:435
  127.8 0.8 shard_map.144
  128.6 2.6 %collective-permute-done.7.other_ref = bf16[152,128]{1,0:T(8,128)(2,1)S(1)} collective-permute-done((bf16[152,128]{1,0:T(8,128)(2,1)S(1)}, bf16[152,128]{1,0:T(8,128)(2,1)S(1)}, u32[]{:S(2)}, u32[]{:S(2)}) %collective-permute-start.7) | collective-permute-done | bytes 38944 | tf_op jit(solution)/shard_map/ppermute | solution.py:435
  131.2 0.8 shard_map.146
  (23 shorter events, 1.0 us)
Async XLA Ops:
  0.6 16.2 %copy-start.4 = (f32[384]{0:T(512)S(1)}, f32[384]{0:T(512)}, u32[]{:S(2)}) copy-start(f32[384]{0:T(512)} %param.10) | copy-start | bytes 4612
  0.6 16.2 %copy-start.5 = (f32[384]{0:T(512)S(1)}, f32[384]{0:T(512)}, u32[]{:S(2)}) copy-start(f32[384]{0:T(512)} %param.11) | copy-start | bytes 4612
  0.7 39.9 %copy-start.2 = (bf16[1152,384]{1,0:T(8,128)(2,1)S(1)}, bf16[1152,384]{1,0:T(8,128)(2,1)}, u32[]{:S(2)}) copy-start(bf16[1152,384]{1,0:T(8,128)(2,1)} %w_qkv.3) | copy-start | bytes 2654212
  0.7 39.9 %copy-start.3 = (bf16[384,384]{1,0:T(8,128)(2,1)S(1)}, bf16[384,384]{1,0:T(8,128)(2,1)}, u32[]{:S(2)}) copy-start(bf16[384,384]{1,0:T(8,128)(2,1)} %w_proj.3) | copy-start | bytes 884740
  2.9 37.7 %all-to-all-start = ((bf16[128,8,384]{2,1,0:T(8,128)(2,1)}), bf16[128,8,384]{2,1,0:T(8,128)(2,1)S(1)}, u32[]{:S(2)}, u32[]{:S(2)}) async-start(bf16[128,8,384]{2,1,0:T(8,128)(2,1)} %shard_map.135), calls=%async_computation | async-start | bytes 1572864 | tf_op jit(solution)/shard_map/all_to_all | solution.py:431
  40.6 4.2 %copy-start = (bf16[1536,384]{1,0:T(8,128)(2,1)S(1)}, bf16[1536,384]{1,0:T(8,128)(2,1)}, u32[]{:S(2)}) copy-start(bf16[1536,384]{1,0:T(8,128)(2,1)} %w_up.1) | copy-start | bytes 3538948
  40.6 4.3 %copy-start.1 = (bf16[384,1536]{1,0:T(8,128)(2,1)S(1)}, bf16[384,1536]{1,0:T(8,128)(2,1)}, u32[]{:S(2)}) copy-start(bf16[384,1536]{1,0:T(8,128)(2,1)} %w_down.1) | copy-start | bytes 3538948
  51.6 10.4 %collective-permute-start = (bf16[8,192,384]{2,1,0:T(8,128)(2,1)S(1)}, bf16[8,192,384]{2,1,0:T(8,128)(2,1)S(1)}, u32[]{:S(2)}, u32[]{:S(2)}) collective-permute-start(bf16[8,192,384]{2,1,0:T(8,128)(2,1)S(1)} %get-tuple-element.45), channel_id=1, source_target_pairs={{0,16},{16,0},{1,17},{17,1},{2,18},{18,2},{3,19},{19,3},{4,20},{20... | collective-permute-start | bytes 3538952 | tf_op jit(solution)/shard_map/ppermute | solution.py:435
  59.7 2.4 %collective-permute-start.1 = (bf16[8,112,384]{2,1,0:T(8,128)(2,1)S(1)}, bf16[8,112,384]{2,1,0:T(8,128)(2,1)S(1)}, u32[]{:S(2)}, u32[]{:S(2)}) collective-permute-start(bf16[8,112,384]{2,1,0:T(8,128)(2,1)S(1)} %get-tuple-element.55), channel_id=1, source_target_pairs={{0,16},{16,0},{1,17},{17,1},{2,18},{18,2},{3,19},{19,3},{4,20},{20... | collective-permute-start | bytes 2064392 | tf_op jit(solution)/shard_map/ppermute | solution.py:435
  62.5 9.3 %collective-permute-start.2 = (bf16[304,384]{1,0:T(8,128)(2,1)S(1)}, bf16[304,384]{1,0:T(8,128)(2,1)S(1)}, u32[]{:S(2)}, u32[]{:S(2)}) collective-permute-start(bf16[304,384]{1,0:T(8,128)(2,1)S(1)} %get-tuple-element.60), channel_id=1, source_target_pairs={{0,64},{64,128},{128,192},{192,0},{1,65},{65,129},{129,193},{193,1... | collective-permute-start | bytes 700424 | tf_op jit(solution)/shard_map/ppermute | solution.py:439
  63.3 8.4 %collective-permute-start.3 = (bf16[304,384]{1,0:T(8,128)(2,1)S(1)}, bf16[304,384]{1,0:T(8,128)(2,1)S(1)}, u32[]{:S(2)}, u32[]{:S(2)}) collective-permute-start(bf16[304,384]{1,0:T(8,128)(2,1)S(1)} %get-tuple-element.61), channel_id=1, source_target_pairs={{0,192},{64,0},{128,64},{192,128},{1,193},{65,1},{129,65},{193,129... | collective-permute-start | bytes 700424 | tf_op jit(solution)/shard_map/ppermute | solution.py:439
  71.9 35.0 %all-to-all-start.1 = ((bf16[128,3,4,128]{3,2,1,0:T(4,128)(2,1)}), bf16[128,3,4,128]{3,2,1,0:T(4,128)(2,1)S(1)}, u32[]{:S(2)}, u32[]{:S(2)}) async-start(bf16[128,3,4,128]{3,2,1,0:T(4,128)(2,1)} %get-tuple-element.68), calls=%async_computation.1 | async-start | bytes 786432 | tf_op jit(solution)/shard_map/all_to_all | solution.py:431
  80.5 18.3 %collective-permute-start.4 = (bf16[2,304,384]{2,1,0:T(8,128)(2,1)S(1)}, bf16[2,304,384]{2,1,0:T(8,128)(2,1)S(1)}, u32[]{:S(2)}, u32[]{:S(2)}) collective-permute-start(bf16[2,304,384]{2,1,0:T(8,128)(2,1)S(1)} %get-tuple-element.64), channel_id=1, source_target_pairs={{0,64},{64,128},{128,192},{192,0},{1,65},{65,129},{129,193},{193,1... | collective-permute-start | bytes 1400840 | tf_op jit(solution)/shard_map/ppermute | solution.py:439
  82.3 16.6 %collective-permute-start.5 = (bf16[2,304,384]{2,1,0:T(8,128)(2,1)S(1)}, bf16[2,304,384]{2,1,0:T(8,128)(2,1)S(1)}, u32[]{:S(2)}, u32[]{:S(2)}) collective-permute-start(bf16[2,304,384]{2,1,0:T(8,128)(2,1)S(1)} %get-tuple-element.65), channel_id=1, source_target_pairs={{0,192},{64,0},{128,64},{192,128},{1,193},{65,1},{129,65},{193,129... | collective-permute-start | bytes 1400840 | tf_op jit(solution)/shard_map/ppermute | solution.py:439
  99.1 7.5 %collective-permute-start.6 = (bf16[304,384]{1,0:T(8,128)(2,1)S(1)}, bf16[304,384]{1,0:T(8,128)(2,1)S(1)}, u32[]{:S(2)}, u32[]{:S(2)}) collective-permute-start(bf16[304,384]{1,0:T(8,128)(2,1)S(1)} %get-tuple-element.67), channel_id=1, source_target_pairs={{0,32},{32,0},{1,33},{33,1},{2,34},{34,2},{3,35},{35,3},{4,36},{36... | collective-permute-start | bytes 700424 | tf_op jit(solution)/shard_map/ppermute | solution.py:435
  125.6 5.6 %collective-permute-start.7 = (bf16[152,128]{1,0:T(8,128)(2,1)S(1)}, bf16[152,128]{1,0:T(8,128)(2,1)S(1)}, u32[]{:S(2)}, u32[]{:S(2)}) collective-permute-start(bf16[152,128]{1,0:T(8,128)(2,1)S(1)} %shard_map.145.own_ref), channel_id=1, source_target_pairs={{0,1},{1,0},{2,3},{3,2},{4,5},{5,4},{6,7},{7,6},{8,9},{9,8},{10,11... | collective-permute-start | bytes 116744 | tf_op jit(solution)/shard_map/ppermute | solution.py:435

commit v5 on v4

--- a/solution.py
+++ b/solution.py
@@ -160,9 +160,9 @@
     mask = head_mask((QUAD * ROWS, 128))
     scale = 32.0 ** -0.5
 
-    @pl.loop(0, 4)
-    def _(pair):
-        units = unit_places(pair)
+    @pl.loop(0, 2)
+    def _(part):
+        units = unit_places(part)
         query = [spread(qkv_ref[rows, pl.ds(lane, 128)], mask) for rows, lane in units]
         probs = [
             probabilities(qkv_ref[rows, pl.ds(384 + lane, 128)], query[n], scale).astype(BF16)
@@ -181,10 +181,10 @@
         resid_ref[rows, :] = (x_ref[rows, :].astype(F32) + branch.astype(F32)).astype(BF16)
 
 
-def unit_places(pair):
+def unit_places(part):
     places = []
-    for half in range(2):
-        rows = pl.ds(pl.multiple_of(pair * 2 * ROWS + half * ROWS, ROWS), ROWS)
+    for group in range(4):
+        rows = pl.ds(pl.multiple_of((part * 4 + group) * ROWS, ROWS), ROWS)
         places.extend((rows, quad * 128) for quad in range(3))
     return places
 
@@ -243,9 +243,9 @@
     mask = head_mask((QUAD * ROWS, 128))
     scale = 32.0 ** -0.5
 
-    @pl.loop(0, 4)
-    def _(pair):
-        units = unit_places(pair)
+    @pl.loop(0, 2)
+    def _(part):
+        units = unit_places(part)
         count = range(len(units))
         query = [spread(qkv_ref[rows, pl.ds(lane, 128)], mask) for rows, lane in units]
         grad = [spread(grad_mixed[rows, pl.ds(lane, 128)], mask) for rows, lane in units]
@@ -476,6 +476,7 @@
         [rows, ((SLOTS * 12, 128), F32)],
         flops=6 * 10**9, nbytes=20 * 10**6,
     )(x, qkv, resid_grad, gain_one, w_qkv, w_proj)
+    returned = exchange(slots, HA + ("wa",))
     late_keep, late_send = call(
         weight_kernel,
         [((8, 112, 384), BF16), ((8, 112, 384), BF16)],
@@ -489,8 +490,6 @@
     near, back = call(ring_kernel, [whole, whole], nbytes=4 * 10**6)(
         near, back, shift(low, 1), shift(high, 3)
     )
-    slots, near, back = lax.optimization_barrier((slots, near, back))
-    returned = exchange(slots, HA + ("wa",))
     keep, send = call(row_kernel, [half, half], [((4, 16, 384), F32)], nbytes=3 * 10**6)(
         own, shift(near, 1), shift(back, 3)
     )

time: 132 us -> 124 us (0.939)
  waiting for transfers between devices: 55.6 us -> 49.6 us
  Pallas kernels: 23.8 us -> 22.3 us
    ppermute x4, waiting for transfers between devices: 20.8 us -> 14.8 us  [shift(): lax.ppermute(values, 'y', [(place, (place + step) % 4) for place in range...]
    pallas_call x12, Pallas kernels: 23.8 us -> 22.3 us  [run(): pl.pallas_call(kernel, out_shape=[jax.ShapeDtypeStruct(shape, dtype) for...]
  transfers between devices with their start and end apart: 10 -> 10, of which waited for: 6 -> 5; matrix products, arithmetic and copies ran while one was open for 0% -> 0% of each run, Pallas kernels for 7% -> 7%
where the time goes in v5:
time: 124 us; the launch traced here: 123 us
  waiting for transfers between devices  49.6 us (40%)
  starting transfers between devices  32.1 us (26%)
  Pallas kernels  22.3 us (18%)
  blocking collectives  18.6 us (15%)
    all_to_all x2, waiting for transfers between devices, exchange(): return lax.all_to_all(values, axes, split_axis=0, concat_axis=0, tiled=True)  23.7 us
    pallas_call x12, Pallas kernels, run(): pl.pallas_call(kernel, out_shape=[jax.ShapeDtypeStruct(shape, dtype) for...  22.3 us
    all_to_all x2, starting transfers between devices, exchange(): return lax.all_to_all(values, axes, split_axis=0, concat_axis=0, tiled=True)  21.4 us
    all_to_all x1, blocking collectives, exchange(): return lax.all_to_all(values, axes, split_axis=0, concat_axis=0, tiled=True)  18.6 us
    ppermute x4, waiting for transfers between devices, shift(): lax.ppermute(values, 'y', [(place, (place + step) % 4) for place in range...  14.8 us
    ppermute x4, waiting for transfers between devices, swap(): return lax.ppermute(values, axis, [(0, 1), (1, 0)])  11.1 us
    ppermute x4, starting transfers between devices, shift(): lax.ppermute(values, 'y', [(place, (place + step) % 4) for place in range...  6.83 us
    ppermute x4, starting transfers between devices, swap(): return lax.ppermute(values, axis, [(0, 1), (1, 0)])  3.79 us
  transfers between devices with their start and end apart: 10, of which 5 were waited for; matrix products, arithmetic and copies ran while one was open for 0% of the time, Pallas kernels for 7%

profile of v5, /device:TPU:2, one launch (start us, length us, event | category | flops | bytes accessed | tf_op | source)
XLA Modules:
  0.0 123.4 jit_solution(12380785568478071372)
XLA Ops:
  0.7 2.2 %shard_map.135 = bf16[128,8,384]{2,1,0:T(8,128)(2,1)} custom-call(bf16[14,7,4,384]{3,2,1,0:T(4,128)(2,1)} %bitcast.7, bf16[14,7,4,384]{3,2,1,0:T(4,128)(2,1)} %bitcast.8), custom_call_target="tpu_custom_call" | custom-call | bytes 2000000 | tf_op jit(solution)/shard_map/pallas_call | solution.py:417
  2.9 13.9 %all-to-all-start = ((bf16[128,8,384]{2,1,0:T(8,128)(2,1)}), bf16[128,8,384]{2,1,0:T(8,128)(2,1)S(1)}, u32[]{:S(2)}, u32[]{:S(2)}) async-start(bf16[128,8,384]{2,1,0:T(8,128)(2,1)} %shard_map.135), calls=%async_computation | async-start | bytes 1572864 | tf_op jit(solution)/shard_map/all_to_all | solution.py:431
  16.9 23.7 %all-to-all-done = bf16[128,8,384]{2,1,0:T(8,128)(2,1)S(1)} async-done(((bf16[128,8,384]{2,1,0:T(8,128)(2,1)}), bf16[128,8,384]{2,1,0:T(8,128)(2,1)S(1)}, u32[]{:S(2)}, u32[]{:S(2)}) %all-to-all-start) | async-done | bytes 786464 | tf_op jit(solution)/shard_map/all_to_all | solution.py:431
  40.6 3.5 %shard_map.136 = (bf16[512,384]{1,0:T(8,128)(2,1)S(1)}, bf16[512,1152]{1,0:T(8,128)(2,1)S(1)}, bf16[512,384]{1,0:T(8,128)(2,1)S(1)}, bf16[512,384]{1,0:T(8,128)(2,1)S(1)}, bf16[512,384]{1,0:T(8,128)(2,1)S(1)}) custom-call(bf16[1024,384]{1,0:T(8,128)(2,1)S(1)} %bitcast.6, f32[1,384]{1,0:T(1,128)S(1)} %reshape.24.gain_one, bf16[1152,384]{1,0:T(8,128)(2,1)S(1)} %copy-done.2, ...), custom_call_target="tpu_custom_call" | custom-call | flops 1000000000 | bytes 4000000 | tf_op jit(solution)/shard_map/pallas_call | solution.py:417
  44.1 6.8 %shard_map.137 = (bf16[512,384]{1,0:T(8,128)(2,1)S(1)}, bf16[8,192,384]{2,1,0:T(8,128)(2,1)S(1)}, bf16[8,192,384]{2,1,0:T(8,128)(2,1)S(1)}, f32[1,384]{1,0:T(1,128)S(1)}) custom-call(bf16[512,384]{1,0:T(8,128)(2,1)S(1)} %get-tuple-element.39.grad_out, bf16[512,384]{1,0:T(8,128)(2,1)S(1)} %get-tuple-element.40.resid, f32[1,384]{1,0:T(1,128)S(1)} %reshape.25.gain_two, ...), custom_call_target="tpu_custom_call" | custom-call | flops 3000000000 | bytes 6000000 | tf_op jit(solution)/shard_map/pallas_call | solution.py:417
  51.1 5.5 %shard_map.138 = (bf16[128,3,4,128]{3,2,1,0:T(4,128)(2,1)}, bf16[512,1152]{1,0:T(8,128)(2,1)S(1)}, bf16[512,384]{1,0:T(8,128)(2,1)S(1)}, f32[1,384]{1,0:T(1,128)S(1)}) custom-call(bf16[512,384]{1,0:T(8,128)(2,1)S(1)} %get-tuple-element.43.x_ref, bf16[512,1152]{1,0:T(8,128)(2,1)S(1)} %get-tuple-element.44.qkv_ref, ...), custom_call_target="tpu_custom_call" | custom-call | flops 6000000000 | bytes 20000000 | tf_op jit(solution)/shard_map/pallas_call | solution.py:417
  56.6 1.6 %shard_map.139 = (bf16[8,112,384]{2,1,0:T(8,128)(2,1)S(1)}, bf16[8,112,384]{2,1,0:T(8,128)(2,1)S(1)}) custom-call(bf16[512,1152]{1,0:T(8,128)(2,1)S(1)} %get-tuple-element.46.rows_grad, bf16[512,384]{1,0:T(8,128)(2,1)S(1)} %get-tuple-element.47.normed, bf16[512,384]{1,0:T(8,128)(2,1)S(1)} %get-tuple-element.45.resid_grad_ref.resid_grad, ...), custom_call_target="tpu_custom_call" | custom-call | flops 1000000000 | bytes 5000000 | tf_op jit(solution)/shard_map/pallas_call | solution.py:417
  58.2 0.6 collective-permute-start.1
  58.8 1.8 %collective-permute-done.1.late_recv = bf16[8,112,384]{2,1,0:T(8,128)(2,1)S(1)} collective-permute-done((bf16[8,112,384]{2,1,0:T(8,128)(2,1)S(1)}, bf16[8,112,384]{2,1,0:T(8,128)(2,1)S(1)}, u32[]{:S(2)}, u32[]{:S(2)}) %collective-permute-start.1) | collective-permute-done | bytes 688160 | tf_op jit(solution)/shard_map/ppermute | solution.py:435
  60.6 0.5 shard_map.140
  61.0 0.8 collective-permute-start.2
  61.9 2.5 %collective-permute-start.3 = (bf16[304,384]{1,0:T(8,128)(2,1)S(1)}, bf16[304,384]{1,0:T(8,128)(2,1)S(1)}, u32[]{:S(2)}, u32[]{:S(2)}) collective-permute-start(bf16[304,384]{1,0:T(8,128)(2,1)S(1)} %get-tuple-element.57), channel_id=1, source_target_pairs={{0,192},{64,0},{128,64},{192,128},{1,193},{65,1},{129,65},{193,129... | collective-permute-start | bytes 700424 | tf_op jit(solution)/shard_map/ppermute | solution.py:439
  64.4 7.5 %all-to-all-start.1 = ((bf16[128,3,4,128]{3,2,1,0:T(4,128)(2,1)}), bf16[128,3,4,128]{3,2,1,0:T(4,128)(2,1)S(1)}, u32[]{:S(2)}, u32[]{:S(2)}) async-start(bf16[128,3,4,128]{3,2,1,0:T(4,128)(2,1)} %get-tuple-element.62), calls=%async_computation.1 | async-start | bytes 786432 | tf_op jit(solution)/shard_map/all_to_all | solution.py:431
  72.1 1.8 %collective-permute-start.4 = (bf16[2,304,384]{2,1,0:T(8,128)(2,1)S(1)}, bf16[2,304,384]{2,1,0:T(8,128)(2,1)S(1)}, u32[]{:S(2)}, u32[]{:S(2)}) collective-permute-start(bf16[2,304,384]{2,1,0:T(8,128)(2,1)S(1)} %get-tuple-element.58), channel_id=1, source_target_pairs={{0,64},{64,128},{128,192},{192,0},{1,65},{65,129},{129,193},{193,1... | collective-permute-start | bytes 1400840 | tf_op jit(solution)/shard_map/ppermute | solution.py:439
  73.8 1.7 %collective-permute-start.5 = (bf16[2,304,384]{2,1,0:T(8,128)(2,1)S(1)}, bf16[2,304,384]{2,1,0:T(8,128)(2,1)S(1)}, u32[]{:S(2)}, u32[]{:S(2)}) collective-permute-start(bf16[2,304,384]{2,1,0:T(8,128)(2,1)S(1)} %get-tuple-element.59), channel_id=1, source_target_pairs={{0,192},{64,0},{128,64},{192,128},{1,193},{65,1},{129,65},{193,129... | collective-permute-start | bytes 1400840 | tf_op jit(solution)/shard_map/ppermute | solution.py:439
  75.6 14.8 %collective-permute-done.4.near = bf16[2,304,384]{2,1,0:T(8,128)(2,1)S(1)} collective-permute-done((bf16[2,304,384]{2,1,0:T(8,128)(2,1)S(1)}, bf16[2,304,384]{2,1,0:T(8,128)(2,1)S(1)}, u32[]{:S(2)}, u32[]{:S(2)}) %collective-permute-start.4) | collective-permute-done | bytes 466976 | tf_op jit(solution)/shard_map/ppermute | solution.py:439
  90.3 0.3 shard_map.142
  90.6 0.7 collective-permute-start.6
  91.4 6.8 %collective-permute-done.6.recv_ref = bf16[304,384]{1,0:T(8,128)(2,1)S(1)} collective-permute-done((bf16[304,384]{1,0:T(8,128)(2,1)S(1)}, bf16[304,384]{1,0:T(8,128)(2,1)S(1)}, u32[]{:S(2)}, u32[]{:S(2)}) %collective-permute-start.6) | collective-permute-done | bytes 233504 | tf_op jit(solution)/shard_map/ppermute | solution.py:435
  98.4 18.6 %all_to_all.15.recv_ref = bf16[8,152,128]{2,1,0:T(8,128)(2,1)S(1)} all-to-all(bf16[8,152,128]{2,1,0:T(8,128)(2,1)S(1)} %shard_map.143), channel_id=1, replica_groups=mesh['y'=4,'xl'=2,'core'=2,'wa'=8,'dp'=2] {'wa'}, dimensions={0} | all-to-all | bytes 622592 | tf_op jit(solution)/shard_map/all_to_all | solution.py:431
  117.1 2.2 %collective-permute-start.7 = (bf16[152,128]{1,0:T(8,128)(2,1)S(1)}, bf16[152,128]{1,0:T(8,128)(2,1)S(1)}, u32[]{:S(2)}, u32[]{:S(2)}) collective-permute-start(bf16[152,128]{1,0:T(8,128)(2,1)S(1)} %shard_map.145.own_ref), channel_id=1, source_target_pairs={{0,1},{1,0},{2,3},{3,2},{4,5},{5,4},{6,7},{7,6},{8,9},{9,8},{10,11... | collective-permute-start | bytes 116744 | tf_op jit(solution)/shard_map/ppermute | solution.py:435
  119.2 0.8 shard_map.144
  120.0 2.6 %collective-permute-done.7.other_ref = bf16[152,128]{1,0:T(8,128)(2,1)S(1)} collective-permute-done((bf16[152,128]{1,0:T(8,128)(2,1)S(1)}, bf16[152,128]{1,0:T(8,128)(2,1)S(1)}, u32[]{:S(2)}, u32[]{:S(2)}) %collective-permute-start.7) | collective-permute-done | bytes 38944 | tf_op jit(solution)/shard_map/ppermute | solution.py:435
  122.6 0.8 shard_map.146
  (23 shorter events, 0.8 us)
Async XLA Ops:
  0.6 16.2 %copy-start.4 = (f32[384]{0:T(512)S(1)}, f32[384]{0:T(512)}, u32[]{:S(2)}) copy-start(f32[384]{0:T(512)} %param.10) | copy-start | bytes 4612
  0.6 16.2 %copy-start.5 = (f32[384]{0:T(512)S(1)}, f32[384]{0:T(512)}, u32[]{:S(2)}) copy-start(f32[384]{0:T(512)} %param.11) | copy-start | bytes 4612
  0.7 39.9 %copy-start.2 = (bf16[1152,384]{1,0:T(8,128)(2,1)S(1)}, bf16[1152,384]{1,0:T(8,128)(2,1)}, u32[]{:S(2)}) copy-start(bf16[1152,384]{1,0:T(8,128)(2,1)} %w_qkv.3) | copy-start | bytes 2654212
  0.7 39.9 %copy-start.3 = (bf16[384,384]{1,0:T(8,128)(2,1)S(1)}, bf16[384,384]{1,0:T(8,128)(2,1)}, u32[]{:S(2)}) copy-start(bf16[384,384]{1,0:T(8,128)(2,1)} %w_proj.3) | copy-start | bytes 884740
  2.9 37.7 %all-to-all-start = ((bf16[128,8,384]{2,1,0:T(8,128)(2,1)}), bf16[128,8,384]{2,1,0:T(8,128)(2,1)S(1)}, u32[]{:S(2)}, u32[]{:S(2)}) async-start(bf16[128,8,384]{2,1,0:T(8,128)(2,1)} %shard_map.135), calls=%async_computation | async-start | bytes 1572864 | tf_op jit(solution)/shard_map/all_to_all | solution.py:431
  40.6 3.5 %copy-start = (bf16[1536,384]{1,0:T(8,128)(2,1)S(1)}, bf16[1536,384]{1,0:T(8,128)(2,1)}, u32[]{:S(2)}) copy-start(bf16[1536,384]{1,0:T(8,128)(2,1)} %w_up.1) | copy-start | bytes 3538948
  40.6 3.5 %copy-start.1 = (bf16[384,1536]{1,0:T(8,128)(2,1)S(1)}, bf16[384,1536]{1,0:T(8,128)(2,1)}, u32[]{:S(2)}) copy-start(bf16[384,1536]{1,0:T(8,128)(2,1)} %w_down.1) | copy-start | bytes 3538948
  50.9 9.7 %collective-permute-start = (bf16[8,192,384]{2,1,0:T(8,128)(2,1)S(1)}, bf16[8,192,384]{2,1,0:T(8,128)(2,1)S(1)}, u32[]{:S(2)}, u32[]{:S(2)}) collective-permute-start(bf16[8,192,384]{2,1,0:T(8,128)(2,1)S(1)} %get-tuple-element.42), channel_id=1, source_target_pairs={{0,16},{16,0},{1,17},{17,1},{2,18},{18,2},{3,19},{19,3},{4,20},{20... | collective-permute-start | bytes 3538952 | tf_op jit(solution)/shard_map/ppermute | solution.py:435
  58.2 2.4 %collective-permute-start.1 = (bf16[8,112,384]{2,1,0:T(8,128)(2,1)S(1)}, bf16[8,112,384]{2,1,0:T(8,128)(2,1)S(1)}, u32[]{:S(2)}, u32[]{:S(2)}) collective-permute-start(bf16[8,112,384]{2,1,0:T(8,128)(2,1)S(1)} %get-tuple-element.52), channel_id=1, source_target_pairs={{0,16},{16,0},{1,17},{17,1},{2,18},{18,2},{3,19},{19,3},{4,20},{20... | collective-permute-start | bytes 2064392 | tf_op jit(solution)/shard_map/ppermute | solution.py:435
  61.0 10.9 %collective-permute-start.2 = (bf16[304,384]{1,0:T(8,128)(2,1)S(1)}, bf16[304,384]{1,0:T(8,128)(2,1)S(1)}, u32[]{:S(2)}, u32[]{:S(2)}) collective-permute-start(bf16[304,384]{1,0:T(8,128)(2,1)S(1)} %get-tuple-element.56), channel_id=1, source_target_pairs={{0,64},{64,128},{128,192},{192,0},{1,65},{65,129},{129,193},{193,1... | collective-permute-start | bytes 700424 | tf_op jit(solution)/shard_map/ppermute | solution.py:439
  61.9 10.0 %collective-permute-start.3 = (bf16[304,384]{1,0:T(8,128)(2,1)S(1)}, bf16[304,384]{1,0:T(8,128)(2,1)S(1)}, u32[]{:S(2)}, u32[]{:S(2)}) collective-permute-start(bf16[304,384]{1,0:T(8,128)(2,1)S(1)} %get-tuple-element.57), channel_id=1, source_target_pairs={{0,192},{64,0},{128,64},{192,128},{1,193},{65,1},{129,65},{193,129... | collective-permute-start | bytes 700424 | tf_op jit(solution)/shard_map/ppermute | solution.py:439
  64.4 34.0 %all-to-all-start.1 = ((bf16[128,3,4,128]{3,2,1,0:T(4,128)(2,1)}), bf16[128,3,4,128]{3,2,1,0:T(4,128)(2,1)S(1)}, u32[]{:S(2)}, u32[]{:S(2)}) async-start(bf16[128,3,4,128]{3,2,1,0:T(4,128)(2,1)} %get-tuple-element.62), calls=%async_computation.1 | async-start | bytes 786432 | tf_op jit(solution)/shard_map/all_to_all | solution.py:431
  72.1 18.3 %collective-permute-start.4 = (bf16[2,304,384]{2,1,0:T(8,128)(2,1)S(1)}, bf16[2,304,384]{2,1,0:T(8,128)(2,1)S(1)}, u32[]{:S(2)}, u32[]{:S(2)}) collective-permute-start(bf16[2,304,384]{2,1,0:T(8,128)(2,1)S(1)} %get-tuple-element.58), channel_id=1, source_target_pairs={{0,64},{64,128},{128,192},{192,0},{1,65},{65,129},{129,193},{193,1... | collective-permute-start | bytes 1400840 | tf_op jit(solution)/shard_map/ppermute | solution.py:439
  73.8 16.5 %collective-permute-start.5 = (bf16[2,304,384]{2,1,0:T(8,128)(2,1)S(1)}, bf16[2,304,384]{2,1,0:T(8,128)(2,1)S(1)}, u32[]{:S(2)}, u32[]{:S(2)}) collective-permute-start(bf16[2,304,384]{2,1,0:T(8,128)(2,1)S(1)} %get-tuple-element.59), channel_id=1, source_target_pairs={{0,192},{64,0},{128,64},{192,128},{1,193},{65,1},{129,65},{193,129... | collective-permute-start | bytes 1400840 | tf_op jit(solution)/shard_map/ppermute | solution.py:439
  90.6 7.5 %collective-permute-start.6 = (bf16[304,384]{1,0:T(8,128)(2,1)S(1)}, bf16[304,384]{1,0:T(8,128)(2,1)S(1)}, u32[]{:S(2)}, u32[]{:S(2)}) collective-permute-start(bf16[304,384]{1,0:T(8,128)(2,1)S(1)} %get-tuple-element.61), channel_id=1, source_target_pairs={{0,32},{32,0},{1,33},{33,1},{2,34},{34,2},{3,35},{35,3},{4,36},{36... | collective-permute-start | bytes 700424 | tf_op jit(solution)/shard_map/ppermute | solution.py:435
  117.1 5.6 %collective-permute-start.7 = (bf16[152,128]{1,0:T(8,128)(2,1)S(1)}, bf16[152,128]{1,0:T(8,128)(2,1)S(1)}, u32[]{:S(2)}, u32[]{:S(2)}) collective-permute-start(bf16[152,128]{1,0:T(8,128)(2,1)S(1)} %shard_map.145.own_ref), channel_id=1, source_target_pairs={{0,1},{1,0},{2,3},{3,2},{4,5},{5,4},{6,7},{7,6},{8,9},{9,8},{10,11... | collective-permute-start | bytes 116744 | tf_op jit(solution)/shard_map/ppermute | solution.py:435

commit v6 on v5

--- a/solution.py
+++ b/solution.py
@@ -160,9 +160,9 @@
     mask = head_mask((QUAD * ROWS, 128))
     scale = 32.0 ** -0.5
 
-    @pl.loop(0, 2)
+    @pl.loop(0, 1)
     def _(part):
-        units = unit_places(part)
+        units = unit_places()
         query = [spread(qkv_ref[rows, pl.ds(lane, 128)], mask) for rows, lane in units]
         probs = [
             probabilities(qkv_ref[rows, pl.ds(384 + lane, 128)], query[n], scale).astype(BF16)
@@ -181,18 +181,14 @@
         resid_ref[rows, :] = (x_ref[rows, :].astype(F32) + branch.astype(F32)).astype(BF16)
 
 
-def unit_places(part):
-    places = []
-    for group in range(4):
-        rows = pl.ds(pl.multiple_of((part * 4 + group) * ROWS, ROWS), ROWS)
-        places.extend((rows, quad * 128) for quad in range(3))
-    return places
+def unit_places():
+    return [(pl.ds(group * ROWS, ROWS), quad * 128) for group in range(8) for quad in range(3)]
 
 
 def mlp_kernel(
     grad_out, resid, gain_two, w_up, w_down,
     resid_grad_ref, keep_ref, send_ref, gain_ref,
-    normed, hidden_grad, grad_turned, up_total, down_total, back, piece_rows,
+    normed, hidden_grad, grad_turned, up_total, down_total, back,
 ):
     for crop in range(4):
         rows = pl.ds(crop * SLOTS, SLOTS)
@@ -212,12 +208,11 @@
     for ref, side in piece_sides(keep_ref, send_ref):
         for piece in range(8):
             owner = 2 * piece + side
-            piece_rows[:96, :] = up_total[pl.ds(pl.multiple_of(owner * 96, 8), 96), :]
-            for part in range(4):
-                piece_rows[96 + 24 * part : 120 + 24 * part, :] = down_total[
-                    pl.ds(pl.multiple_of(owner * 24, 8), 24), part * 384 : (part + 1) * 384
-                ]
-            ref[piece] = piece_rows[...].astype(BF16)
+            ref[piece, :96] = up_total[pl.ds(pl.multiple_of(owner * 96, 8), 96), :].astype(BF16)
+            rows = pl.ds(pl.multiple_of(owner * 24, 8), 24)
+            ref[piece, 96:] = jnp.concatenate(
+                [down_total[rows, part * 384 : (part + 1) * 384] for part in range(4)], axis=0
+            ).astype(BF16)
     gain = jnp.zeros((1, 384), F32)
     for crop in range(4):
         rows = pl.ds(crop * SLOTS, SLOTS)
@@ -243,9 +238,9 @@
     mask = head_mask((QUAD * ROWS, 128))
     scale = 32.0 ** -0.5
 
-    @pl.loop(0, 2)
+    @pl.loop(0, 1)
     def _(part):
-        units = unit_places(part)
+        units = unit_places()
         count = range(len(units))
         query = [spread(qkv_ref[rows, pl.ds(lane, 128)], mask) for rows, lane in units]
         grad = [spread(grad_mixed[rows, pl.ds(lane, 128)], mask) for rows, lane in units]
@@ -308,46 +303,33 @@
             ref[piece] = piece_rows[...].astype(BF16)
 
 
-def core_kernel(
-    early_keep, early_recv, late_keep, late_recv, own, near, back, far_low, far_high,
+def core_kernel(keep_ref, recv_ref, out_keep, out_send):
+    row, col = lax.axis_index("y"), lax.axis_index("xl")
+    for ref, side in ((out_keep, col), (out_send, 1 - col)):
+        for step in range(4):
+            piece = ((row + step) & 3) * 2 + side
+            ref[step] = (keep_ref[piece].astype(F32) + recv_ref[piece].astype(F32)).astype(BF16)
+
+
+def side_kernel(
+    early_keep, early_recv, late_keep, late_recv, own, near, back, far_early, far_late,
 ):
-    row = lax.axis_index("y")
-
-    def put(ref, step, col):
-        piece = ((row + step) & 3) * 2 + col
-        early = early_keep[piece].astype(F32) + early_recv[piece].astype(F32)
-        late = late_keep[piece].astype(F32) + late_recv[piece].astype(F32)
+    for step, ref in ((0, own), (1, near), (3, back)):
+        early = early_keep[step].astype(F32) + early_recv[step].astype(F32)
+        late = late_keep[step].astype(F32) + late_recv[step].astype(F32)
         ref[:192] = early.astype(BF16)
-        if step == 2:
-            late = jnp.concatenate([late[:96], pltpu.roll(late[96:], 2, 0)], axis=0)
         ref[192:] = late.astype(BF16)
-
-    for ref, step in ((own, 0), (near, 1), (back, 3)):
-        for col in range(2):
-            put(ref.at[col], step, col)
-    put(far_low, 2, 0)
-    put(far_high, 2, 1)
-
-
-def ring_kernel(near, back, far_low, far_high, out_near, out_back):
-    out_near[0] = (near[0].astype(F32) + far_low[...].astype(F32)).astype(BF16)
-    out_near[1] = near[1]
-    out_back[0] = back[0]
-    out_back[1] = (back[1].astype(F32) + far_high[...].astype(F32)).astype(BF16)
-
-
-def row_kernel(own, near, back, keep_ref, send_ref, gains):
-    row, col = lax.axis_index("y"), lax.axis_index("xl")
-    first, second, third = (ref[0, 288:].astype(F32) for ref in (own, near, back))
-    gains[row] = first
-    gains[(row + 3) & 3] = second
-    gains[(row + 1) & 3] = third
-    gains[(row + 2) & 3] = pltpu.roll(second, 14, 0)
-    gain = ((gains[0] + gains[1]) + (gains[2] + gains[3])).astype(BF16)
-    for ref, side in ((keep_ref, col), (send_ref, 1 - col)):
-        total = own[side, :288].astype(F32) + near[side, :288].astype(F32)
-        ref[:288] = (total + back[side, :288].astype(F32)).astype(BF16)
-        ref[288:] = gain
+    far_early[...] = (early_keep[2].astype(F32) + early_recv[2].astype(F32)).astype(BF16)
+    late = late_keep[2].astype(F32) + late_recv[2].astype(F32)
+    far_late[:96] = late[:96].astype(BF16)
+    far_late[96:] = pltpu.roll(late[96:], 2, 0).astype(BF16)
+
+
+def ring_kernel(near, back, far_early, far_late, out_near, out_back):
+    out_near[:192] = (near[:192].astype(F32) + far_early[...].astype(F32)).astype(BF16)
+    out_near[192:] = near[192:]
+    out_back[:192] = back[:192]
+    out_back[192:] = (back[192:].astype(F32) + far_late[...].astype(F32)).astype(BF16)
 
 
 def pack_columns(rows, col):
@@ -356,10 +338,17 @@
     return jnp.where(iota((48, 128), 1) < 64, low, high)
 
 
-def pack_kernel(keep_ref, recv_ref, out_ref):
-    total = keep_ref[...].astype(F32) + recv_ref[...].astype(F32)
+def pack_kernel(own, near, back, out_ref, gains):
+    row = lax.axis_index("y")
+    first, second, third = (ref[288:].astype(F32) for ref in (own, near, back))
+    gains[row] = first
+    gains[(row + 3) & 3] = second
+    gains[(row + 1) & 3] = third
+    gains[(row + 2) & 3] = pltpu.roll(third, 14, 0)
+    gain = (gains[0] + gains[1]) + (gains[2] + gains[3])
+    total = own[:288].astype(F32) + near[:288].astype(F32) + back[:288].astype(F32)
     gain_rows = [
-        total[288 + which : 289 + which, part * 128 : (part + 1) * 128]
+        gain[which : which + 1, part * 128 : (part + 1) * 128]
         for which in range(2)
         for part in range(3)
     ]
@@ -433,6 +422,11 @@
 
 def swap(values, axis):
     return lax.ppermute(values, axis, [(0, 1), (1, 0)])
+
+
+def side_pieces(keep, recv):
+    half = ((4, keep.shape[1], 384), BF16)
+    return call(core_kernel, [half, half], nbytes=4 * 10**6)(keep, recv)
 
 
 def shift(values, step):
@@ -466,7 +460,7 @@
         [rows, ((8, 192, 384), BF16), ((8, 192, 384), BF16), ((1, 384), F32)],
         [
             rows, ((512, 1536), BF16), ((384, 512), BF16), ((1536, 384), F32), ((384, 1536), F32),
-            ((512, 384), F32), ((192, 384), F32),
+            ((512, 384), F32),
         ],
         flops=3 * 10**9, nbytes=6 * 10**6,
     )(grad_rows, resid, gain_two, w_up, w_down)
@@ -477,23 +471,27 @@
         flops=6 * 10**9, nbytes=20 * 10**6,
     )(x, qkv, resid_grad, gain_one, w_qkv, w_proj)
     returned = exchange(slots, HA + ("wa",))
+    early = side_pieces(early_keep, swap(early_send, "core"))
+    rows_grad, *early = lax.optimization_barrier((rows_grad, *early))
     late_keep, late_send = call(
         weight_kernel,
         [((8, 112, 384), BF16), ((8, 112, 384), BF16)],
         [((1152, 384), F32), ((384, 384), F32), ((112, 384), F32)],
         flops=10**9, nbytes=5 * 10**6,
     )(rows_grad, normed, resid_grad, mixed, gain_sum_one, gain_sum_two)
-    whole, half = ((2, 304, 384), BF16), ((304, 384), BF16)
-    own, near, back, low, high = call(core_kernel, [whole, whole, whole, half, half], nbytes=10**7)(
-        early_keep, swap(early_send, "core"), late_keep, swap(late_send, "core")
+    late = side_pieces(late_keep, swap(late_send, "core"))
+    piece = ((304, 384), BF16)
+    own, near, back, far_early, far_late = call(
+        side_kernel,
+        [piece, piece, piece, ((192, 384), BF16), ((112, 384), BF16)],
+        nbytes=5 * 10**6,
+    )(early[0], swap(early[1], "xl"), late[0], swap(late[1], "xl"))
+    near, back = call(ring_kernel, [piece, piece], nbytes=2 * 10**6)(
+        near, back, shift(far_early, 1), shift(far_late, 3)
     )
-    near, back = call(ring_kernel, [whole, whole], nbytes=4 * 10**6)(
-        near, back, shift(low, 1), shift(high, 3)
-    )
-    keep, send = call(row_kernel, [half, half], [((4, 16, 384), F32)], nbytes=3 * 10**6)(
-        own, shift(near, 1), shift(back, 3)
-    )
-    (blocks,) = call(pack_kernel, [((8, 152, 128), BF16)], nbytes=10**6)(keep, swap(send, "xl"))
+    (blocks,) = call(
+        pack_kernel, [((8, 152, 128), BF16)], [((4, 16, 384), F32)], nbytes=10**6
+    )(own, shift(near, 1), shift(back, 3))
     blocks, returned = lax.optimization_barrier((blocks, returned))
     (total,) = call(block_sum, [((152, 128), BF16)], nbytes=10**6)(exchange(blocks, "wa"))
     other = swap(total, "dp")

time: 124 us -> 122 us (0.984)
  blocking collectives: 18.6 us -> 13.7 us
  waiting for transfers between devices: 49.6 us -> 51.8 us
    ppermute x4 -> x5, waiting for transfers between devices: 11.1 us -> 20.8 us  [swap(): return lax.ppermute(values, axis, [(0, 1), (1, 0)])]
    ppermute x4, waiting for transfers between devices: 14.8 us -> 7.31 us  [shift(): lax.ppermute(values, 'y', [(place, (place + step) % 4) for place in range...]
    all_to_all x1, blocking collectives: 18.6 us -> 13.7 us  [exchange(): return lax.all_to_all(values, axes, split_axis=0, concat_axis=0, tiled=True)]
    ppermute x4 -> x5, starting transfers between devices: 3.79 us -> 6.21 us  [swap(): return lax.ppermute(values, axis, [(0, 1), (1, 0)])]
    all_to_all x2, starting transfers between devices: 21.4 us -> 19.6 us  [exchange(): return lax.all_to_all(values, axes, split_axis=0, concat_axis=0, tiled=True)]
    pallas_call x12 -> x13, Pallas kernels: 22.3 us -> 22.1 us  [run(): pl.pallas_call(kernel, out_shape=[jax.ShapeDtypeStruct(shape, dtype) for...]
  transfers between devices with their start and end apart: 10 -> 11, of which waited for: 5 -> 7; matrix products, arithmetic and copies ran while one was open for 0% -> 0% of each run, Pallas kernels for 7% -> 6%
where the time goes in v6:
time: 122 us; the launch traced here: 121 us
  waiting for transfers between devices  51.8 us (42%)
  starting transfers between devices  32.4 us (27%)
  Pallas kernels  22.1 us (18%)
  blocking collectives  13.7 us (11%)
    all_to_all x2, waiting for transfers between devices, exchange(): return lax.all_to_all(values, axes, split_axis=0, concat_axis=0, tiled=True)  23.7 us
    pallas_call x13, Pallas kernels, run(): pl.pallas_call(kernel, out_shape=[jax.ShapeDtypeStruct(shape, dtype) for...  22.1 us
    ppermute x5, waiting for transfers between devices, swap(): return lax.ppermute(values, axis, [(0, 1), (1, 0)])  20.8 us
    all_to_all x2, starting transfers between devices, exchange(): return lax.all_to_all(values, axes, split_axis=0, concat_axis=0, tiled=True)  19.6 us
    all_to_all x1, blocking collectives, exchange(): return lax.all_to_all(values, axes, split_axis=0, concat_axis=0, tiled=True)  13.7 us
    ppermute x4, waiting for transfers between devices, shift(): lax.ppermute(values, 'y', [(place, (place + step) % 4) for place in range...  7.31 us
    ppermute x4, starting transfers between devices, shift(): lax.ppermute(values, 'y', [(place, (place + step) % 4) for place in range...  6.62 us
    ppermute x5, starting transfers between devices, swap(): return lax.ppermute(values, axis, [(0, 1), (1, 0)])  6.21 us
  transfers between devices with their start and end apart: 11, of which 7 were waited for; matrix products, arithmetic and copies ran while one was open for 0% of the time, Pallas kernels for 6%

profile of v6, /device:TPU:2, one launch (start us, length us, event | category | flops | bytes accessed | tf_op | source)
XLA Modules:
  0.0 120.9 jit_solution(17762914026176754900)
XLA Ops:
  0.7 2.2 %shard_map.135 = bf16[128,8,384]{2,1,0:T(8,128)(2,1)} custom-call(bf16[14,7,4,384]{3,2,1,0:T(4,128)(2,1)} %bitcast.7, bf16[14,7,4,384]{3,2,1,0:T(4,128)(2,1)} %bitcast.8), custom_call_target="tpu_custom_call" | custom-call | bytes 2000000 | tf_op jit(solution)/shard_map/pallas_call | solution.py:406
  2.9 13.9 %all-to-all-start = ((bf16[128,8,384]{2,1,0:T(8,128)(2,1)}), bf16[128,8,384]{2,1,0:T(8,128)(2,1)S(1)}, u32[]{:S(2)}, u32[]{:S(2)}) async-start(bf16[128,8,384]{2,1,0:T(8,128)(2,1)} %shard_map.135), calls=%async_computation | async-start | bytes 1572864 | tf_op jit(solution)/shard_map/all_to_all | solution.py:420
  16.9 23.7 %all-to-all-done = bf16[128,8,384]{2,1,0:T(8,128)(2,1)S(1)} async-done(((bf16[128,8,384]{2,1,0:T(8,128)(2,1)}), bf16[128,8,384]{2,1,0:T(8,128)(2,1)S(1)}, u32[]{:S(2)}, u32[]{:S(2)}) %all-to-all-start) | async-done | bytes 786464 | tf_op jit(solution)/shard_map/all_to_all | solution.py:420
  40.6 2.9 %shard_map.136 = (bf16[512,384]{1,0:T(8,128)(2,1)S(1)}, bf16[512,1152]{1,0:T(8,128)(2,1)S(1)}, bf16[512,384]{1,0:T(8,128)(2,1)S(1)}, bf16[512,384]{1,0:T(8,128)(2,1)S(1)}, bf16[512,384]{1,0:T(8,128)(2,1)S(1)}) custom-call(bf16[1024,384]{1,0:T(8,128)(2,1)S(1)} %bitcast.6, f32[1,384]{1,0:T(1,128)S(1)} %reshape.24.gain_one, bf16[1152,384]{1,0:T(8,128)(2,1)S(1)} %copy-done.2, ...), custom_call_target="tpu_custom_call" | custom-call | flops 1000000000 | bytes 4000000 | tf_op jit(solution)/shard_map/pallas_call | solution.py:406
  43.5 6.8 %shard_map.137 = (bf16[512,384]{1,0:T(8,128)(2,1)S(1)}, bf16[8,192,384]{2,1,0:T(8,128)(2,1)S(1)}, bf16[8,192,384]{2,1,0:T(8,128)(2,1)S(1)}, f32[1,384]{1,0:T(1,128)S(1)}) custom-call(bf16[512,384]{1,0:T(8,128)(2,1)S(1)} %get-tuple-element.46.grad_out, bf16[512,384]{1,0:T(8,128)(2,1)S(1)} %get-tuple-element.47.resid, f32[1,384]{1,0:T(1,128)S(1)} %reshape.25.gain_two, ...), custom_call_target="tpu_custom_call" | custom-call | flops 3000000000 | bytes 6000000 | tf_op jit(solution)/shard_map/pallas_call | solution.py:406
  50.6 5.1 %shard_map.138 = (bf16[128,3,4,128]{3,2,1,0:T(4,128)(2,1)}, bf16[512,1152]{1,0:T(8,128)(2,1)S(1)}, bf16[512,384]{1,0:T(8,128)(2,1)S(1)}, f32[1,384]{1,0:T(1,128)S(1)}) custom-call(bf16[512,384]{1,0:T(8,128)(2,1)S(1)} %get-tuple-element.44.x_ref, bf16[512,1152]{1,0:T(8,128)(2,1)S(1)} %get-tuple-element.45.qkv_ref, ...), custom_call_target="tpu_custom_call" | custom-call | flops 6000000000 | bytes 20000000 | tf_op jit(solution)/shard_map/pallas_call | solution.py:406
  56.0 2.5 %shard_map.140 = (bf16[8,112,384]{2,1,0:T(8,128)(2,1)S(1)}, bf16[8,112,384]{2,1,0:T(8,128)(2,1)}) custom-call(bf16[512,1152]{1,0:T(8,128)(2,1)S(1)} %get-tuple-element.56.rows_grad, bf16[512,384]{1,0:T(8,128)(2,1)S(1)} %get-tuple-element.57.normed, bf16[512,384]{1,0:T(8,128)(2,1)S(1)} %get-tuple-element.48.resid_grad_ref.resid_grad, ...), custom_call_target="tpu_custom_call" | custom-call | flops 1000000000 | bytes 5000000 | tf_op jit(solution)/shard_map/pallas_call | solution.py:406
  58.4 0.5 collective-permute-start.2
  59.0 2.2 %collective-permute-start.1 = (bf16[4,192,384]{2,1,0:T(8,128)(2,1)S(1)}, bf16[4,192,384]{2,1,0:T(8,128)(2,1)S(1)}, u32[]{:S(2)}, u32[]{:S(2)}) collective-permute-start(bf16[4,192,384]{2,1,0:T(8,128)(2,1)S(1)} %get-tuple-element.55), channel_id=1, source_target_pairs={{0,32},{32,0},{1,33},{33,1},{2,34},{34,2},{3,35},{35,3},{4,36},{36... | collective-permute-start | bytes 1769480 | tf_op jit(solution)/shard_map/ppermute | solution.py:424
  61.2 5.7 %all-to-all-start.1 = ((bf16[128,3,4,128]{3,2,1,0:T(4,128)(2,1)}), bf16[128,3,4,128]{3,2,1,0:T(4,128)(2,1)S(1)}, u32[]{:S(2)}, u32[]{:S(2)}) async-start(bf16[128,3,4,128]{3,2,1,0:T(4,128)(2,1)} %get-tuple-element.72), calls=%async_computation.1 | async-start | bytes 786432 | tf_op jit(solution)/shard_map/all_to_all | solution.py:420
  67.0 1.0 collective-permute-start.3
  68.0 10.9 %collective-permute-done.1.early_recv = bf16[4,192,384]{2,1,0:T(8,128)(2,1)S(1)} collective-permute-done((bf16[4,192,384]{2,1,0:T(8,128)(2,1)S(1)}, bf16[4,192,384]{2,1,0:T(8,128)(2,1)S(1)}, u32[]{:S(2)}, u32[]{:S(2)}) %collective-permute-start.1) | collective-permute-done | bytes 589856 | tf_op jit(solution)/shard_map/ppermute | solution.py:424
  78.9 7.4 %collective-permute-done.3.late_recv = bf16[4,112,384]{2,1,0:T(8,128)(2,1)S(1)} collective-permute-done((bf16[4,112,384]{2,1,0:T(8,128)(2,1)S(1)}, bf16[4,112,384]{2,1,0:T(8,128)(2,1)S(1)}, u32[]{:S(2)}, u32[]{:S(2)}) %collective-permute-start.3) | collective-permute-done | bytes 344096 | tf_op jit(solution)/shard_map/ppermute | solution.py:424
  86.5 0.4 collective-permute-start.4
  86.8 3.0 %collective-permute-start.5 = (bf16[112,384]{1,0:T(8,128)(2,1)S(1)}, bf16[112,384]{1,0:T(8,128)(2,1)S(1)}, u32[]{:S(2)}, u32[]{:S(2)}) collective-permute-start(bf16[112,384]{1,0:T(8,128)(2,1)S(1)} %get-tuple-element.69), channel_id=1, source_target_pairs={{0,192},{64,0},{128,64},{192,128},{1,193},{65,1},{129,65},{193,129... | collective-permute-start | bytes 258056 | tf_op jit(solution)/shard_map/ppermute | solution.py:433
  89.8 2.1 %collective-permute-done.5.far_late = bf16[112,384]{1,0:T(8,128)(2,1)S(1)} collective-permute-done((bf16[112,384]{1,0:T(8,128)(2,1)S(1)}, bf16[112,384]{1,0:T(8,128)(2,1)S(1)}, u32[]{:S(2)}, u32[]{:S(2)}) %collective-permute-start.5) | collective-permute-done | bytes 86048 | tf_op jit(solution)/shard_map/ppermute | solution.py:433
  91.9 1.1 collective-permute-done.4.far_early
  93.2 3.2 %collective-permute-start.7 = (bf16[304,384]{1,0:T(8,128)(2,1)S(1)}, bf16[304,384]{1,0:T(8,128)(2,1)S(1)}, u32[]{:S(2)}, u32[]{:S(2)}) collective-permute-start(bf16[304,384]{1,0:T(8,128)(2,1)S(1)} %get-tuple-element.71), channel_id=1, source_target_pairs={{0,192},{64,0},{128,64},{192,128},{1,193},{65,1},{129,65},{193,129... | collective-permute-start | bytes 700424 | tf_op jit(solution)/shard_map/ppermute | solution.py:433
  96.4 4.1 %collective-permute-done.6.near = bf16[304,384]{1,0:T(8,128)(2,1)S(1)} collective-permute-done((bf16[304,384]{1,0:T(8,128)(2,1)S(1)}, bf16[304,384]{1,0:T(8,128)(2,1)S(1)}, u32[]{:S(2)}, u32[]{:S(2)}) %collective-permute-start.6) | collective-permute-done | bytes 233504 | tf_op jit(solution)/shard_map/ppermute | solution.py:433
  100.8 13.7 %all_to_all.15.recv_ref = bf16[8,152,128]{2,1,0:T(8,128)(2,1)S(1)} all-to-all(bf16[8,152,128]{2,1,0:T(8,128)(2,1)S(1)} %shard_map.144), channel_id=1, replica_groups=mesh['y'=4,'xl'=2,'core'=2,'wa'=8,'dp'=2] {'wa'}, dimensions={0} | all-to-all | bytes 622592 | tf_op jit(solution)/shard_map/all_to_all | solution.py:420
  114.6 2.2 %collective-permute-start.8 = (bf16[152,128]{1,0:T(8,128)(2,1)S(1)}, bf16[152,128]{1,0:T(8,128)(2,1)S(1)}, u32[]{:S(2)}, u32[]{:S(2)}) collective-permute-start(bf16[152,128]{1,0:T(8,128)(2,1)S(1)} %shard_map.146.own_ref), channel_id=1, source_target_pairs={{0,1},{1,0},{2,3},{3,2},{4,5},{5,4},{6,7},{7,6},{8,9},{9,8},{10,11... | collective-permute-start | bytes 116744 | tf_op jit(solution)/shard_map/ppermute | solution.py:424
  116.8 0.8 shard_map.145
  117.6 2.5 %collective-permute-done.8.other_ref = bf16[152,128]{1,0:T(8,128)(2,1)S(1)} collective-permute-done((bf16[152,128]{1,0:T(8,128)(2,1)S(1)}, bf16[152,128]{1,0:T(8,128)(2,1)S(1)}, u32[]{:S(2)}, u32[]{:S(2)}) %collective-permute-start.8) | collective-permute-done | bytes 38944 | tf_op jit(solution)/shard_map/ppermute | solution.py:424
  120.1 0.8 shard_map.147
  (26 shorter events, 1.5 us)
Async XLA Ops:
  0.6 16.2 %copy-start.4 = (f32[384]{0:T(512)S(1)}, f32[384]{0:T(512)}, u32[]{:S(2)}) copy-start(f32[384]{0:T(512)} %param.10) | copy-start | bytes 4612
  0.6 16.2 %copy-start.5 = (f32[384]{0:T(512)S(1)}, f32[384]{0:T(512)}, u32[]{:S(2)}) copy-start(f32[384]{0:T(512)} %param.11) | copy-start | bytes 4612
  0.7 39.9 %copy-start.2 = (bf16[1152,384]{1,0:T(8,128)(2,1)S(1)}, bf16[1152,384]{1,0:T(8,128)(2,1)}, u32[]{:S(2)}) copy-start(bf16[1152,384]{1,0:T(8,128)(2,1)} %w_qkv.3) | copy-start | bytes 2654212
  0.7 39.9 %copy-start.3 = (bf16[384,384]{1,0:T(8,128)(2,1)S(1)}, bf16[384,384]{1,0:T(8,128)(2,1)}, u32[]{:S(2)}) copy-start(bf16[384,384]{1,0:T(8,128)(2,1)} %w_proj.3) | copy-start | bytes 884740
  2.9 37.7 %all-to-all-start = ((bf16[128,8,384]{2,1,0:T(8,128)(2,1)}), bf16[128,8,384]{2,1,0:T(8,128)(2,1)S(1)}, u32[]{:S(2)}, u32[]{:S(2)}) async-start(bf16[128,8,384]{2,1,0:T(8,128)(2,1)} %shard_map.135), calls=%async_computation | async-start | bytes 1572864 | tf_op jit(solution)/shard_map/all_to_all | solution.py:420
  40.6 2.9 %copy-start = (bf16[1536,384]{1,0:T(8,128)(2,1)S(1)}, bf16[1536,384]{1,0:T(8,128)(2,1)}, u32[]{:S(2)}) copy-start(bf16[1536,384]{1,0:T(8,128)(2,1)} %w_up.1) | copy-start | bytes 3538948
  40.6 2.9 %copy-start.1 = (bf16[384,1536]{1,0:T(8,128)(2,1)S(1)}, bf16[384,1536]{1,0:T(8,128)(2,1)}, u32[]{:S(2)}) copy-start(bf16[384,1536]{1,0:T(8,128)(2,1)} %w_down.1) | copy-start | bytes 3538948
  50.3 5.4 %collective-permute-start = (bf16[8,192,384]{2,1,0:T(8,128)(2,1)S(1)}, bf16[8,192,384]{2,1,0:T(8,128)(2,1)S(1)}, u32[]{:S(2)}, u32[]{:S(2)}) collective-permute-start(bf16[8,192,384]{2,1,0:T(8,128)(2,1)S(1)} %get-tuple-element.51), channel_id=1, source_target_pairs={{0,16},{16,0},{1,17},{17,1},{2,18},{18,2},{3,19},{19,3},{4,20},{20... | collective-permute-start | bytes 3538952 | tf_op jit(solution)/shard_map/ppermute | solution.py:424
  58.4 8.4 %collective-permute-start.2 = (bf16[8,112,384]{2,1,0:T(8,128)(2,1)}, bf16[8,112,384]{2,1,0:T(8,128)(2,1)S(1)}, u32[]{:S(2)}, u32[]{:S(2)}) collective-permute-start(bf16[8,112,384]{2,1,0:T(8,128)(2,1)} %get-tuple-element.62), channel_id=1, source_target_pairs={{0,16},{16,0},{1,17},{17,1},{2,18},{18,2},{3,19},{19,3},{4,20},{20... | collective-permute-start | bytes 2064392 | tf_op jit(solution)/shard_map/ppermute | solution.py:424
  59.0 19.9 %collective-permute-start.1 = (bf16[4,192,384]{2,1,0:T(8,128)(2,1)S(1)}, bf16[4,192,384]{2,1,0:T(8,128)(2,1)S(1)}, u32[]{:S(2)}, u32[]{:S(2)}) collective-permute-start(bf16[4,192,384]{2,1,0:T(8,128)(2,1)S(1)} %get-tuple-element.55), channel_id=1, source_target_pairs={{0,32},{32,0},{1,33},{33,1},{2,34},{34,2},{3,35},{35,3},{4,36},{36... | collective-permute-start | bytes 1769480 | tf_op jit(solution)/shard_map/ppermute | solution.py:424
  61.2 39.6 %all-to-all-start.1 = ((bf16[128,3,4,128]{3,2,1,0:T(4,128)(2,1)}), bf16[128,3,4,128]{3,2,1,0:T(4,128)(2,1)S(1)}, u32[]{:S(2)}, u32[]{:S(2)}) async-start(bf16[128,3,4,128]{3,2,1,0:T(4,128)(2,1)} %get-tuple-element.72), calls=%async_computation.1 | async-start | bytes 786432 | tf_op jit(solution)/shard_map/all_to_all | solution.py:420
  67.0 19.2 %collective-permute-start.3 = (bf16[4,112,384]{2,1,0:T(8,128)(2,1)S(1)}, bf16[4,112,384]{2,1,0:T(8,128)(2,1)S(1)}, u32[]{:S(2)}, u32[]{:S(2)}) collective-permute-start(bf16[4,112,384]{2,1,0:T(8,128)(2,1)S(1)} %get-tuple-element.64), channel_id=1, source_target_pairs={{0,32},{32,0},{1,33},{33,1},{2,34},{34,2},{3,35},{35,3},{4,36},{36... | collective-permute-start | bytes 1032200 | tf_op jit(solution)/shard_map/ppermute | solution.py:424
  86.5 6.5 %collective-permute-start.4 = (bf16[192,384]{1,0:T(8,128)(2,1)S(1)}, bf16[192,384]{1,0:T(8,128)(2,1)S(1)}, u32[]{:S(2)}, u32[]{:S(2)}) collective-permute-start(bf16[192,384]{1,0:T(8,128)(2,1)S(1)} %get-tuple-element.68), channel_id=1, source_target_pairs={{0,64},{64,128},{128,192},{192,0},{1,65},{65,129},{129,193},{193,1... | collective-permute-start | bytes 442376 | tf_op jit(solution)/shard_map/ppermute | solution.py:433
  86.8 5.1 %collective-permute-start.5 = (bf16[112,384]{1,0:T(8,128)(2,1)S(1)}, bf16[112,384]{1,0:T(8,128)(2,1)S(1)}, u32[]{:S(2)}, u32[]{:S(2)}) collective-permute-start(bf16[112,384]{1,0:T(8,128)(2,1)S(1)} %get-tuple-element.69), channel_id=1, source_target_pairs={{0,192},{64,0},{128,64},{192,128},{1,193},{65,1},{129,65},{193,129... | collective-permute-start | bytes 258056 | tf_op jit(solution)/shard_map/ppermute | solution.py:433
  93.1 7.4 %collective-permute-start.6 = (bf16[304,384]{1,0:T(8,128)(2,1)S(1)}, bf16[304,384]{1,0:T(8,128)(2,1)S(1)}, u32[]{:S(2)}, u32[]{:S(2)}) collective-permute-start(bf16[304,384]{1,0:T(8,128)(2,1)S(1)} %get-tuple-element.70), channel_id=1, source_target_pairs={{0,64},{64,128},{128,192},{192,0},{1,65},{65,129},{129,193},{193,1... | collective-permute-start | bytes 700424 | tf_op jit(solution)/shard_map/ppermute | solution.py:433
  93.2 7.3 %collective-permute-start.7 = (bf16[304,384]{1,0:T(8,128)(2,1)S(1)}, bf16[304,384]{1,0:T(8,128)(2,1)S(1)}, u32[]{:S(2)}, u32[]{:S(2)}) collective-permute-start(bf16[304,384]{1,0:T(8,128)(2,1)S(1)} %get-tuple-element.71), channel_id=1, source_target_pairs={{0,192},{64,0},{128,64},{192,128},{1,193},{65,1},{129,65},{193,129... | collective-permute-start | bytes 700424 | tf_op jit(solution)/shard_map/ppermute | solution.py:433
  114.6 5.6 %collective-permute-start.8 = (bf16[152,128]{1,0:T(8,128)(2,1)S(1)}, bf16[152,128]{1,0:T(8,128)(2,1)S(1)}, u32[]{:S(2)}, u32[]{:S(2)}) collective-permute-start(bf16[152,128]{1,0:T(8,128)(2,1)S(1)} %shard_map.146.own_ref), channel_id=1, source_target_pairs={{0,1},{1,0},{2,3},{3,2},{4,5},{5,4},{6,7},{7,6},{8,9},{9,8},{10,11... | collective-permute-start | bytes 116744 | tf_op jit(solution)/shard_map/ppermute | solution.py:424

commit v7 on v6

--- a/solution.py
+++ b/solution.py
@@ -303,24 +303,44 @@
             ref[piece] = piece_rows[...].astype(BF16)
 
 
-def core_kernel(keep_ref, recv_ref, out_keep, out_send):
-    row, col = lax.axis_index("y"), lax.axis_index("xl")
-    for ref, side in ((out_keep, col), (out_send, 1 - col)):
-        for step in range(4):
-            piece = ((row + step) & 3) * 2 + side
-            ref[step] = (keep_ref[piece].astype(F32) + recv_ref[piece].astype(F32)).astype(BF16)
+def core_total(keep_ref, recv_ref, step, side):
+    piece = ((lax.axis_index("y") + step) & 3) * 2 + side
+    return (keep_ref[piece].astype(F32) + recv_ref[piece].astype(F32)).astype(BF16)
+
+
+def early_kernel(keep_ref, recv_ref, out_keep, out_up, out_down):
+    col = lax.axis_index("xl")
+    for step in range(4):
+        out_keep[step] = core_total(keep_ref, recv_ref, step, col)
+        other = core_total(keep_ref, recv_ref, step, 1 - col)
+        out_up[step] = other[:96]
+        out_down[step] = other[96:]
+
+
+def late_kernel(keep_ref, recv_ref, up_ref, out_keep, out_send):
+    col = lax.axis_index("xl")
+    for step in range(4):
+        out_keep[step] = core_total(keep_ref, recv_ref, step, col)
+        out_send[step, :96] = up_ref[step]
+        out_send[step, 96:] = core_total(keep_ref, recv_ref, step, 1 - col)
 
 
 def side_kernel(
-    early_keep, early_recv, late_keep, late_recv, own, near, back, far_early, far_late,
+    early_keep, down_recv, late_keep, late_recv, own, near, back, far_early, far_late,
 ):
+    def total(step):
+        up = early_keep[step, :96].astype(F32) + late_recv[step, :96].astype(F32)
+        down = early_keep[step, 96:].astype(F32) + down_recv[step].astype(F32)
+        return up, down, late_keep[step].astype(F32) + late_recv[step, 96:].astype(F32)
+
     for step, ref in ((0, own), (1, near), (3, back)):
-        early = early_keep[step].astype(F32) + early_recv[step].astype(F32)
-        late = late_keep[step].astype(F32) + late_recv[step].astype(F32)
-        ref[:192] = early.astype(BF16)
+        up, down, late = total(step)
+        ref[:96] = up.astype(BF16)
+        ref[96:192] = down.astype(BF16)
         ref[192:] = late.astype(BF16)
-    far_early[...] = (early_keep[2].astype(F32) + early_recv[2].astype(F32)).astype(BF16)
-    late = late_keep[2].astype(F32) + late_recv[2].astype(F32)
+    up, down, late = total(2)
+    far_early[:96] = up.astype(BF16)
+    far_early[96:] = down.astype(BF16)
     far_late[:96] = late[:96].astype(BF16)
     far_late[96:] = pltpu.roll(late[96:], 2, 0).astype(BF16)
 
@@ -422,11 +442,6 @@
 
 def swap(values, axis):
     return lax.ppermute(values, axis, [(0, 1), (1, 0)])
-
-
-def side_pieces(keep, recv):
-    half = ((4, keep.shape[1], 384), BF16)
-    return call(core_kernel, [half, half], nbytes=4 * 10**6)(keep, recv)
 
 
 def shift(values, step):
@@ -471,21 +486,26 @@
         flops=6 * 10**9, nbytes=20 * 10**6,
     )(x, qkv, resid_grad, gain_one, w_qkv, w_proj)
     returned = exchange(slots, HA + ("wa",))
-    early = side_pieces(early_keep, swap(early_send, "core"))
-    rows_grad, *early = lax.optimization_barrier((rows_grad, *early))
+    part = ((4, 96, 384), BF16)
+    early = call(early_kernel, [((4, 192, 384), BF16), part, part], nbytes=4 * 10**6)(
+        early_keep, swap(early_send, "core")
+    )
+    rows_grad, early_keep, up_send, down_send = lax.optimization_barrier((rows_grad, *early))
     late_keep, late_send = call(
         weight_kernel,
         [((8, 112, 384), BF16), ((8, 112, 384), BF16)],
         [((1152, 384), F32), ((384, 384), F32), ((112, 384), F32)],
         flops=10**9, nbytes=5 * 10**6,
     )(rows_grad, normed, resid_grad, mixed, gain_sum_one, gain_sum_two)
-    late = side_pieces(late_keep, swap(late_send, "core"))
+    late_keep, late_send = call(
+        late_kernel, [((4, 112, 384), BF16), ((4, 208, 384), BF16)], nbytes=4 * 10**6
+    )(late_keep, swap(late_send, "core"), up_send)
     piece = ((304, 384), BF16)
     own, near, back, far_early, far_late = call(
         side_kernel,
         [piece, piece, piece, ((192, 384), BF16), ((112, 384), BF16)],
         nbytes=5 * 10**6,
-    )(early[0], swap(early[1], "xl"), late[0], swap(late[1], "xl"))
+    )(early_keep, swap(down_send, "xl"), late_keep, swap(late_send, "xl"))
     near, back = call(ring_kernel, [piece, piece], nbytes=2 * 10**6)(
         near, back, shift(far_early, 1), shift(far_late, 3)
     )

time: 122 us -> 124 us (1.016)
  waiting for transfers between devices: 51.8 us -> 54.6 us
    ppermute x5, waiting for transfers between devices: 20.8 us -> 22.9 us  [swap(): return lax.ppermute(values, axis, [(0, 1), (1, 0)])]
  transfers between devices with their start and end apart: 11 -> 11, of which waited for: 7 -> 7; matrix products, arithmetic and copies ran while one was open for 0% -> 0% of each run, Pallas kernels for 6% -> 5%
where the time goes in v7:
time: 124 us; the launch traced here: 123 us
  waiting for transfers between devices  54.6 us (44%)
  starting transfers between devices  32.8 us (26%)
  Pallas kernels  21.3 us (17%)
  blocking collectives  13.7 us (11%)
    all_to_all x2, waiting for transfers between devices, exchange(): return lax.all_to_all(values, axes, split_axis=0, concat_axis=0, tiled=True)  23.7 us
    ppermute x5, waiting for transfers between devices, swap(): return lax.ppermute(values, axis, [(0, 1), (1, 0)])  22.9 us
    pallas_call x13, Pallas kernels, run(): pl.pallas_call(kernel, out_shape=[jax.ShapeDtypeStruct(shape, dtype) for...  21.3 us
    all_to_all x2, starting transfers between devices, exchange(): return lax.all_to_all(values, axes, split_axis=0, concat_axis=0, tiled=True)  19.8 us
    all_to_all x1, blocking collectives, exchange(): return lax.all_to_all(values, axes, split_axis=0, concat_axis=0, tiled=True)  13.7 us
    ppermute x4, waiting for transfers between devices, shift(): lax.ppermute(values, 'y', [(place, (place + step) % 4) for place in range...  8.02 us
    ppermute x4, starting transfers between devices, shift(): lax.ppermute(values, 'y', [(place, (place + step) % 4) for place in range...  6.62 us
    ppermute x5, starting transfers between devices, swap(): return lax.ppermute(values, axis, [(0, 1), (1, 0)])  6.37 us
  transfers between devices with their start and end apart: 11, of which 7 were waited for; matrix products, arithmetic and copies ran while one was open for 0% of the time, Pallas kernels for 5%

profile of v7, /device:TPU:2, one launch (start us, length us, event | category | flops | bytes accessed | tf_op | source)
XLA Modules:
  0.0 123.3 jit_solution(6874088465592455123)
XLA Ops:
  0.7 2.2 %shard_map.135 = bf16[128,8,384]{2,1,0:T(8,128)(2,1)} custom-call(bf16[14,7,4,384]{3,2,1,0:T(4,128)(2,1)} %bitcast.7, bf16[14,7,4,384]{3,2,1,0:T(4,128)(2,1)} %bitcast.8), custom_call_target="tpu_custom_call" | custom-call | bytes 2000000 | tf_op jit(solution)/shard_map/pallas_call | solution.py:426
  2.9 13.9 %all-to-all-start = ((bf16[128,8,384]{2,1,0:T(8,128)(2,1)}), bf16[128,8,384]{2,1,0:T(8,128)(2,1)S(1)}, u32[]{:S(2)}, u32[]{:S(2)}) async-start(bf16[128,8,384]{2,1,0:T(8,128)(2,1)} %shard_map.135), calls=%async_computation | async-start | bytes 1572864 | tf_op jit(solution)/shard_map/all_to_all | solution.py:440
  16.9 23.7 %all-to-all-done = bf16[128,8,384]{2,1,0:T(8,128)(2,1)S(1)} async-done(((bf16[128,8,384]{2,1,0:T(8,128)(2,1)}), bf16[128,8,384]{2,1,0:T(8,128)(2,1)S(1)}, u32[]{:S(2)}, u32[]{:S(2)}) %all-to-all-start) | async-done | bytes 786464 | tf_op jit(solution)/shard_map/all_to_all | solution.py:440
  40.6 2.9 %shard_map.136 = (bf16[512,384]{1,0:T(8,128)(2,1)S(1)}, bf16[512,1152]{1,0:T(8,128)(2,1)S(1)}, bf16[512,384]{1,0:T(8,128)(2,1)S(1)}, bf16[512,384]{1,0:T(8,128)(2,1)S(1)}, bf16[512,384]{1,0:T(8,128)(2,1)S(1)}) custom-call(bf16[1024,384]{1,0:T(8,128)(2,1)S(1)} %bitcast.6, f32[1,384]{1,0:T(1,128)S(1)} %reshape.24.gain_one, bf16[1152,384]{1,0:T(8,128)(2,1)S(1)} %copy-done.2, ...), custom_call_target="tpu_custom_call" | custom-call | flops 1000000000 | bytes 4000000 | tf_op jit(solution)/shard_map/pallas_call | solution.py:426
  43.5 6.8 %shard_map.137 = (bf16[512,384]{1,0:T(8,128)(2,1)S(1)}, bf16[8,192,384]{2,1,0:T(8,128)(2,1)S(1)}, bf16[8,192,384]{2,1,0:T(8,128)(2,1)S(1)}, f32[1,384]{1,0:T(1,128)S(1)}) custom-call(bf16[512,384]{1,0:T(8,128)(2,1)S(1)} %get-tuple-element.48.grad_out, bf16[512,384]{1,0:T(8,128)(2,1)S(1)} %get-tuple-element.49.resid, f32[1,384]{1,0:T(1,128)S(1)} %reshape.25.gain_two, ...), custom_call_target="tpu_custom_call" | custom-call | flops 3000000000 | bytes 6000000 | tf_op jit(solution)/shard_map/pallas_call | solution.py:426
  50.6 5.1 %shard_map.138 = (bf16[128,3,4,128]{3,2,1,0:T(4,128)(2,1)}, bf16[512,1152]{1,0:T(8,128)(2,1)S(1)}, bf16[512,384]{1,0:T(8,128)(2,1)S(1)}, f32[1,384]{1,0:T(1,128)S(1)}) custom-call(bf16[512,384]{1,0:T(8,128)(2,1)S(1)} %get-tuple-element.46.x_ref, bf16[512,1152]{1,0:T(8,128)(2,1)S(1)} %get-tuple-element.47.qkv_ref, ...), custom_call_target="tpu_custom_call" | custom-call | flops 6000000000 | bytes 20000000 | tf_op jit(solution)/shard_map/pallas_call | solution.py:426
  56.0 1.6 %shard_map.140 = (bf16[8,112,384]{2,1,0:T(8,128)(2,1)S(1)}, bf16[8,112,384]{2,1,0:T(8,128)(2,1)S(1)}) custom-call(bf16[512,1152]{1,0:T(8,128)(2,1)S(1)} %get-tuple-element.59.rows_grad, bf16[512,384]{1,0:T(8,128)(2,1)S(1)} %get-tuple-element.60.normed, bf16[512,384]{1,0:T(8,128)(2,1)S(1)} %get-tuple-element.50.resid_grad_ref.resid_grad, ...), custom_call_target="tpu_custom_call" | custom-call | flops 1000000000 | bytes 5000000 | tf_op jit(solution)/shard_map/pallas_call | solution.py:426
  57.6 0.6 collective-permute-start.2
  58.2 1.8 %collective-permute-done.2.recv_ref = bf16[8,112,384]{2,1,0:T(8,128)(2,1)S(1)} collective-permute-done((bf16[8,112,384]{2,1,0:T(8,128)(2,1)S(1)}, bf16[8,112,384]{2,1,0:T(8,128)(2,1)S(1)}, u32[]{:S(2)}, u32[]{:S(2)}) %collective-permute-start.2) | collective-permute-done | bytes 688160 | tf_op jit(solution)/shard_map/ppermute | solution.py:444
  60.1 2.3 %collective-permute-start.3 = (bf16[4,208,384]{2,1,0:T(8,128)(2,1)S(1)}, bf16[4,208,384]{2,1,0:T(8,128)(2,1)S(1)}, u32[]{:S(2)}, u32[]{:S(2)}) collective-permute-start(bf16[4,208,384]{2,1,0:T(8,128)(2,1)S(1)} %get-tuple-element.68), channel_id=1, source_target_pairs={{0,32},{32,0},{1,33},{33,1},{2,34},{34,2},{3,35},{35,3},{4,36},{36... | collective-permute-start | bytes 1916936 | tf_op jit(solution)/shard_map/ppermute | solution.py:444
  62.5 5.8 %all-to-all-start.1 = ((bf16[128,3,4,128]{3,2,1,0:T(4,128)(2,1)}), bf16[128,3,4,128]{3,2,1,0:T(4,128)(2,1)S(1)}, u32[]{:S(2)}, u32[]{:S(2)}) async-start(bf16[128,3,4,128]{3,2,1,0:T(4,128)(2,1)} %get-tuple-element.76), calls=%async_computation.1 | async-start | bytes 786432 | tf_op jit(solution)/shard_map/all_to_all | solution.py:440
  68.3 1.0 collective-permute-start.1
  69.3 18.6 %collective-permute-done.1.down_recv = bf16[4,96,384]{2,1,0:T(8,128)(2,1)S(1)} collective-permute-done((bf16[4,96,384]{2,1,0:T(8,128)(2,1)S(1)}, bf16[4,96,384]{2,1,0:T(8,128)(2,1)S(1)}, u32[]{:S(2)}, u32[]{:S(2)}) %collective-permute-start.1) | collective-permute-done | bytes 294944 | tf_op jit(solution)/shard_map/ppermute | solution.py:444
  88.1 0.3 collective-permute-start.4
  88.5 3.0 %collective-permute-start.5 = (bf16[112,384]{1,0:T(8,128)(2,1)S(1)}, bf16[112,384]{1,0:T(8,128)(2,1)S(1)}, u32[]{:S(2)}, u32[]{:S(2)}) collective-permute-start(bf16[112,384]{1,0:T(8,128)(2,1)S(1)} %get-tuple-element.73), channel_id=1, source_target_pairs={{0,192},{64,0},{128,64},{192,128},{1,193},{65,1},{129,65},{193,129... | collective-permute-start | bytes 258056 | tf_op jit(solution)/shard_map/ppermute | solution.py:448
  91.4 2.1 %collective-permute-done.5.far_late = bf16[112,384]{1,0:T(8,128)(2,1)S(1)} collective-permute-done((bf16[112,384]{1,0:T(8,128)(2,1)S(1)}, bf16[112,384]{1,0:T(8,128)(2,1)S(1)}, u32[]{:S(2)}, u32[]{:S(2)}) %collective-permute-start.5) | collective-permute-done | bytes 86048 | tf_op jit(solution)/shard_map/ppermute | solution.py:448
  93.5 1.4 %collective-permute-done.4.far_early = bf16[192,384]{1,0:T(8,128)(2,1)S(1)} collective-permute-done((bf16[192,384]{1,0:T(8,128)(2,1)S(1)}, bf16[192,384]{1,0:T(8,128)(2,1)S(1)}, u32[]{:S(2)}, u32[]{:S(2)}) %collective-permute-start.4) | collective-permute-done | bytes 147488 | tf_op jit(solution)/shard_map/ppermute | solution.py:448
  95.1 3.2 %collective-permute-start.7 = (bf16[304,384]{1,0:T(8,128)(2,1)S(1)}, bf16[304,384]{1,0:T(8,128)(2,1)S(1)}, u32[]{:S(2)}, u32[]{:S(2)}) collective-permute-start(bf16[304,384]{1,0:T(8,128)(2,1)S(1)} %get-tuple-element.75), channel_id=1, source_target_pairs={{0,192},{64,0},{128,64},{192,128},{1,193},{65,1},{129,65},{193,129... | collective-permute-start | bytes 700424 | tf_op jit(solution)/shard_map/ppermute | solution.py:448
  98.4 4.5 %collective-permute-done.6.near = bf16[304,384]{1,0:T(8,128)(2,1)S(1)} collective-permute-done((bf16[304,384]{1,0:T(8,128)(2,1)S(1)}, bf16[304,384]{1,0:T(8,128)(2,1)S(1)}, u32[]{:S(2)}, u32[]{:S(2)}) %collective-permute-start.6) | collective-permute-done | bytes 233504 | tf_op jit(solution)/shard_map/ppermute | solution.py:448
  103.2 13.7 %all_to_all.15.recv_ref = bf16[8,152,128]{2,1,0:T(8,128)(2,1)S(1)} all-to-all(bf16[8,152,128]{2,1,0:T(8,128)(2,1)S(1)} %shard_map.144), channel_id=1, replica_groups=mesh['y'=4,'xl'=2,'core'=2,'wa'=8,'dp'=2] {'wa'}, dimensions={0} | all-to-all | bytes 622592 | tf_op jit(solution)/shard_map/all_to_all | solution.py:440
  116.9 2.2 %collective-permute-start.8 = (bf16[152,128]{1,0:T(8,128)(2,1)S(1)}, bf16[152,128]{1,0:T(8,128)(2,1)S(1)}, u32[]{:S(2)}, u32[]{:S(2)}) collective-permute-start(bf16[152,128]{1,0:T(8,128)(2,1)S(1)} %shard_map.146.own_ref), channel_id=1, source_target_pairs={{0,1},{1,0},{2,3},{3,2},{4,5},{5,4},{6,7},{7,6},{8,9},{9,8},{10,11... | collective-permute-start | bytes 116744 | tf_op jit(solution)/shard_map/ppermute | solution.py:444
  119.2 0.8 shard_map.145
  120.0 2.5 %collective-permute-done.8.other_ref = bf16[152,128]{1,0:T(8,128)(2,1)S(1)} collective-permute-done((bf16[152,128]{1,0:T(8,128)(2,1)S(1)}, bf16[152,128]{1,0:T(8,128)(2,1)S(1)}, u32[]{:S(2)}, u32[]{:S(2)}) %collective-permute-start.8) | collective-permute-done | bytes 38944 | tf_op jit(solution)/shard_map/ppermute | solution.py:444
  122.5 0.8 shard_map.147
  (26 shorter events, 1.5 us)
Async XLA Ops:
  0.6 16.2 %copy-start.4 = (f32[384]{0:T(512)S(1)}, f32[384]{0:T(512)}, u32[]{:S(2)}) copy-start(f32[384]{0:T(512)} %param.10) | copy-start | bytes 4612
  0.6 16.2 %copy-start.5 = (f32[384]{0:T(512)S(1)}, f32[384]{0:T(512)}, u32[]{:S(2)}) copy-start(f32[384]{0:T(512)} %param.11) | copy-start | bytes 4612
  0.7 39.9 %copy-start.2 = (bf16[1152,384]{1,0:T(8,128)(2,1)S(1)}, bf16[1152,384]{1,0:T(8,128)(2,1)}, u32[]{:S(2)}) copy-start(bf16[1152,384]{1,0:T(8,128)(2,1)} %w_qkv.3) | copy-start | bytes 2654212
  0.7 39.9 %copy-start.3 = (bf16[384,384]{1,0:T(8,128)(2,1)S(1)}, bf16[384,384]{1,0:T(8,128)(2,1)}, u32[]{:S(2)}) copy-start(bf16[384,384]{1,0:T(8,128)(2,1)} %w_proj.3) | copy-start | bytes 884740
  2.9 37.7 %all-to-all-start = ((bf16[128,8,384]{2,1,0:T(8,128)(2,1)}), bf16[128,8,384]{2,1,0:T(8,128)(2,1)S(1)}, u32[]{:S(2)}, u32[]{:S(2)}) async-start(bf16[128,8,384]{2,1,0:T(8,128)(2,1)} %shard_map.135), calls=%async_computation | async-start | bytes 1572864 | tf_op jit(solution)/shard_map/all_to_all | solution.py:440
  40.6 2.9 %copy-start = (bf16[1536,384]{1,0:T(8,128)(2,1)S(1)}, bf16[1536,384]{1,0:T(8,128)(2,1)}, u32[]{:S(2)}) copy-start(bf16[1536,384]{1,0:T(8,128)(2,1)} %w_up.1) | copy-start | bytes 3538948
  40.6 2.9 %copy-start.1 = (bf16[384,1536]{1,0:T(8,128)(2,1)S(1)}, bf16[384,1536]{1,0:T(8,128)(2,1)}, u32[]{:S(2)}) copy-start(bf16[384,1536]{1,0:T(8,128)(2,1)} %w_down.1) | copy-start | bytes 3538948
  50.3 5.4 %collective-permute-start = (bf16[8,192,384]{2,1,0:T(8,128)(2,1)S(1)}, bf16[8,192,384]{2,1,0:T(8,128)(2,1)S(1)}, u32[]{:S(2)}, u32[]{:S(2)}) collective-permute-start(bf16[8,192,384]{2,1,0:T(8,128)(2,1)S(1)} %get-tuple-element.53), channel_id=1, source_target_pairs={{0,16},{16,0},{1,17},{17,1},{2,18},{18,2},{3,19},{19,3},{4,20},{20... | collective-permute-start | bytes 3538952 | tf_op jit(solution)/shard_map/ppermute | solution.py:444
  57.6 2.4 %collective-permute-start.2 = (bf16[8,112,384]{2,1,0:T(8,128)(2,1)S(1)}, bf16[8,112,384]{2,1,0:T(8,128)(2,1)S(1)}, u32[]{:S(2)}, u32[]{:S(2)}) collective-permute-start(bf16[8,112,384]{2,1,0:T(8,128)(2,1)S(1)} %get-tuple-element.65), channel_id=1, source_target_pairs={{0,16},{16,0},{1,17},{17,1},{2,18},{18,2},{3,19},{19,3},{4,20},{20... | collective-permute-start | bytes 2064392 | tf_op jit(solution)/shard_map/ppermute | solution.py:444
  60.1 27.8 %collective-permute-start.3 = (bf16[4,208,384]{2,1,0:T(8,128)(2,1)S(1)}, bf16[4,208,384]{2,1,0:T(8,128)(2,1)S(1)}, u32[]{:S(2)}, u32[]{:S(2)}) collective-permute-start(bf16[4,208,384]{2,1,0:T(8,128)(2,1)S(1)} %get-tuple-element.68), channel_id=1, source_target_pairs={{0,32},{32,0},{1,33},{33,1},{2,34},{34,2},{3,35},{35,3},{4,36},{36... | collective-permute-start | bytes 1916936 | tf_op jit(solution)/shard_map/ppermute | solution.py:444
  62.5 40.7 %all-to-all-start.1 = ((bf16[128,3,4,128]{3,2,1,0:T(4,128)(2,1)}), bf16[128,3,4,128]{3,2,1,0:T(4,128)(2,1)S(1)}, u32[]{:S(2)}, u32[]{:S(2)}) async-start(bf16[128,3,4,128]{3,2,1,0:T(4,128)(2,1)} %get-tuple-element.76), calls=%async_computation.1 | async-start | bytes 786432 | tf_op jit(solution)/shard_map/all_to_all | solution.py:440
  68.3 19.6 %collective-permute-start.1 = (bf16[4,96,384]{2,1,0:T(8,128)(2,1)S(1)}, bf16[4,96,384]{2,1,0:T(8,128)(2,1)S(1)}, u32[]{:S(2)}, u32[]{:S(2)}) collective-permute-start(bf16[4,96,384]{2,1,0:T(8,128)(2,1)S(1)} %get-tuple-element.58), channel_id=1, source_target_pairs={{0,32},{32,0},{1,33},{33,1},{2,34},{34,2},{3,35},{35,3},{4,36},{36... | collective-permute-start | bytes 884744 | tf_op jit(solution)/shard_map/ppermute | solution.py:444
  88.1 6.8 %collective-permute-start.4 = (bf16[192,384]{1,0:T(8,128)(2,1)S(1)}, bf16[192,384]{1,0:T(8,128)(2,1)S(1)}, u32[]{:S(2)}, u32[]{:S(2)}) collective-permute-start(bf16[192,384]{1,0:T(8,128)(2,1)S(1)} %get-tuple-element.72), channel_id=1, source_target_pairs={{0,64},{64,128},{128,192},{192,0},{1,65},{65,129},{129,193},{193,1... | collective-permute-start | bytes 442376 | tf_op jit(solution)/shard_map/ppermute | solution.py:448
  88.5 5.1 %collective-permute-start.5 = (bf16[112,384]{1,0:T(8,128)(2,1)S(1)}, bf16[112,384]{1,0:T(8,128)(2,1)S(1)}, u32[]{:S(2)}, u32[]{:S(2)}) collective-permute-start(bf16[112,384]{1,0:T(8,128)(2,1)S(1)} %get-tuple-element.73), channel_id=1, source_target_pairs={{0,192},{64,0},{128,64},{192,128},{1,193},{65,1},{129,65},{193,129... | collective-permute-start | bytes 258056 | tf_op jit(solution)/shard_map/ppermute | solution.py:448
  95.0 7.8 %collective-permute-start.6 = (bf16[304,384]{1,0:T(8,128)(2,1)S(1)}, bf16[304,384]{1,0:T(8,128)(2,1)S(1)}, u32[]{:S(2)}, u32[]{:S(2)}) collective-permute-start(bf16[304,384]{1,0:T(8,128)(2,1)S(1)} %get-tuple-element.74), channel_id=1, source_target_pairs={{0,64},{64,128},{128,192},{192,0},{1,65},{65,129},{129,193},{193,1... | collective-permute-start | bytes 700424 | tf_op jit(solution)/shard_map/ppermute | solution.py:448
  95.1 7.7 %collective-permute-start.7 = (bf16[304,384]{1,0:T(8,128)(2,1)S(1)}, bf16[304,384]{1,0:T(8,128)(2,1)S(1)}, u32[]{:S(2)}, u32[]{:S(2)}) collective-permute-start(bf16[304,384]{1,0:T(8,128)(2,1)S(1)} %get-tuple-element.75), channel_id=1, source_target_pairs={{0,192},{64,0},{128,64},{192,128},{1,193},{65,1},{129,65},{193,129... | collective-permute-start | bytes 700424 | tf_op jit(solution)/shard_map/ppermute | solution.py:448
  116.9 5.6 %collective-permute-start.8 = (bf16[152,128]{1,0:T(8,128)(2,1)S(1)}, bf16[152,128]{1,0:T(8,128)(2,1)S(1)}, u32[]{:S(2)}, u32[]{:S(2)}) collective-permute-start(bf16[152,128]{1,0:T(8,128)(2,1)S(1)} %shard_map.146.own_ref), channel_id=1, source_target_pairs={{0,1},{1,0},{2,3},{3,2},{4,5},{5,4},{6,7},{7,6},{8,9},{9,8},{10,11... | collective-permute-start | bytes 116744 | tf_op jit(solution)/shard_map/ppermute | solution.py:444

commit v8 on v6

--- a/solution.py
+++ b/solution.py
@@ -303,26 +303,24 @@
             ref[piece] = piece_rows[...].astype(BF16)
 
 
-def core_kernel(keep_ref, recv_ref, out_keep, out_send):
+def core_kernel(early_keep, early_recv, late_keep, late_recv, out_keep, out_send):
     row, col = lax.axis_index("y"), lax.axis_index("xl")
     for ref, side in ((out_keep, col), (out_send, 1 - col)):
         for step in range(4):
             piece = ((row + step) & 3) * 2 + side
-            ref[step] = (keep_ref[piece].astype(F32) + recv_ref[piece].astype(F32)).astype(BF16)
-
-
-def side_kernel(
-    early_keep, early_recv, late_keep, late_recv, own, near, back, far_early, far_late,
-):
+            early = early_keep[piece].astype(F32) + early_recv[piece].astype(F32)
+            late = late_keep[piece].astype(F32) + late_recv[piece].astype(F32)
+            ref[step, :192] = early.astype(BF16)
+            ref[step, 192:] = late.astype(BF16)
+
+
+def side_kernel(keep_ref, recv_ref, own, near, back, far_early, far_late):
     for step, ref in ((0, own), (1, near), (3, back)):
-        early = early_keep[step].astype(F32) + early_recv[step].astype(F32)
-        late = late_keep[step].astype(F32) + late_recv[step].astype(F32)
-        ref[:192] = early.astype(BF16)
-        ref[192:] = late.astype(BF16)
-    far_early[...] = (early_keep[2].astype(F32) + early_recv[2].astype(F32)).astype(BF16)
-    late = late_keep[2].astype(F32) + late_recv[2].astype(F32)
-    far_late[:96] = late[:96].astype(BF16)
-    far_late[96:] = pltpu.roll(late[96:], 2, 0).astype(BF16)
+        ref[...] = (keep_ref[step].astype(F32) + recv_ref[step].astype(F32)).astype(BF16)
+    total = keep_ref[2].astype(F32) + recv_ref[2].astype(F32)
+    far_early[...] = total[:192].astype(BF16)
+    far_late[:96] = total[192:288].astype(BF16)
+    far_late[96:] = pltpu.roll(total[288:], 2, 0).astype(BF16)
 
 
 def ring_kernel(near, back, far_early, far_late, out_near, out_back):
@@ -422,11 +420,6 @@
 
 def swap(values, axis):
     return lax.ppermute(values, axis, [(0, 1), (1, 0)])
-
-
-def side_pieces(keep, recv):
-    half = ((4, keep.shape[1], 384), BF16)
-    return call(core_kernel, [half, half], nbytes=4 * 10**6)(keep, recv)
 
 
 def shift(values, step):
@@ -471,21 +464,22 @@
         flops=6 * 10**9, nbytes=20 * 10**6,
     )(x, qkv, resid_grad, gain_one, w_qkv, w_proj)
     returned = exchange(slots, HA + ("wa",))
-    early = side_pieces(early_keep, swap(early_send, "core"))
-    rows_grad, *early = lax.optimization_barrier((rows_grad, *early))
     late_keep, late_send = call(
         weight_kernel,
         [((8, 112, 384), BF16), ((8, 112, 384), BF16)],
         [((1152, 384), F32), ((384, 384), F32), ((112, 384), F32)],
         flops=10**9, nbytes=5 * 10**6,
     )(rows_grad, normed, resid_grad, mixed, gain_sum_one, gain_sum_two)
-    late = side_pieces(late_keep, swap(late_send, "core"))
+    half = ((4, 304, 384), BF16)
+    keep, send = call(core_kernel, [half, half], nbytes=10**7)(
+        early_keep, swap(early_send, "core"), late_keep, swap(late_send, "core")
+    )
     piece = ((304, 384), BF16)
     own, near, back, far_early, far_late = call(
         side_kernel,
         [piece, piece, piece, ((192, 384), BF16), ((112, 384), BF16)],
         nbytes=5 * 10**6,
-    )(early[0], swap(early[1], "xl"), late[0], swap(late[1], "xl"))
+    )(keep, swap(send, "xl"))
     near, back = call(ring_kernel, [piece, piece], nbytes=2 * 10**6)(
         near, back, shift(far_early, 1), shift(far_late, 3)
     )

time: 122 us -> 123 us (level)
  waiting for transfers between devices: 51.8 us -> 54.8 us
    ppermute x5 -> x4, waiting for transfers between devices: 20.8 us -> 23.7 us  [swap(): return lax.ppermute(values, axis, [(0, 1), (1, 0)])]
    pallas_call x13 -> x12, Pallas kernels: 22.1 us -> 21.2 us  [run(): pl.pallas_call(kernel, out_shape=[jax.ShapeDtypeStruct(shape, dtype) for...]
    ppermute x5 -> x4, starting transfers between devices: 6.21 us -> 5.41 us  [swap(): return lax.ppermute(values, axis, [(0, 1), (1, 0)])]
  transfers between devices with their start and end apart: 11 -> 10, of which waited for: 7 -> 7; matrix products, arithmetic and copies ran while one was open for 0% -> 0% of each run, Pallas kernels for 6% -> 7%
where the time goes in v8:
time: 123 us; the launch traced here: 122 us
  waiting for transfers between devices  54.8 us (45%)
  starting transfers between devices  31.8 us (26%)
  Pallas kernels  21.2 us (17%)
  blocking collectives  13.5 us (11%)
    all_to_all x2, waiting for transfers between devices, exchange(): return lax.all_to_all(values, axes, split_axis=0, concat_axis=0, tiled=True)  23.7 us
    ppermute x4, waiting for transfers between devices, swap(): return lax.ppermute(values, axis, [(0, 1), (1, 0)])  23.7 us
    pallas_call x12, Pallas kernels, run(): pl.pallas_call(kernel, out_shape=[jax.ShapeDtypeStruct(shape, dtype) for...  21.2 us
    all_to_all x2, starting transfers between devices, exchange(): return lax.all_to_all(values, axes, split_axis=0, concat_axis=0, tiled=True)  19.7 us
    all_to_all x1, blocking collectives, exchange(): return lax.all_to_all(values, axes, split_axis=0, concat_axis=0, tiled=True)  13.5 us
    ppermute x4, waiting for transfers between devices, shift(): lax.ppermute(values, 'y', [(place, (place + step) % 4) for place in range...  7.45 us
    ppermute x4, starting transfers between devices, shift(): lax.ppermute(values, 'y', [(place, (place + step) % 4) for place in range...  6.62 us
    ppermute x4, starting transfers between devices, swap(): return lax.ppermute(values, axis, [(0, 1), (1, 0)])  5.41 us
  transfers between devices with their start and end apart: 10, of which 7 were waited for; matrix products, arithmetic and copies ran while one was open for 0% of the time, Pallas kernels for 7%

profile of v8, /device:TPU:2, one launch (start us, length us, event | category | flops | bytes accessed | tf_op | source)
XLA Modules:
  0.0 122.1 jit_solution(5622800096170371918)
XLA Ops:
  0.7 2.2 %shard_map.135 = bf16[128,8,384]{2,1,0:T(8,128)(2,1)} custom-call(bf16[14,7,4,384]{3,2,1,0:T(4,128)(2,1)} %bitcast.7, bf16[14,7,4,384]{3,2,1,0:T(4,128)(2,1)} %bitcast.8), custom_call_target="tpu_custom_call" | custom-call | bytes 2000000 | tf_op jit(solution)/shard_map/pallas_call | solution.py:404
  2.9 13.9 %all-to-all-start = ((bf16[128,8,384]{2,1,0:T(8,128)(2,1)}), bf16[128,8,384]{2,1,0:T(8,128)(2,1)S(1)}, u32[]{:S(2)}, u32[]{:S(2)}) async-start(bf16[128,8,384]{2,1,0:T(8,128)(2,1)} %shard_map.135), calls=%async_computation | async-start | bytes 1572864 | tf_op jit(solution)/shard_map/all_to_all | solution.py:418
  16.9 23.7 %all-to-all-done = bf16[128,8,384]{2,1,0:T(8,128)(2,1)S(1)} async-done(((bf16[128,8,384]{2,1,0:T(8,128)(2,1)}), bf16[128,8,384]{2,1,0:T(8,128)(2,1)S(1)}, u32[]{:S(2)}, u32[]{:S(2)}) %all-to-all-start) | async-done | bytes 786464 | tf_op jit(solution)/shard_map/all_to_all | solution.py:418
  40.6 2.9 %shard_map.136 = (bf16[512,384]{1,0:T(8,128)(2,1)S(1)}, bf16[512,1152]{1,0:T(8,128)(2,1)S(1)}, bf16[512,384]{1,0:T(8,128)(2,1)S(1)}, bf16[512,384]{1,0:T(8,128)(2,1)S(1)}, bf16[512,384]{1,0:T(8,128)(2,1)S(1)}) custom-call(bf16[1024,384]{1,0:T(8,128)(2,1)S(1)} %bitcast.6, f32[1,384]{1,0:T(1,128)S(1)} %reshape.24.gain_one, bf16[1152,384]{1,0:T(8,128)(2,1)S(1)} %copy-done.2, ...), custom_call_target="tpu_custom_call" | custom-call | flops 1000000000 | bytes 4000000 | tf_op jit(solution)/shard_map/pallas_call | solution.py:404
  43.5 6.8 %shard_map.137 = (bf16[512,384]{1,0:T(8,128)(2,1)S(1)}, bf16[8,192,384]{2,1,0:T(8,128)(2,1)S(1)}, bf16[8,192,384]{2,1,0:T(8,128)(2,1)S(1)}, f32[1,384]{1,0:T(1,128)S(1)}) custom-call(bf16[512,384]{1,0:T(8,128)(2,1)S(1)} %get-tuple-element.39.grad_out, bf16[512,384]{1,0:T(8,128)(2,1)S(1)} %get-tuple-element.40.resid, f32[1,384]{1,0:T(1,128)S(1)} %reshape.25.gain_two, ...), custom_call_target="tpu_custom_call" | custom-call | flops 3000000000 | bytes 6000000 | tf_op jit(solution)/shard_map/pallas_call | solution.py:404
  50.6 5.1 %shard_map.138 = (bf16[128,3,4,128]{3,2,1,0:T(4,128)(2,1)}, bf16[512,1152]{1,0:T(8,128)(2,1)S(1)}, bf16[512,384]{1,0:T(8,128)(2,1)S(1)}, f32[1,384]{1,0:T(1,128)S(1)}) custom-call(bf16[512,384]{1,0:T(8,128)(2,1)S(1)} %get-tuple-element.43.x_ref, bf16[512,1152]{1,0:T(8,128)(2,1)S(1)} %get-tuple-element.44.qkv_ref, ...), custom_call_target="tpu_custom_call" | custom-call | flops 6000000000 | bytes 20000000 | tf_op jit(solution)/shard_map/pallas_call | solution.py:404
  55.6 1.6 %shard_map.139 = (bf16[8,112,384]{2,1,0:T(8,128)(2,1)S(1)}, bf16[8,112,384]{2,1,0:T(8,128)(2,1)S(1)}) custom-call(bf16[512,1152]{1,0:T(8,128)(2,1)S(1)} %get-tuple-element.46.rows_grad, bf16[512,384]{1,0:T(8,128)(2,1)S(1)} %get-tuple-element.47.normed, bf16[512,384]{1,0:T(8,128)(2,1)S(1)} %get-tuple-element.45.resid_grad_ref.resid_grad, ...), custom_call_target="tpu_custom_call" | custom-call | flops 1000000000 | bytes 5000000 | tf_op jit(solution)/shard_map/pallas_call | solution.py:404
  57.2 0.6 collective-permute-start.1
  57.8 1.8 %collective-permute-done.1.late_recv = bf16[8,112,384]{2,1,0:T(8,128)(2,1)S(1)} collective-permute-done((bf16[8,112,384]{2,1,0:T(8,128)(2,1)S(1)}, bf16[8,112,384]{2,1,0:T(8,128)(2,1)S(1)}, u32[]{:S(2)}, u32[]{:S(2)}) %collective-permute-start.1) | collective-permute-done | bytes 688160 | tf_op jit(solution)/shard_map/ppermute | solution.py:422
  59.6 0.4 shard_map.140
  60.1 2.3 %collective-permute-start.2 = (bf16[4,304,384]{2,1,0:T(8,128)(2,1)S(1)}, bf16[4,304,384]{2,1,0:T(8,128)(2,1)S(1)}, u32[]{:S(2)}, u32[]{:S(2)}) collective-permute-start(bf16[4,304,384]{2,1,0:T(8,128)(2,1)S(1)} %get-tuple-element.54), channel_id=1, source_target_pairs={{0,32},{32,0},{1,33},{33,1},{2,34},{34,2},{3,35},{35,3},{4,36},{36... | collective-permute-start | bytes 2801672 | tf_op jit(solution)/shard_map/ppermute | solution.py:422
  62.4 5.8 %all-to-all-start.1 = ((bf16[128,3,4,128]{3,2,1,0:T(4,128)(2,1)}), bf16[128,3,4,128]{3,2,1,0:T(4,128)(2,1)S(1)}, u32[]{:S(2)}, u32[]{:S(2)}) async-start(bf16[128,3,4,128]{3,2,1,0:T(4,128)(2,1)} %get-tuple-element.62), calls=%async_computation.1 | async-start | bytes 786432 | tf_op jit(solution)/shard_map/all_to_all | solution.py:418
  68.2 19.3 %collective-permute-done.2.recv_ref = bf16[4,304,384]{2,1,0:T(8,128)(2,1)S(1)} collective-permute-done((bf16[4,304,384]{2,1,0:T(8,128)(2,1)S(1)}, bf16[4,304,384]{2,1,0:T(8,128)(2,1)S(1)}, u32[]{:S(2)}, u32[]{:S(2)}) %collective-permute-start.2) | collective-permute-done | bytes 933920 | tf_op jit(solution)/shard_map/ppermute | solution.py:422
  87.8 0.3 collective-permute-start.3
  88.1 3.0 %collective-permute-start.4 = (bf16[112,384]{1,0:T(8,128)(2,1)S(1)}, bf16[112,384]{1,0:T(8,128)(2,1)S(1)}, u32[]{:S(2)}, u32[]{:S(2)}) collective-permute-start(bf16[112,384]{1,0:T(8,128)(2,1)S(1)} %get-tuple-element.59), channel_id=1, source_target_pairs={{0,192},{64,0},{128,64},{192,128},{1,193},{65,1},{129,65},{193,129... | collective-permute-start | bytes 258056 | tf_op jit(solution)/shard_map/ppermute | solution.py:426
  91.1 2.1 %collective-permute-done.4.far_late = bf16[112,384]{1,0:T(8,128)(2,1)S(1)} collective-permute-done((bf16[112,384]{1,0:T(8,128)(2,1)S(1)}, bf16[112,384]{1,0:T(8,128)(2,1)S(1)}, u32[]{:S(2)}, u32[]{:S(2)}) %collective-permute-start.4) | collective-permute-done | bytes 86048 | tf_op jit(solution)/shard_map/ppermute | solution.py:426
  93.2 1.2 collective-permute-done.3.far_early
  94.5 3.2 %collective-permute-start.6 = (bf16[304,384]{1,0:T(8,128)(2,1)S(1)}, bf16[304,384]{1,0:T(8,128)(2,1)S(1)}, u32[]{:S(2)}, u32[]{:S(2)}) collective-permute-start(bf16[304,384]{1,0:T(8,128)(2,1)S(1)} %get-tuple-element.61), channel_id=1, source_target_pairs={{0,192},{64,0},{128,64},{192,128},{1,193},{65,1},{129,65},{193,129... | collective-permute-start | bytes 700424 | tf_op jit(solution)/shard_map/ppermute | solution.py:426
  97.8 4.2 %collective-permute-done.5.near = bf16[304,384]{1,0:T(8,128)(2,1)S(1)} collective-permute-done((bf16[304,384]{1,0:T(8,128)(2,1)S(1)}, bf16[304,384]{1,0:T(8,128)(2,1)S(1)}, u32[]{:S(2)}, u32[]{:S(2)}) %collective-permute-start.5) | collective-permute-done | bytes 233504 | tf_op jit(solution)/shard_map/ppermute | solution.py:426
  102.3 13.5 %all_to_all.15.recv_ref = bf16[8,152,128]{2,1,0:T(8,128)(2,1)S(1)} all-to-all(bf16[8,152,128]{2,1,0:T(8,128)(2,1)S(1)} %shard_map.143), channel_id=1, replica_groups=mesh['y'=4,'xl'=2,'core'=2,'wa'=8,'dp'=2] {'wa'}, dimensions={0} | all-to-all | bytes 622592 | tf_op jit(solution)/shard_map/all_to_all | solution.py:418
  115.8 2.2 %collective-permute-start.7 = (bf16[152,128]{1,0:T(8,128)(2,1)S(1)}, bf16[152,128]{1,0:T(8,128)(2,1)S(1)}, u32[]{:S(2)}, u32[]{:S(2)}) collective-permute-start(bf16[152,128]{1,0:T(8,128)(2,1)S(1)} %shard_map.145.own_ref), channel_id=1, source_target_pairs={{0,1},{1,0},{2,3},{3,2},{4,5},{5,4},{6,7},{7,6},{8,9},{9,8},{10,11... | collective-permute-start | bytes 116744 | tf_op jit(solution)/shard_map/ppermute | solution.py:422
  118.0 0.8 shard_map.144
  118.8 2.6 %collective-permute-done.7.other_ref = bf16[152,128]{1,0:T(8,128)(2,1)S(1)} collective-permute-done((bf16[152,128]{1,0:T(8,128)(2,1)S(1)}, bf16[152,128]{1,0:T(8,128)(2,1)S(1)}, u32[]{:S(2)}, u32[]{:S(2)}) %collective-permute-start.7) | collective-permute-done | bytes 38944 | tf_op jit(solution)/shard_map/ppermute | solution.py:422
  121.4 0.8 shard_map.146
  (23 shorter events, 1.0 us)
Async XLA Ops:
  0.6 16.2 %copy-start.4 = (f32[384]{0:T(512)S(1)}, f32[384]{0:T(512)}, u32[]{:S(2)}) copy-start(f32[384]{0:T(512)} %param.10) | copy-start | bytes 4612
  0.6 16.2 %copy-start.5 = (f32[384]{0:T(512)S(1)}, f32[384]{0:T(512)}, u32[]{:S(2)}) copy-start(f32[384]{0:T(512)} %param.11) | copy-start | bytes 4612
  0.7 39.9 %copy-start.2 = (bf16[1152,384]{1,0:T(8,128)(2,1)S(1)}, bf16[1152,384]{1,0:T(8,128)(2,1)}, u32[]{:S(2)}) copy-start(bf16[1152,384]{1,0:T(8,128)(2,1)} %w_qkv.3) | copy-start | bytes 2654212
  0.7 39.9 %copy-start.3 = (bf16[384,384]{1,0:T(8,128)(2,1)S(1)}, bf16[384,384]{1,0:T(8,128)(2,1)}, u32[]{:S(2)}) copy-start(bf16[384,384]{1,0:T(8,128)(2,1)} %w_proj.3) | copy-start | bytes 884740
  2.9 37.7 %all-to-all-start = ((bf16[128,8,384]{2,1,0:T(8,128)(2,1)}), bf16[128,8,384]{2,1,0:T(8,128)(2,1)S(1)}, u32[]{:S(2)}, u32[]{:S(2)}) async-start(bf16[128,8,384]{2,1,0:T(8,128)(2,1)} %shard_map.135), calls=%async_computation | async-start | bytes 1572864 | tf_op jit(solution)/shard_map/all_to_all | solution.py:418
  40.6 2.9 %copy-start = (bf16[1536,384]{1,0:T(8,128)(2,1)S(1)}, bf16[1536,384]{1,0:T(8,128)(2,1)}, u32[]{:S(2)}) copy-start(bf16[1536,384]{1,0:T(8,128)(2,1)} %w_up.1) | copy-start | bytes 3538948
  40.6 2.9 %copy-start.1 = (bf16[384,1536]{1,0:T(8,128)(2,1)S(1)}, bf16[384,1536]{1,0:T(8,128)(2,1)}, u32[]{:S(2)}) copy-start(bf16[384,1536]{1,0:T(8,128)(2,1)} %w_down.1) | copy-start | bytes 3538948
  50.3 9.3 %collective-permute-start = (bf16[8,192,384]{2,1,0:T(8,128)(2,1)S(1)}, bf16[8,192,384]{2,1,0:T(8,128)(2,1)S(1)}, u32[]{:S(2)}, u32[]{:S(2)}) collective-permute-start(bf16[8,192,384]{2,1,0:T(8,128)(2,1)S(1)} %get-tuple-element.42), channel_id=1, source_target_pairs={{0,16},{16,0},{1,17},{17,1},{2,18},{18,2},{3,19},{19,3},{4,20},{20... | collective-permute-start | bytes 3538952 | tf_op jit(solution)/shard_map/ppermute | solution.py:422
  57.2 2.4 %collective-permute-start.1 = (bf16[8,112,384]{2,1,0:T(8,128)(2,1)S(1)}, bf16[8,112,384]{2,1,0:T(8,128)(2,1)S(1)}, u32[]{:S(2)}, u32[]{:S(2)}) collective-permute-start(bf16[8,112,384]{2,1,0:T(8,128)(2,1)S(1)} %get-tuple-element.52), channel_id=1, source_target_pairs={{0,16},{16,0},{1,17},{17,1},{2,18},{18,2},{3,19},{19,3},{4,20},{20... | collective-permute-start | bytes 2064392 | tf_op jit(solution)/shard_map/ppermute | solution.py:422
  60.1 27.5 %collective-permute-start.2 = (bf16[4,304,384]{2,1,0:T(8,128)(2,1)S(1)}, bf16[4,304,384]{2,1,0:T(8,128)(2,1)S(1)}, u32[]{:S(2)}, u32[]{:S(2)}) collective-permute-start(bf16[4,304,384]{2,1,0:T(8,128)(2,1)S(1)} %get-tuple-element.54), channel_id=1, source_target_pairs={{0,32},{32,0},{1,33},{33,1},{2,34},{34,2},{3,35},{35,3},{4,36},{36... | collective-permute-start | bytes 2801672 | tf_op jit(solution)/shard_map/ppermute | solution.py:422
  62.4 39.9 %all-to-all-start.1 = ((bf16[128,3,4,128]{3,2,1,0:T(4,128)(2,1)}), bf16[128,3,4,128]{3,2,1,0:T(4,128)(2,1)S(1)}, u32[]{:S(2)}, u32[]{:S(2)}) async-start(bf16[128,3,4,128]{3,2,1,0:T(4,128)(2,1)} %get-tuple-element.62), calls=%async_computation.1 | async-start | bytes 786432 | tf_op jit(solution)/shard_map/all_to_all | solution.py:418
  87.8 6.6 %collective-permute-start.3 = (bf16[192,384]{1,0:T(8,128)(2,1)S(1)}, bf16[192,384]{1,0:T(8,128)(2,1)S(1)}, u32[]{:S(2)}, u32[]{:S(2)}) collective-permute-start(bf16[192,384]{1,0:T(8,128)(2,1)S(1)} %get-tuple-element.58), channel_id=1, source_target_pairs={{0,64},{64,128},{128,192},{192,0},{1,65},{65,129},{129,193},{193,1... | collective-permute-start | bytes 442376 | tf_op jit(solution)/shard_map/ppermute | solution.py:426
  88.1 5.1 %collective-permute-start.4 = (bf16[112,384]{1,0:T(8,128)(2,1)S(1)}, bf16[112,384]{1,0:T(8,128)(2,1)S(1)}, u32[]{:S(2)}, u32[]{:S(2)}) collective-permute-start(bf16[112,384]{1,0:T(8,128)(2,1)S(1)} %get-tuple-element.59), channel_id=1, source_target_pairs={{0,192},{64,0},{128,64},{192,128},{1,193},{65,1},{129,65},{193,129... | collective-permute-start | bytes 258056 | tf_op jit(solution)/shard_map/ppermute | solution.py:426
  94.4 7.5 %collective-permute-start.5 = (bf16[304,384]{1,0:T(8,128)(2,1)S(1)}, bf16[304,384]{1,0:T(8,128)(2,1)S(1)}, u32[]{:S(2)}, u32[]{:S(2)}) collective-permute-start(bf16[304,384]{1,0:T(8,128)(2,1)S(1)} %get-tuple-element.60), channel_id=1, source_target_pairs={{0,64},{64,128},{128,192},{192,0},{1,65},{65,129},{129,193},{193,1... | collective-permute-start | bytes 700424 | tf_op jit(solution)/shard_map/ppermute | solution.py:426
  94.5 7.4 %collective-permute-start.6 = (bf16[304,384]{1,0:T(8,128)(2,1)S(1)}, bf16[304,384]{1,0:T(8,128)(2,1)S(1)}, u32[]{:S(2)}, u32[]{:S(2)}) collective-permute-start(bf16[304,384]{1,0:T(8,128)(2,1)S(1)} %get-tuple-element.61), channel_id=1, source_target_pairs={{0,192},{64,0},{128,64},{192,128},{1,193},{65,1},{129,65},{193,129... | collective-permute-start | bytes 700424 | tf_op jit(solution)/shard_map/ppermute | solution.py:426
  115.8 5.6 %collective-permute-start.7 = (bf16[152,128]{1,0:T(8,128)(2,1)S(1)}, bf16[152,128]{1,0:T(8,128)(2,1)S(1)}, u32[]{:S(2)}, u32[]{:S(2)}) collective-permute-start(bf16[152,128]{1,0:T(8,128)(2,1)S(1)} %shard_map.145.own_ref), channel_id=1, source_target_pairs={{0,1},{1,0},{2,3},{3,2},{4,5},{5,4},{6,7},{7,6},{8,9},{9,8},{10,11... | collective-permute-start | bytes 116744 | tf_op jit(solution)/shard_map/ppermute | solution.py:422

commit v9 on v6

--- a/solution.py
+++ b/solution.py
@@ -477,7 +477,7 @@
         weight_kernel,
         [((8, 112, 384), BF16), ((8, 112, 384), BF16)],
         [((1152, 384), F32), ((384, 384), F32), ((112, 384), F32)],
-        flops=10**9, nbytes=5 * 10**6,
+        flops=10**9, nbytes=5 * 10**6, limit=8,
     )(rows_grad, normed, resid_grad, mixed, gain_sum_one, gain_sum_two)
     late = side_pieces(late_keep, swap(late_send, "core"))
     piece = ((304, 384), BF16)

time: 122 us -> 122 us (level)
  no operation moved by 1% of the time
where the time goes in v9:
time: 122 us; the launch traced here: 121 us
  waiting for transfers between devices  51.8 us (42%)
  starting transfers between devices  32.4 us (27%)
  Pallas kernels  22.1 us (18%)
  blocking collectives  13.7 us (11%)
    all_to_all x2, waiting for transfers between devices, exchange(): return lax.all_to_all(values, axes, split_axis=0, concat_axis=0, tiled=True)  23.7 us
    pallas_call x13, Pallas kernels, run(): pl.pallas_call(kernel, out_shape=[jax.ShapeDtypeStruct(shape, dtype) for...  22.1 us
    ppermute x5, waiting for transfers between devices, swap(): return lax.ppermute(values, axis, [(0, 1), (1, 0)])  20.8 us
    all_to_all x2, starting transfers between devices, exchange(): return lax.all_to_all(values, axes, split_axis=0, concat_axis=0, tiled=True)  19.6 us
    all_to_all x1, blocking collectives, exchange(): return lax.all_to_all(values, axes, split_axis=0, concat_axis=0, tiled=True)  13.7 us
    ppermute x4, waiting for transfers between devices, shift(): lax.ppermute(values, 'y', [(place, (place + step) % 4) for place in range...  7.31 us
    ppermute x4, starting transfers between devices, shift(): lax.ppermute(values, 'y', [(place, (place + step) % 4) for place in range...  6.62 us
    ppermute x5, starting transfers between devices, swap(): return lax.ppermute(values, axis, [(0, 1), (1, 0)])  6.21 us
  transfers between devices with their start and end apart: 11, of which 7 were waited for; matrix products, arithmetic and copies ran while one was open for 0% of the time, Pallas kernels for 6%

profile of v9, /device:TPU:2, one launch (start us, length us, event | category | flops | bytes accessed | tf_op | source)
XLA Modules:
  0.0 120.9 jit_solution(17762914026176754900)
XLA Ops:
  0.7 2.2 %shard_map.135 = bf16[128,8,384]{2,1,0:T(8,128)(2,1)} custom-call(bf16[14,7,4,384]{3,2,1,0:T(4,128)(2,1)} %bitcast.7, bf16[14,7,4,384]{3,2,1,0:T(4,128)(2,1)} %bitcast.8), custom_call_target="tpu_custom_call" | custom-call | bytes 2000000 | tf_op jit(solution)/shard_map/pallas_call | solution.py:406
  2.9 13.9 %all-to-all-start = ((bf16[128,8,384]{2,1,0:T(8,128)(2,1)}), bf16[128,8,384]{2,1,0:T(8,128)(2,1)S(1)}, u32[]{:S(2)}, u32[]{:S(2)}) async-start(bf16[128,8,384]{2,1,0:T(8,128)(2,1)} %shard_map.135), calls=%async_computation | async-start | bytes 1572864 | tf_op jit(solution)/shard_map/all_to_all | solution.py:420
  16.9 23.7 %all-to-all-done = bf16[128,8,384]{2,1,0:T(8,128)(2,1)S(1)} async-done(((bf16[128,8,384]{2,1,0:T(8,128)(2,1)}), bf16[128,8,384]{2,1,0:T(8,128)(2,1)S(1)}, u32[]{:S(2)}, u32[]{:S(2)}) %all-to-all-start) | async-done | bytes 786464 | tf_op jit(solution)/shard_map/all_to_all | solution.py:420
  40.6 2.9 %shard_map.136 = (bf16[512,384]{1,0:T(8,128)(2,1)S(1)}, bf16[512,1152]{1,0:T(8,128)(2,1)S(1)}, bf16[512,384]{1,0:T(8,128)(2,1)S(1)}, bf16[512,384]{1,0:T(8,128)(2,1)S(1)}, bf16[512,384]{1,0:T(8,128)(2,1)S(1)}) custom-call(bf16[1024,384]{1,0:T(8,128)(2,1)S(1)} %bitcast.6, f32[1,384]{1,0:T(1,128)S(1)} %reshape.24.gain_one, bf16[1152,384]{1,0:T(8,128)(2,1)S(1)} %copy-done.2, ...), custom_call_target="tpu_custom_call" | custom-call | flops 1000000000 | bytes 4000000 | tf_op jit(solution)/shard_map/pallas_call | solution.py:406
  43.5 6.8 %shard_map.137 = (bf16[512,384]{1,0:T(8,128)(2,1)S(1)}, bf16[8,192,384]{2,1,0:T(8,128)(2,1)S(1)}, bf16[8,192,384]{2,1,0:T(8,128)(2,1)S(1)}, f32[1,384]{1,0:T(1,128)S(1)}) custom-call(bf16[512,384]{1,0:T(8,128)(2,1)S(1)} %get-tuple-element.46.grad_out, bf16[512,384]{1,0:T(8,128)(2,1)S(1)} %get-tuple-element.47.resid, f32[1,384]{1,0:T(1,128)S(1)} %reshape.25.gain_two, ...), custom_call_target="tpu_custom_call" | custom-call | flops 3000000000 | bytes 6000000 | tf_op jit(solution)/shard_map/pallas_call | solution.py:406
  50.6 5.1 %shard_map.138 = (bf16[128,3,4,128]{3,2,1,0:T(4,128)(2,1)}, bf16[512,1152]{1,0:T(8,128)(2,1)S(1)}, bf16[512,384]{1,0:T(8,128)(2,1)S(1)}, f32[1,384]{1,0:T(1,128)S(1)}) custom-call(bf16[512,384]{1,0:T(8,128)(2,1)S(1)} %get-tuple-element.44.x_ref, bf16[512,1152]{1,0:T(8,128)(2,1)S(1)} %get-tuple-element.45.qkv_ref, ...), custom_call_target="tpu_custom_call" | custom-call | flops 6000000000 | bytes 20000000 | tf_op jit(solution)/shard_map/pallas_call | solution.py:406
  56.0 2.5 %shard_map.140 = (bf16[8,112,384]{2,1,0:T(8,128)(2,1)S(1)}, bf16[8,112,384]{2,1,0:T(8,128)(2,1)}) custom-call(bf16[512,1152]{1,0:T(8,128)(2,1)S(1)} %get-tuple-element.56.rows_grad, bf16[512,384]{1,0:T(8,128)(2,1)S(1)} %get-tuple-element.57.normed, bf16[512,384]{1,0:T(8,128)(2,1)S(1)} %get-tuple-element.48.resid_grad_ref.resid_grad, ...), custom_call_target="tpu_custom_call" | custom-call | flops 1000000000 | bytes 5000000 | tf_op jit(solution)/shard_map/pallas_call | solution.py:406
  58.4 0.5 collective-permute-start.2
  59.0 2.2 %collective-permute-start.1 = (bf16[4,192,384]{2,1,0:T(8,128)(2,1)S(1)}, bf16[4,192,384]{2,1,0:T(8,128)(2,1)S(1)}, u32[]{:S(2)}, u32[]{:S(2)}) collective-permute-start(bf16[4,192,384]{2,1,0:T(8,128)(2,1)S(1)} %get-tuple-element.55), channel_id=1, source_target_pairs={{0,32},{32,0},{1,33},{33,1},{2,34},{34,2},{3,35},{35,3},{4,36},{36... | collective-permute-start | bytes 1769480 | tf_op jit(solution)/shard_map/ppermute | solution.py:424
  61.2 5.7 %all-to-all-start.1 = ((bf16[128,3,4,128]{3,2,1,0:T(4,128)(2,1)}), bf16[128,3,4,128]{3,2,1,0:T(4,128)(2,1)S(1)}, u32[]{:S(2)}, u32[]{:S(2)}) async-start(bf16[128,3,4,128]{3,2,1,0:T(4,128)(2,1)} %get-tuple-element.72), calls=%async_computation.1 | async-start | bytes 786432 | tf_op jit(solution)/shard_map/all_to_all | solution.py:420
  67.0 1.0 collective-permute-start.3
  68.0 10.9 %collective-permute-done.1.early_recv = bf16[4,192,384]{2,1,0:T(8,128)(2,1)S(1)} collective-permute-done((bf16[4,192,384]{2,1,0:T(8,128)(2,1)S(1)}, bf16[4,192,384]{2,1,0:T(8,128)(2,1)S(1)}, u32[]{:S(2)}, u32[]{:S(2)}) %collective-permute-start.1) | collective-permute-done | bytes 589856 | tf_op jit(solution)/shard_map/ppermute | solution.py:424
  78.9 7.4 %collective-permute-done.3.late_recv = bf16[4,112,384]{2,1,0:T(8,128)(2,1)S(1)} collective-permute-done((bf16[4,112,384]{2,1,0:T(8,128)(2,1)S(1)}, bf16[4,112,384]{2,1,0:T(8,128)(2,1)S(1)}, u32[]{:S(2)}, u32[]{:S(2)}) %collective-permute-start.3) | collective-permute-done | bytes 344096 | tf_op jit(solution)/shard_map/ppermute | solution.py:424
  86.5 0.4 collective-permute-start.4
  86.8 3.0 %collective-permute-start.5 = (bf16[112,384]{1,0:T(8,128)(2,1)S(1)}, bf16[112,384]{1,0:T(8,128)(2,1)S(1)}, u32[]{:S(2)}, u32[]{:S(2)}) collective-permute-start(bf16[112,384]{1,0:T(8,128)(2,1)S(1)} %get-tuple-element.69), channel_id=1, source_target_pairs={{0,192},{64,0},{128,64},{192,128},{1,193},{65,1},{129,65},{193,129... | collective-permute-start | bytes 258056 | tf_op jit(solution)/shard_map/ppermute | solution.py:433
  89.8 2.1 %collective-permute-done.5.far_late = bf16[112,384]{1,0:T(8,128)(2,1)S(1)} collective-permute-done((bf16[112,384]{1,0:T(8,128)(2,1)S(1)}, bf16[112,384]{1,0:T(8,128)(2,1)S(1)}, u32[]{:S(2)}, u32[]{:S(2)}) %collective-permute-start.5) | collective-permute-done | bytes 86048 | tf_op jit(solution)/shard_map/ppermute | solution.py:433
  91.9 1.1 collective-permute-done.4.far_early
  93.2 3.2 %collective-permute-start.7 = (bf16[304,384]{1,0:T(8,128)(2,1)S(1)}, bf16[304,384]{1,0:T(8,128)(2,1)S(1)}, u32[]{:S(2)}, u32[]{:S(2)}) collective-permute-start(bf16[304,384]{1,0:T(8,128)(2,1)S(1)} %get-tuple-element.71), channel_id=1, source_target_pairs={{0,192},{64,0},{128,64},{192,128},{1,193},{65,1},{129,65},{193,129... | collective-permute-start | bytes 700424 | tf_op jit(solution)/shard_map/ppermute | solution.py:433
  96.4 4.1 %collective-permute-done.6.near = bf16[304,384]{1,0:T(8,128)(2,1)S(1)} collective-permute-done((bf16[304,384]{1,0:T(8,128)(2,1)S(1)}, bf16[304,384]{1,0:T(8,128)(2,1)S(1)}, u32[]{:S(2)}, u32[]{:S(2)}) %collective-permute-start.6) | collective-permute-done | bytes 233504 | tf_op jit(solution)/shard_map/ppermute | solution.py:433
  100.8 13.7 %all_to_all.15.recv_ref = bf16[8,152,128]{2,1,0:T(8,128)(2,1)S(1)} all-to-all(bf16[8,152,128]{2,1,0:T(8,128)(2,1)S(1)} %shard_map.144), channel_id=1, replica_groups=mesh['y'=4,'xl'=2,'core'=2,'wa'=8,'dp'=2] {'wa'}, dimensions={0} | all-to-all | bytes 622592 | tf_op jit(solution)/shard_map/all_to_all | solution.py:420
  114.6 2.2 %collective-permute-start.8 = (bf16[152,128]{1,0:T(8,128)(2,1)S(1)}, bf16[152,128]{1,0:T(8,128)(2,1)S(1)}, u32[]{:S(2)}, u32[]{:S(2)}) collective-permute-start(bf16[152,128]{1,0:T(8,128)(2,1)S(1)} %shard_map.146.own_ref), channel_id=1, source_target_pairs={{0,1},{1,0},{2,3},{3,2},{4,5},{5,4},{6,7},{7,6},{8,9},{9,8},{10,11... | collective-permute-start | bytes 116744 | tf_op jit(solution)/shard_map/ppermute | solution.py:424
  116.8 0.8 shard_map.145
  117.6 2.5 %collective-permute-done.8.other_ref = bf16[152,128]{1,0:T(8,128)(2,1)S(1)} collective-permute-done((bf16[152,128]{1,0:T(8,128)(2,1)S(1)}, bf16[152,128]{1,0:T(8,128)(2,1)S(1)}, u32[]{:S(2)}, u32[]{:S(2)}) %collective-permute-start.8) | collective-permute-done | bytes 38944 | tf_op jit(solution)/shard_map/ppermute | solution.py:424
  120.1 0.8 shard_map.147
  (26 shorter events, 1.5 us)
Async XLA Ops:
  0.6 16.2 %copy-start.4 = (f32[384]{0:T(512)S(1)}, f32[384]{0:T(512)}, u32[]{:S(2)}) copy-start(f32[384]{0:T(512)} %param.10) | copy-start | bytes 4612
  0.6 16.2 %copy-start.5 = (f32[384]{0:T(512)S(1)}, f32[384]{0:T(512)}, u32[]{:S(2)}) copy-start(f32[384]{0:T(512)} %param.11) | copy-start | bytes 4612
  0.7 39.9 %copy-start.2 = (bf16[1152,384]{1,0:T(8,128)(2,1)S(1)}, bf16[1152,384]{1,0:T(8,128)(2,1)}, u32[]{:S(2)}) copy-start(bf16[1152,384]{1,0:T(8,128)(2,1)} %w_qkv.3) | copy-start | bytes 2654212
  0.7 39.9 %copy-start.3 = (bf16[384,384]{1,0:T(8,128)(2,1)S(1)}, bf16[384,384]{1,0:T(8,128)(2,1)}, u32[]{:S(2)}) copy-start(bf16[384,384]{1,0:T(8,128)(2,1)} %w_proj.3) | copy-start | bytes 884740
  2.9 37.7 %all-to-all-start = ((bf16[128,8,384]{2,1,0:T(8,128)(2,1)}), bf16[128,8,384]{2,1,0:T(8,128)(2,1)S(1)}, u32[]{:S(2)}, u32[]{:S(2)}) async-start(bf16[128,8,384]{2,1,0:T(8,128)(2,1)} %shard_map.135), calls=%async_computation | async-start | bytes 1572864 | tf_op jit(solution)/shard_map/all_to_all | solution.py:420
  40.6 2.9 %copy-start = (bf16[1536,384]{1,0:T(8,128)(2,1)S(1)}, bf16[1536,384]{1,0:T(8,128)(2,1)}, u32[]{:S(2)}) copy-start(bf16[1536,384]{1,0:T(8,128)(2,1)} %w_up.1) | copy-start | bytes 3538948
  40.6 2.9 %copy-start.1 = (bf16[384,1536]{1,0:T(8,128)(2,1)S(1)}, bf16[384,1536]{1,0:T(8,128)(2,1)}, u32[]{:S(2)}) copy-start(bf16[384,1536]{1,0:T(8,128)(2,1)} %w_down.1) | copy-start | bytes 3538948
  50.3 5.4 %collective-permute-start = (bf16[8,192,384]{2,1,0:T(8,128)(2,1)S(1)}, bf16[8,192,384]{2,1,0:T(8,128)(2,1)S(1)}, u32[]{:S(2)}, u32[]{:S(2)}) collective-permute-start(bf16[8,192,384]{2,1,0:T(8,128)(2,1)S(1)} %get-tuple-element.51), channel_id=1, source_target_pairs={{0,16},{16,0},{1,17},{17,1},{2,18},{18,2},{3,19},{19,3},{4,20},{20... | collective-permute-start | bytes 3538952 | tf_op jit(solution)/shard_map/ppermute | solution.py:424
  58.4 8.4 %collective-permute-start.2 = (bf16[8,112,384]{2,1,0:T(8,128)(2,1)}, bf16[8,112,384]{2,1,0:T(8,128)(2,1)S(1)}, u32[]{:S(2)}, u32[]{:S(2)}) collective-permute-start(bf16[8,112,384]{2,1,0:T(8,128)(2,1)} %get-tuple-element.62), channel_id=1, source_target_pairs={{0,16},{16,0},{1,17},{17,1},{2,18},{18,2},{3,19},{19,3},{4,20},{20... | collective-permute-start | bytes 2064392 | tf_op jit(solution)/shard_map/ppermute | solution.py:424
  59.0 19.9 %collective-permute-start.1 = (bf16[4,192,384]{2,1,0:T(8,128)(2,1)S(1)}, bf16[4,192,384]{2,1,0:T(8,128)(2,1)S(1)}, u32[]{:S(2)}, u32[]{:S(2)}) collective-permute-start(bf16[4,192,384]{2,1,0:T(8,128)(2,1)S(1)} %get-tuple-element.55), channel_id=1, source_target_pairs={{0,32},{32,0},{1,33},{33,1},{2,34},{34,2},{3,35},{35,3},{4,36},{36... | collective-permute-start | bytes 1769480 | tf_op jit(solution)/shard_map/ppermute | solution.py:424
  61.2 39.6 %all-to-all-start.1 = ((bf16[128,3,4,128]{3,2,1,0:T(4,128)(2,1)}), bf16[128,3,4,128]{3,2,1,0:T(4,128)(2,1)S(1)}, u32[]{:S(2)}, u32[]{:S(2)}) async-start(bf16[128,3,4,128]{3,2,1,0:T(4,128)(2,1)} %get-tuple-element.72), calls=%async_computation.1 | async-start | bytes 786432 | tf_op jit(solution)/shard_map/all_to_all | solution.py:420
  67.0 19.2 %collective-permute-start.3 = (bf16[4,112,384]{2,1,0:T(8,128)(2,1)S(1)}, bf16[4,112,384]{2,1,0:T(8,128)(2,1)S(1)}, u32[]{:S(2)}, u32[]{:S(2)}) collective-permute-start(bf16[4,112,384]{2,1,0:T(8,128)(2,1)S(1)} %get-tuple-element.64), channel_id=1, source_target_pairs={{0,32},{32,0},{1,33},{33,1},{2,34},{34,2},{3,35},{35,3},{4,36},{36... | collective-permute-start | bytes 1032200 | tf_op jit(solution)/shard_map/ppermute | solution.py:424
  86.5 6.5 %collective-permute-start.4 = (bf16[192,384]{1,0:T(8,128)(2,1)S(1)}, bf16[192,384]{1,0:T(8,128)(2,1)S(1)}, u32[]{:S(2)}, u32[]{:S(2)}) collective-permute-start(bf16[192,384]{1,0:T(8,128)(2,1)S(1)} %get-tuple-element.68), channel_id=1, source_target_pairs={{0,64},{64,128},{128,192},{192,0},{1,65},{65,129},{129,193},{193,1... | collective-permute-start | bytes 442376 | tf_op jit(solution)/shard_map/ppermute | solution.py:433
  86.8 5.1 %collective-permute-start.5 = (bf16[112,384]{1,0:T(8,128)(2,1)S(1)}, bf16[112,384]{1,0:T(8,128)(2,1)S(1)}, u32[]{:S(2)}, u32[]{:S(2)}) collective-permute-start(bf16[112,384]{1,0:T(8,128)(2,1)S(1)} %get-tuple-element.69), channel_id=1, source_target_pairs={{0,192},{64,0},{128,64},{192,128},{1,193},{65,1},{129,65},{193,129... | collective-permute-start | bytes 258056 | tf_op jit(solution)/shard_map/ppermute | solution.py:433
  93.1 7.4 %collective-permute-start.6 = (bf16[304,384]{1,0:T(8,128)(2,1)S(1)}, bf16[304,384]{1,0:T(8,128)(2,1)S(1)}, u32[]{:S(2)}, u32[]{:S(2)}) collective-permute-start(bf16[304,384]{1,0:T(8,128)(2,1)S(1)} %get-tuple-element.70), channel_id=1, source_target_pairs={{0,64},{64,128},{128,192},{192,0},{1,65},{65,129},{129,193},{193,1... | collective-permute-start | bytes 700424 | tf_op jit(solution)/shard_map/ppermute | solution.py:433
  93.2 7.3 %collective-permute-start.7 = (bf16[304,384]{1,0:T(8,128)(2,1)S(1)}, bf16[304,384]{1,0:T(8,128)(2,1)S(1)}, u32[]{:S(2)}, u32[]{:S(2)}) collective-permute-start(bf16[304,384]{1,0:T(8,128)(2,1)S(1)} %get-tuple-element.71), channel_id=1, source_target_pairs={{0,192},{64,0},{128,64},{192,128},{1,193},{65,1},{129,65},{193,129... | collective-permute-start | bytes 700424 | tf_op jit(solution)/shard_map/ppermute | solution.py:433
  114.6 5.6 %collective-permute-start.8 = (bf16[152,128]{1,0:T(8,128)(2,1)S(1)}, bf16[152,128]{1,0:T(8,128)(2,1)S(1)}, u32[]{:S(2)}, u32[]{:S(2)}) collective-permute-start(bf16[152,128]{1,0:T(8,128)(2,1)S(1)} %shard_map.146.own_ref), channel_id=1, source_target_pairs={{0,1},{1,0},{2,3},{3,2},{4,5},{5,4},{6,7},{7,6},{8,9},{9,8},{10,11... | collective-permute-start | bytes 116744 | tf_op jit(solution)/shard_map/ppermute | solution.py:424
